TPU v7x, 32 devices: a whole 2x2x4 slice. The times are simulated.
32 devices in a mesh: tower: 2 (over x), batch: 16 (over z, y, core).
Axes of the slice: x: 2, y: 2, z: 4, core: 2. Of those that a mesh axis runs over, the one named last changes fastest.
Arguments:
- dense_feats: bfloat16 [16384, 13], P('batch'), may hold values from -6 to 6
- category_ids: int32 [16384, 26], P('batch'), may hold values from 0 to 65535, as said below
- labels: int32 [16384], P('batch'), may hold values from 0 to 1
- valid_mask: int32 [16384], P('batch'), may hold values from 0 to 1
- embed_table: float32 [65536, 39], P(('tower', 'batch')), may hold values from -3 to 3
- table_first: float32 [65536, 39], P(('tower', 'batch')), may hold values from -5.722046e-06 to 5.722046e-06
- table_second: float32 [65536, 39], P(('tower', 'batch')), may hold values from 8.717179e-14 to 3.4868717e-13
- cross_weight: float32 [2, 1027, 1027], P('tower'), may hold values from -0.1875 to 0.1875
- cross_first: float32 [2, 1027, 1027], P('tower'), may hold values from -0.00015258789 to 0.00015258789
- cross_second: float32 [2, 1027, 1027], P('tower'), may hold values from 5.493164e-11 to 2.1972656e-10
- deep_weight: float32 [1024, 1027], P(('tower', 'batch')), may hold values from -0.1875 to 0.1875
- deep_first: float32 [1024, 1027], P(('tower', 'batch')), may hold values from -6.1035156e-05 to 6.1035156e-05
- deep_second: float32 [1024, 1027], P(('tower', 'batch')), may hold values from 8.789062e-12 to 3.515625e-11
- vectors: float32 [5130], replicated, may hold values from -0.3 to 0.3
- vector_first: float32 [5130], replicated, may hold values from -0.0007324219 to 0.0007324219
- vector_second: float32 [5130], replicated, may hold values from 1.373291e-09 to 5.493164e-09
Outputs:
- loss_sum: float32 [], replicated
- valid_count: float32 [], replicated
- cross_grad: float32 [2, 1027, 1027], P('tower')
- cross_first_new: float32 [2, 1027, 1027], P('tower')
- cross_second_new: float32 [2, 1027, 1027], P('tower')
- cross_new: float32 [2, 1027, 1027], P('tower')
- cross_copy: bfloat16 [2, 1027, 1027], P('tower')
- deep_grad: float32 [1024, 1027], P(('tower', 'batch'))
- deep_first_new: float32 [1024, 1027], P(('tower', 'batch'))
- deep_second_new: float32 [1024, 1027], P(('tower', 'batch'))
- deep_new: float32 [1024, 1027], P(('tower', 'batch'))
- deep_copy: bfloat16 [1024, 1027], P(('tower', 'batch'))
- table_grad: float32 [65536, 39], P(('tower', 'batch'))
- table_first_new: float32 [65536, 39], P(('tower', 'batch'))
- table_second_new: float32 [65536, 39], P(('tower', 'batch'))
- table_new: float32 [65536, 39], P(('tower', 'batch'))
- vector_grad: float32 [5130], replicated
- vector_first_new: float32 [5130], replicated
- vector_second_new: float32 [5130], replicated
- vector_new: float32 [5130], replicated
Inputs may be any that keep to these rules, and one draw needn't show every extreme that they name: `category_ids`: in each aligned block of 512 examples, exactly 416 of its ids fall in each aligned block of 2048 table rows.
All inputs are finite; a program needn't handle non-finite values.
Results may differ from a plain program's by a relative error of at most 0.0075.
Values may be sent and summed in bfloat16 or wider, within the bound.
No kernel may reach another device: no remote copies, remote signals or barrier semaphores. Data moves between devices by JAX's collectives and lax.ppermute only.
A program may use at most 128 MiB of HBM per device.

v0:
```python
import jax
import jax.numpy as jnp
from jax import lax
from jax.sharding import PartitionSpec as P

STEP = 5


def adamw(weight, grad, first, second, rate):
    first_new = 0.9 * first + 0.1 * grad
    second_new = 0.999 * second + 0.001 * grad * grad
    update = (
        first_new / (1.0 - 0.9**STEP) / (jnp.sqrt(second_new / (1.0 - 0.999**STEP)) + 1e-08)
        + 0.01 * weight
    )
    return (first_new, second_new, weight - rate * update)


def widen(block, target):
    return jnp.pad(block, [(0, 0)] * (block.ndim - 1) + [(0, target - block.shape[-1])])


def contract(left, right, left_dim, right_dim):
    return lax.dot_general(
        left, right, (((left_dim,), (right_dim,)), ((), ())), preferred_element_type=jnp.float32
    )


def cross_pass(inputs, cross_low, cross_bias):
    base = inputs.astype(jnp.float32)
    pre_first = contract(inputs, cross_low[0], 1, 0) + cross_bias[0]
    layer_one = base * pre_first + base
    one_low = layer_one.astype(jnp.bfloat16)
    pre_second = contract(one_low, cross_low[1], 1, 0) + cross_bias[1]
    layer_two = base * pre_second + layer_one
    return (base, pre_first, one_low, pre_second, layer_two)


def cross_backward(inputs, cross_low, kept, d_two):
    base, pre_first, one_low, pre_second, layer_two = kept
    d_pre_second = (d_two * base).astype(jnp.bfloat16)
    grad_second = contract(one_low, d_pre_second, 0, 0)
    d_one = contract(d_pre_second, cross_low[1], 1, 1) + d_two
    d_pre_first = (d_one * base).astype(jnp.bfloat16)
    grad_first = contract(inputs, d_pre_first, 0, 0)
    d_inputs = (
        contract(d_pre_first, cross_low[0], 1, 1) + d_one * (1.0 + pre_first) + d_two * pre_second
    )
    bias_grads = jnp.stack(
        [
            jnp.sum(d_pre_first.astype(jnp.float32), axis=0),
            jnp.sum(d_pre_second.astype(jnp.float32), axis=0),
        ]
    )
    return (d_inputs, jnp.stack([grad_first, grad_second]), bias_grads)


def deep_backward(inputs, deep_low, pre_deep, d_hidden):
    gate = jax.nn.sigmoid(pre_deep)
    d_pre_deep = (d_hidden * gate * (1.0 + pre_deep * (1.0 - gate))).astype(jnp.bfloat16)
    grad_deep = contract(d_pre_deep, inputs, 0, 0)
    d_inputs = contract(d_pre_deep, deep_low, 1, 0)
    return (d_inputs, grad_deep, jnp.sum(d_pre_deep.astype(jnp.float32), axis=0))


def local(
    dense_feats,
    category_ids,
    labels,
    valid_mask,
    embed_table,
    table_first,
    table_second,
    cross_weight,
    cross_first,
    cross_second,
    deep_weight,
    deep_first,
    deep_second,
    vectors,
    vector_first,
    vector_second,
):
    tower = lax.axis_index("tower")
    owners = lax.axis_size(("tower", "batch"))
    myself = lax.axis_index(("tower", "batch"))
    rows_own, embed = embed_table.shape
    examples, feats = category_ids.shape
    half = examples // 2
    width = cross_weight.shape[1]
    hidden_units = deep_weight.shape[0] * owners
    dense_width = dense_feats.shape[1]
    span = max(width, hidden_units)
    my_ids = lax.dynamic_slice_in_dim(category_ids, tower * half, half, 0).reshape(-1)
    order = jnp.argsort(my_ids // rows_own, stable=True)
    inverse = jnp.argsort(order, stable=True)
    slots = my_ids.shape[0] // owners
    asked = my_ids[order].reshape(owners, slots)
    arrived = lax.all_to_all(asked, ("tower", "batch"), split_axis=0, concat_axis=0, tiled=True)
    local_rows = arrived.reshape(-1) - myself * rows_own
    found = embed_table.astype(jnp.bfloat16)[local_rows].reshape(owners, slots, embed)
    returned = lax.all_to_all(found, ("tower", "batch"), split_axis=0, concat_axis=0, tiled=True)
    mine = returned.reshape(-1, embed)[inverse].reshape(half, feats * embed)
    cross_low = lax.all_gather(cross_weight.astype(jnp.bfloat16), "tower", axis=0, tiled=True)
    deep_low = lax.all_gather(
        deep_weight.astype(jnp.bfloat16), ("tower", "batch"), axis=0, tiled=True
    )
    cross_bias = vectors[: 2 * width].reshape(2, width)
    deep_bias = vectors[2 * width : 2 * width + hidden_units]
    head_cross = vectors[2 * width + hidden_units : 3 * width + hidden_units]
    head_deep = vectors[3 * width + hidden_units : 3 * width + 2 * hidden_units]
    head_bias = vectors[3 * width + 2 * hidden_units]
    cross_head_low = head_cross.astype(jnp.bfloat16)
    deep_head_low = head_deep.astype(jnp.bfloat16)
    valid_all = valid_mask.astype(jnp.float32)
    count = lax.psum(jnp.sum(valid_all), "batch")
    embedded = lax.all_gather(mine, "tower", axis=0, tiled=True)
    inputs = jnp.concatenate([dense_feats, embedded], axis=1)
    head_pair = jnp.stack([widen(cross_head_low, span), widen(deep_head_low, span)])
    head_own = head_pair[tower]

    def deep_pre():
        return contract(inputs, deep_low, 1, 1) + deep_bias

    def run_cross(unused):
        return widen(cross_pass(inputs, cross_low, cross_bias)[4], span)

    def run_deep(unused):
        return widen(jax.nn.silu(deep_pre()), span)

    out_low = lax.cond(tower == 0, run_cross, run_deep, 0).astype(jnp.bfloat16)
    both = lax.all_gather(out_low[None], "tower", axis=0, tiled=True)
    logit = jnp.einsum("tbw,tw->b", both, head_pair, preferred_element_type=jnp.float32) + head_bias
    target = labels.astype(jnp.float32)
    is_first = (tower == 0).astype(jnp.float32)
    loss_part = jnp.sum(valid_all * (jax.nn.softplus(logit) - target * logit)) * is_first
    d_logit = valid_all * (jax.nn.sigmoid(logit) - target) / count
    d_out = d_logit[:, None] * head_own.astype(jnp.float32)
    head_grad = jnp.dot(d_logit, out_low, preferred_element_type=jnp.float32)

    def back_cross(unused):
        kept = cross_pass(inputs, cross_low, cross_bias)
        d_inputs, grads, bias_grads = cross_backward(inputs, cross_low, kept, d_out)
        return (
            d_inputs,
            grads,
            bias_grads,
            jnp.zeros((hidden_units, width), jnp.float32),
            jnp.zeros((hidden_units,), jnp.float32),
        )

    def back_deep(unused):
        d_inputs, grad_deep, bias_deep = deep_backward(
            inputs, deep_low, deep_pre(), d_out[:, :hidden_units]
        )
        return (
            d_inputs,
            jnp.zeros((2, width, width), jnp.float32),
            jnp.zeros((2, width), jnp.float32),
            grad_deep,
            bias_deep,
        )

    d_inputs, cross_local, cross_bias_grad, deep_local, deep_bias_grad = lax.cond(
        tower == 0, back_cross, back_deep, 0
    )
    d_rows = lax.psum_scatter(d_inputs[:, dense_width:], "tower", scatter_dimension=0, tiled=True)
    head_parts = [
        head_grad * is_first,
        head_grad[:hidden_units] * (1.0 - is_first),
        (jnp.sum(d_logit) * is_first)[None],
    ]
    sent_back = d_rows.reshape(-1, embed)[order].reshape(owners, slots, embed)
    got_back = lax.all_to_all(
        sent_back, ("tower", "batch"), split_axis=0, concat_axis=0, tiled=True
    )
    table_grad = jnp.zeros_like(embed_table).at[local_rows].add(got_back.reshape(-1, embed))
    summed = lax.psum(cross_local, "batch")
    cross_grad = lax.psum_scatter(summed, "tower", scatter_dimension=0, tiled=True)
    deep_grad = lax.psum_scatter(deep_local, ("tower", "batch"), scatter_dimension=0, tiled=True)
    vector_local = jnp.concatenate([cross_bias_grad.reshape(-1), deep_bias_grad] + head_parts)
    vector_grad, loss_sum = lax.psum((vector_local, loss_part), ("tower", "batch"))
    cross_one, cross_two, cross_new = adamw(
        cross_weight, cross_grad, cross_first, cross_second, 0.03
    )
    deep_one, deep_two, deep_new = adamw(deep_weight, deep_grad, deep_first, deep_second, 0.03)
    table_one, table_two, table_new = adamw(
        embed_table, table_grad, table_first, table_second, 0.25
    )
    vector_one, vector_two, vector_new = adamw(
        vectors, vector_grad, vector_first, vector_second, 0.03
    )
    return (
        loss_sum,
        count,
        cross_grad,
        cross_one,
        cross_two,
        cross_new,
        cross_new.astype(jnp.bfloat16),
        deep_grad,
        deep_one,
        deep_two,
        deep_new,
        deep_new.astype(jnp.bfloat16),
        table_grad,
        table_one,
        table_two,
        table_new,
        vector_grad,
        vector_one,
        vector_two,
        vector_new,
    )


def solution(mesh):
    placed = (
        P("batch", None),
        P("batch", None),
        P("batch"),
        P("batch"),
        P(("tower", "batch"), None),
        P(("tower", "batch"), None),
        P(("tower", "batch"), None),
        P("tower", None, None),
        P("tower", None, None),
        P("tower", None, None),
        P(("tower", "batch"), None),
        P(("tower", "batch"), None),
        P(("tower", "batch"), None),
        P(),
        P(),
        P(),
    )
    return jax.shard_map(
        local,
        mesh=mesh,
        in_specs=placed,
        out_specs=(
            P(),
            P(),
            P("tower", None, None),
            P("tower", None, None),
            P("tower", None, None),
            P("tower", None, None),
            P("tower", None, None),
            P(("tower", "batch"), None),
            P(("tower", "batch"), None),
            P(("tower", "batch"), None),
            P(("tower", "batch"), None),
            P(("tower", "batch"), None),
            P(("tower", "batch"), None),
            P(("tower", "batch"), None),
            P(("tower", "batch"), None),
            P(("tower", "batch"), None),
            P(),
            P(),
            P(),
            P(),
        ),
        check_vma=False,
    )
```

profile of v0, /device:TPU:0, one launch (start us, length us, event | category | flops | bytes accessed | tf_op | source)
XLA Modules:
  0.0 1108.4 jit_solution(15981537293039310580)
XLA Ops:
  17.7 73.7 %gather_fusion = s32[13312]{0:T(1024)S(1)} fusion(s32[13312]{0:T(1024)S(1)} %reshape.101, s32[13312]{0:T(1024)S(1)} %fusion.34), kind=kCustom, calls=%fused_computation | custom fusion | bytes 159744 | tf_op jit(solution)/shard_map/gather | solution.py:98
  107.3 47.2 %gather_fusion.1 = bf16[13312,39]{1,0:T(8,128)(2,1)} fusion(bf16[2048,39]{1,0:T(8,128)(2,1)S(1)} %copy.133, s32[13312]{0:T(1024)S(1)} %broadcast_clamp_fusion), kind=kCustom, calls=%fused_computation.1 | custom fusion | bytes 2129920 | tf_op jit(solution)/shard_map/gather | solution.py:101
  172.2 23.0 %all-to-all-done.1 = bf16[32,416,39]{1,2,0:T(8,128)(2,1)} async-done(((bf16[32,416,39]{1,2,0:T(8,128)(2,1)}), bf16[32,416,39]{1,2,0:T(8,128)(2,1)}, u32[]{:S(2)}, u32[]{:S(2)}) %all-to-all-start.1) | async-done | bytes 1038368 | tf_op jit(solution)/shard_map/all_to_all | solution.py:102
  198.6 47.2 %gather_fusion.2 = bf16[13312,39]{1,0:T(8,128)(2,1)} fusion(bf16[13312,39]{1,0:T(8,128)(2,1)S(1)} %bitcast.53, s32[13312]{0:T(1024)S(1)} %fusion.35), kind=kCustom, calls=%fused_computation.2 | custom fusion | bytes 2129920 | tf_op jit(solution)/shard_map/gather | solution.py:103
  256.2 25.2 %all-gather.6.cloned.1.call-done = bf16[1024,1014]{1,0:T(8,128)(2,1)} async-done(((bf16[512,1014]{1,0:T(8,128)(2,1)}), bf16[1024,1014]{1,0:T(8,128)(2,1)}) %all-gather.6.cloned.1.call-update) | async-done | bytes 2076688 | tf_op jit(solution)/shard_map/all_gather | solution.py:117
  284.3 58.0 %all-gather.8.cloned.1.call-done = bf16[1024,1027]{1,0:T(8,128)(2,1)} async-done(((bf16[32,1027]{1,0:T(8,128)(2,1)}), bf16[1024,1027]{1,0:T(8,128)(2,1)}) %all-gather.8.cloned.1.call-update) | async-done | bytes 2103312 | tf_op jit(solution)/shard_map/all_gather | solution.py:105
  342.2 64.1 %all-gather.10.cloned.1.call-done = bf16[2,1027,1027]{2,1,0:T(8,128)(2,1)} async-done(((bf16[1,1027,1027]{2,1,0:T(8,128)(2,1)}), bf16[2,1027,1027]{2,1,0:T(8,128)(2,1)}) %all-gather.10.cloned.1.call-update) | async-done | bytes 4218932 | tf_op jit(solution)/shard_map/all_gather | solution.py:104
  406.3 12.9 %conditional.2 = (bf16[1024,1027]{0,1:T(8,128)(2,1)}) conditional(s32[]{:T(128)} %convert_element_type.70, (bf16[1024,1027]{1,0:T(8,128)(2,1)S(1)}, bf16[1024,1027]{1,0:T(8,128)(2,1)}, f32[1024]{0:T(1024)S(1)}) %tuple.24, (bf16[1024,1027]{1,0:T(8,128)(2,1)S(1)}, bf16[2,1027,1027]{2,1,0:T(8,128)(2,1)}, f32[2,1027]{1,0:T(2,128)S(1)}) %tuple.25), branch_computations={%region_2.3_spmd, %region_3.4_spmd} | conditional | flops 4330686464 | bytes 55374092 | solution.py:131
  420.2 56.4 %all-gather.12.cloned.1.call-done = bf16[2048,1027]{0,1:T(8,128)(2,1)} async-done(((bf16[1024,1027]{0,1:T(8,128)(2,1)}), bf16[2048,1027]{0,1:T(8,128)(2,1)}) %all-gather.12.cloned.1.call-update) | async-done | bytes 4206608 | tf_op jit(solution)/shard_map/all_gather | solution.py:132
  476.5 11.2 %reshape.150 = bf16[2,1024,1027]{1,0,2:T(2,128)(2,1)} reshape(bf16[2048,1027]{0,1:T(8,128)(2,1)} %all-gather.12.cloned.1.call-done) | data formatting | bytes 8413184 | tf_op jit(solution)/shard_map/all_gather | solution.py:132
  492.4 33.8 %psum.29 = f32[]{:T(128)} all-reduce(f32[]{:T(128)} %get-tuple-element.240), channel_id=1, replica_groups=mesh['tower'=2,'batch'=16] {'batch'}, use_global_device_ids=true, to_apply=%region_7.8 | all-reduce | flops 1 | bytes 8 | tf_op jit(solution)/shard_map/psum | solution.py:116
  530.5 47.1 %conditional.3 = (f32[1024,1027]{0,1:T(8,128)S(1)}, f32[2,1027,1027]{1,2,0:T(8,128)}, f32[1024,1027]{1,0:T(8,128)}, f32[1024]{0:T(1024)S(1)}, f32[2054]{0:T(1024)S(1)}) conditional(s32[]{:T(128)} %convert_element_type.70, (f32[1024,1027]{0,1:T(8,128)}, bf16[1024,1027]{1,0:T(8,128)(2,1)S(1)}, bf16[1024,1027]{1,0:T(8,128)(2,1)}, ...), branch_computations={%region_8.10_spmd, %region_10.13_spmd} | conditional | flops 12995220480 | bytes 280392800 | solution.py:164
  580.5 12.0 %copy.141 = f32[2,1027,1027]{2,1,0:T(8,128)} copy(f32[2,1027,1027]{1,2,0:T(8,128)} %get-tuple-element.75) | data formatting | bytes 16875664 | tf_op jit(solution)/shard_map/cond | solution.py:164
  593.3 37.1 %reduce-scatter.8.cloned.1.call-done = f32[512,1014]{0,1:T(8,128)} async-done(((f32[1024,1014]{0,1:T(8,128)}), f32[512,1014]{0,1:T(8,128)}) %reduce-scatter.8.cloned.1.call-update) | async-done | bytes 2076688 | tf_op jit(solution)/shard_map/reduce_scatter | solution.py:167
  637.9 47.9 %gather_fusion.3 = f32[13312,39]{1,0:T(8,128)} fusion(f32[13312,39]{1,0:T(8,128)} %reshape.106, s32[13312]{0:T(1024)S(1)} %copy-done.14), kind=kCustom, calls=%fused_computation.3 | custom fusion | bytes 4206592 | tf_op jit(solution)/shard_map/gather | solution.py:173
  696.9 75.4 %reduce-scatter.10.cloned.1.call-done = f32[1,1027,1027]{2,1,0:T(8,128)} async-done(((f32[2,1027,1027]{2,1,0:T(8,128)}), f32[1,1027,1027]{2,1,0:T(8,128)}) %reduce-scatter.10.cloned.1.call-update) | async-done | bytes 4218932
  774.4 40.1 %all-reduce.3 = (f32[]{:T(128)}, f32[5130]{0:T(1024)S(1)}) all-reduce(f32[]{:T(128)S(6)} %mul.249, f32[5130]{0:T(1024)S(1)} %concatenate.7), channel_id=1, replica_groups=mesh['tower'=2,'batch'=16] {'tower','batch'}, use_global_device_ids=true, to_apply=%region_5.6 | all-reduce | flops 5131 | bytes 41048 | tf_op jit(solution)/shard_map/psum | solution.py:182
  815.1 70.3 %reduce-scatter.6.cloned.1.call-done = f32[32,1027]{1,0:T(8,128)} async-done(((f32[1024,1027]{1,0:T(8,128)}), f32[32,1027]{1,0:T(8,128)}) %reduce-scatter.6.cloned.1.call-update) | async-done | bytes 131472 | tf_op jit(solution)/shard_map/reduce_scatter | solution.py:180
  893.2 71.7 %scatter_custom_fusion = f32[2048,39]{1,0:T(8,128)S(1)} fusion(s32[13312]{0:T(1024)} %bitcast.64, f32[13312,39]{1,0:T(8,128)} %bitcast.60, f32[]{:T(128)} %constant.53.clone.1), kind=kCustom, calls=%fused_computation.63 | custom fusion | flops 519168 | bytes 320000 | tf_op jit(solution)/shard_map/scatter-add | solution.py:177
  966.4 40.2 %all-reduce.6.cloned.1.call-done = f32[1,1027,1027]{2,1,0:T(8,128)} async-done(((f32[1,1027,1027]{2,1,0:T(8,128)}), f32[1,1027,1027]{2,1,0:T(8,128)}) %all-reduce.6.cloned.1.call-update) | async-done | bytes 4218932 | tf_op jit(solution)/shard_map/psum | solution.py:178
  1016.4 21.2 %copy.156 = f32[1,1027,1027]{2,0,1:T(1,128)} copy(f32[1,1027,1027]{2,1,0:T(8,128)S(1)} %get-tuple-element.257) | data formatting | bytes 8437832
  1037.7 21.2 %copy.155 = f32[1,1027,1027]{2,0,1:T(1,128)} copy(f32[1,1027,1027]{2,1,0:T(8,128)S(1)} %get-tuple-element.258) | data formatting | bytes 8437832
  1058.9 21.2 %copy.154 = f32[1,1027,1027]{2,0,1:T(1,128)} copy(f32[1,1027,1027]{2,1,0:T(8,128)S(1)} %get-tuple-element.259) | data formatting | bytes 8437832
  1080.1 21.3 %copy.153 = f32[1,1027,1027]{2,0,1:T(1,128)} copy(f32[1,1027,1027]{2,1,0:T(8,128)S(1)} %bitcast.56) | data formatting | bytes 8437832
  (184 shorter events, 172.1 us)
Async XLA Ops:
  17.7 73.7 %copy-start.13 = (s32[13312]{0:T(1024)}, s32[13312]{0:T(1024)S(1)}, u32[]{:S(2)}) copy-start(s32[13312]{0:T(1024)S(1)} %fusion.34) | copy-start | bytes 159748
  17.7 81.8 %copy-start.8 = (f32[2048,39]{0,1:T(8,128)S(1)}, f32[2048,39]{0,1:T(8,128)}, u32[]{:S(2)}) copy-start(f32[2048,39]{0,1:T(8,128)} %param.24) | copy-start | bytes 958468
  92.2 14.7 %all-to-all-start = ((s32[32,1,416]{2,1,0:T(1,128)}), s32[32,1,416]{2,1,0:T(1,128)S(1)}, u32[]{:S(2)}, u32[]{:S(2)}) async-start(s32[32,1,416]{2,1,0:T(1,128)} %all_to_all.12), calls=%async_computation | async-start | bytes 131072 | tf_op jit(solution)/shard_map/all_to_all | solution.py:99
  159.1 36.1 %all-to-all-start.1 = ((bf16[32,416,39]{1,2,0:T(8,128)(2,1)}), bf16[32,416,39]{1,2,0:T(8,128)(2,1)}, u32[]{:S(2)}, u32[]{:S(2)}) async-start(bf16[32,416,39]{1,2,0:T(8,128)(2,1)} %copy.134), calls=%async_computation.1 | async-start | bytes 2621440 | tf_op jit(solution)/shard_map/all_to_all | solution.py:102
  162.5 118.9 %all-gather.6.cloned.1.call-start = ((), (), s32[]{:S(2)}) async-start(), calls=%async_computation.6 | async-start | bytes 3145728 | tf_op jit(solution)/shard_map/all_gather | solution.py:117
  250.9 91.3 %all-gather.8.cloned.1.call-start = ((), (), s32[]{:S(2)}) async-start(), calls=%async_computation.7 | async-start | bytes 2433024 | tf_op jit(solution)/shard_map/all_gather | solution.py:105
  251.7 154.6 %all-gather.10.cloned.1.call-start = ((), (), s32[]{:S(2)}) async-start(), calls=%async_computation.8 | async-start | bytes 7133184 | tf_op jit(solution)/shard_map/all_gather | solution.py:104
  255.8 220.7 %all-gather.12.cloned.1.call-start = ((), (), s32[]{:S(2)}) async-start(), calls=%async_computation.11 | async-start | bytes 6340608 | tf_op jit(solution)/shard_map/all_gather | solution.py:132
  419.3 211.2 %reduce-scatter.8.cloned.1.call-start = ((), (), s32[]{:S(2)}) async-start(), calls=%async_computation.10 | async-start | bytes 6242304 | tf_op jit(solution)/shard_map/reduce_scatter | solution.py:167
  580.5 191.8 %reduce-scatter.10.cloned.1.call-start = ((), (), s32[]{:S(2)}) async-start(), calls=%async_computation.13 | async-start | bytes 14266368
  592.5 292.9 %reduce-scatter.6.cloned.1.call-start = ((), (), s32[]{:S(2)}) async-start(), calls=%async_computation.9 | async-start | bytes 4866048 | tf_op jit(solution)/shard_map/reduce_scatter | solution.py:180
  691.9 81.7 %copy-start.2 = (bf16[1024,1027]{0,1:T(8,128)(2,1)S(1)}, bf16[1024,1027]{0,1:T(8,128)(2,1)}, u32[]{:S(2)}) copy-start(bf16[1024,1027]{0,1:T(8,128)(2,1)} %get-tuple-element.276) | copy-start | bytes 6309892
  691.9 195.3 %all-to-all-start.2 = ((f32[32,416,39]{1,2,0:T(8,128)}), f32[32,416,39]{1,2,0:T(8,128)}, u32[]{:S(2)}, u32[]{:S(2)}) async-start(f32[32,416,39]{1,2,0:T(8,128)} %copy.147), calls=%async_computation.4 | async-start | bytes 5242880 | tf_op jit(solution)/shard_map/all_to_all | solution.py:174
  696.8 117.7 %copy-start.22 = (f32[5130]{0:T(1024)S(1)}, f32[5130]{0:T(1024)}, u32[]{:S(2)}) copy-start(f32[5130]{0:T(1024)} %param.35) | copy-start | bytes 61564
  696.8 117.7 %copy-start.23 = (f32[5130]{0:T(1024)S(1)}, f32[5130]{0:T(1024)}, u32[]{:S(2)}) copy-start(f32[5130]{0:T(1024)} %param.34) | copy-start | bytes 61564
  696.8 188.6 %copy-start.12 = (f32[32,1027]{1,0:T(8,128)S(1)}, f32[32,1027]{1,0:T(8,128)}, u32[]{:S(2)}) copy-start(f32[32,1027]{1,0:T(8,128)} %param.30) | copy-start | bytes 394372
  696.8 188.6 %copy-start.19 = (f32[32,1027]{1,0:T(8,128)S(1)}, f32[32,1027]{1,0:T(8,128)}, u32[]{:S(2)}) copy-start(f32[32,1027]{1,0:T(8,128)} %param.32) | copy-start | bytes 394372
  696.8 188.6 %copy-start.20 = (f32[32,1027]{1,0:T(8,128)S(1)}, f32[32,1027]{1,0:T(8,128)}, u32[]{:S(2)}) copy-start(f32[32,1027]{1,0:T(8,128)} %param.31) | copy-start | bytes 394372
  696.8 309.8 %all-reduce.6.cloned.1.call-start = ((), (), s32[]{:S(2)}) async-start(), calls=%async_computation.12 | async-start | bytes 9510912 | tf_op jit(solution)/shard_map/psum | solution.py:178
  814.5 78.7 %copy-start.24 = (f32[5130]{0:T(1024)}, f32[5130]{0:T(1024)S(1)}, u32[]{:S(2)}) copy-start(f32[5130]{0:T(1024)S(1)} %get-tuple-element.243) | copy-start | bytes 61564
  887.2 78.1 %copy-start.9 = (f32[2048,39]{0,1:T(8,128)S(1)}, f32[2048,39]{0,1:T(8,128)}, u32[]{:S(2)}) copy-start(f32[2048,39]{0,1:T(8,128)} %param.24) | copy-start | bytes 958468
  887.2 78.1 %copy-start.15 = (f32[2048,39]{0,1:T(8,128)S(1)}, f32[2048,39]{0,1:T(8,128)}, u32[]{:S(2)}) copy-start(f32[2048,39]{0,1:T(8,128)} %param.26) | copy-start | bytes 958468
  887.2 78.1 %copy-start.16 = (f32[2048,39]{0,1:T(8,128)S(1)}, f32[2048,39]{0,1:T(8,128)}, u32[]{:S(2)}) copy-start(f32[2048,39]{0,1:T(8,128)} %param.25) | copy-start | bytes 958468
  965.2 51.2 %copy-start.10 = (f32[2048,39]{0,1:T(8,128)}, f32[2048,39]{0,1:T(8,128)S(1)}, u32[]{:S(2)}) copy-start(f32[2048,39]{0,1:T(8,128)S(1)} %copy.157) | copy-start | bytes 958468
  (30 other events, 317.4 us)
Sparse Core Ops, SparseCore 0:
  251.0 30.3 all-gather.5
  284.9 57.2 all-gather.7
  344.3 61.9 all-gather.9
  419.4 57.1 all-gather.11
  580.6 49.7 reduce-scatter.7
  632.6 139.6 reduce-scatter.9
  778.3 107.0 reduce-scatter.5
  889.5 117.0 all-reduce.5
where the time goes:
time: 1120 us; the launch traced here: 1110 us
  waiting for transfers between devices  458 us (41%)
  local copies, waits for them, and re-layouts  379 us (34%)
  other arithmetic  117 us (10%)
  blocking collectives  73.9 us (7%)
  matrix products  47.8 us (4%)
  starting transfers between devices  16.3 us (1%)
  between operations  16.1 us (1%)
    unnamed x55, local copies, waits for them, and re-layouts  90.5 us
    unnamed x9, waiting for transfers between devices  76.2 us
    gather x1, local copies, waits for them, and re-layouts, local(): asked = my_ids[order].reshape(owners, slots)  73.7 us
    scatter-add x1, other arithmetic, local(): jnp.zeros_like(embed_table).at[local_rows].add(got_back.reshape(-1, embed))  71.7 us
    reduce_scatter x1, waiting for transfers between devices, local(): lax.psum_scatter(deep_local, ('tower', 'batch'), scatter_dimension=0, til...  70.3 us
    all_gather x1, waiting for transfers between devices, local(): lax.all_gather(cross_weight.astype(jnp.bfloat16), 'tower', axis=0, tiled=...  64.1 us
    all_gather x1, waiting for transfers between devices, local(): lax.all_gather(deep_weight.astype(jnp.bfloat16), ('tower', 'batch'), axis...  58 us
    all_gather x1, waiting for transfers between devices, local(): both = lax.all_gather(out_low[None], 'tower', axis=0, tiled=True)  56.4 us
  transfers between devices with their start and end apart: 11, of which 10 were waited for; matrix products, arithmetic and copies ran while one was open for 16% of the time, Pallas kernels for 0%

commit v1 on v0

v1 whole, which is shorter than its diff:
```python
import functools

import jax
import jax.numpy as jnp
from jax import lax
from jax.experimental import pallas as pl
from jax.experimental.pallas import tpu as pltpu
from jax.sharding import PartitionSpec as P

STEP = 5
LANES = 128
UNROLL = 64
BF16 = jnp.bfloat16
F32 = jnp.float32


def round_up(value, unit):
    return -(-value // unit) * unit


def adamw(weight, grad, first, second, rate):
    first_new = 0.9 * first + 0.1 * grad
    second_new = 0.999 * second + 0.001 * grad * grad
    update = (
        first_new / (1.0 - 0.9**STEP) / (jnp.sqrt(second_new / (1.0 - 0.999**STEP)) + 1e-08)
        + 0.01 * weight
    )
    return (first_new, second_new, weight - rate * update)


def contract(left, right, left_dim, right_dim):
    return lax.dot_general(
        left, right, (((left_dim,), (right_dim,)), ((), ())), preferred_element_type=F32
    )


def iota(shape, dim):
    return lax.broadcasted_iota(jnp.int32, shape, dim)


def in_vmem():
    return pl.BlockSpec(memory_space=pltpu.VMEM)


def in_smem():
    return pl.BlockSpec(memory_space=pltpu.SMEM)


def params(mib):
    return pltpu.CompilerParams(vmem_limit_bytes=mib * 2**20)


def slots_kernel(shift, slots, stride, ids_ref, valid_ref, asked_ref, place_ref):
    feats, half = ids_ref.shape
    owners = asked_ref.shape[0]
    before = (iota((half, half), 0) < iota((half, half), 1)).astype(BF16)
    owner_of = iota((owners, half), 0)
    slot_of = iota((slots, half), 0)
    base = jnp.zeros((owners, 1), F32)
    total = jnp.zeros((slots, 2 * owners), F32)
    for feat in range(feats):
        ids = ids_ref[feat : feat + 1, :]
        owner = lax.shift_right_logical(ids, shift)
        row = ids & ((1 << shift) - 1)
        hit = (owner_of == owner).astype(F32)
        earlier = contract(hit.astype(BF16), before, 1, 0) + base
        rank = jnp.sum(hit * earlier, axis=0, keepdims=True)
        base = base + jnp.sum(hit, axis=1, keepdims=True)
        rank = rank.astype(jnp.int32)
        spot = owner * stride + rank
        for k in range(half // LANES):
            at = feat * (half // LANES) + k
            place_ref[at : at + 1, :] = spot[:, k * LANES : k * LANES + LANES]
        high = lax.shift_right_logical(row, 8).astype(F32)
        low = (row & 255).astype(F32)
        values = jnp.concatenate([hit * high, hit * low], axis=0).astype(BF16)
        put = (slot_of == rank).astype(F32).astype(BF16)
        total = total + contract(put, values, 1, 1)
    rows = total[:, :owners] * 256.0 + total[:, owners:]
    tall = round_up(slots, LANES)
    if tall > slots:
        rows = jnp.concatenate([rows, jnp.zeros((tall - slots, owners), F32)], axis=0)
    count = jnp.sum(valid_ref[...])
    wide = asked_ref.shape[1]
    flat = rows.T
    if wide > tall:
        flat = jnp.concatenate([flat, jnp.zeros((owners, wide - tall), F32)], axis=1)
    asked_ref[...] = jnp.where(iota((owners, wide), 1) < slots, flat.astype(jnp.int32), count)


def lookup_kernel(slots, stride, ids_ref, table_ref, rows_ref, blocks_ref):
    embed, rows_own = table_ref.shape
    tall = round_up(embed, 8)
    parts = rows_own // 256
    wide = ids_ref.shape[1]
    third = stride // 3
    blocks_ref[...] = jnp.zeros_like(blocks_ref)
    for part in range(parts):
        blocks_ref[part * tall : part * tall + embed, :] = table_ref[:, part * 256 : part * 256 + 256]
    blocks = blocks_ref[...].astype(BF16)
    low_of = iota((256, wide), 0)

    def step(owner, carry):
        ids = ids_ref[pl.ds(owner, 1), :]
        high = lax.shift_right_logical(ids, 8)
        pick = (low_of == (ids & 255)).astype(F32).astype(BF16)
        found = contract(blocks, pick, 1, 0)
        mine = jnp.zeros((tall, wide), F32)
        for part in range(parts):
            mine = jnp.where(high == part, found[part * tall : part * tall + tall], mine)
        square = jnp.concatenate([mine, jnp.zeros((LANES - tall, wide), F32)], axis=0).T
        packed = square[:third]
        for piece in (1, 2):
            packed = packed + pltpu.roll(square[piece * third : piece * third + third], embed * piece, 1)
        rows_ref[pl.ds(pl.multiple_of(owner * third, 16), third), :] = packed.astype(BF16)
        return carry

    lax.fori_loop(0, ids_ref.shape[0], step, 0)


def column_map(feat, dense_width, embed):
    start = dense_width + embed * feat
    tile = start // LANES
    lane = iota((LANES, 2 * LANES), 0)
    column = iota((LANES, 2 * LANES), 1)
    hit = (column == lane + (start - tile * LANES)) & (lane < embed)
    return tile * LANES, hit.astype(F32).astype(BF16)


def inputs_kernel(feats, stride, embed, dense_width, place_ref, rows_ref, dense_ref, x_ref, far_ref, near_ref, sum_ref):
    half = near_ref.shape[0]
    third = stride // 3
    width = dense_width + embed * feats

    def unpack(owner, carry):
        block = rows_ref[pl.ds(pl.multiple_of(owner * third, 16), third), :].astype(F32)
        for piece in range(3):
            rolled = block if piece == 0 else pltpu.roll(block, LANES - embed * piece, 1)
            far_ref[pl.ds(pl.multiple_of(owner * stride + piece * third, 16), third), :] = rolled
        return carry

    lax.fori_loop(0, far_ref.shape[0] // stride, unpack, 0)
    sum_ref[...] = jnp.zeros_like(sum_ref)
    sum_ref[:, :LANES] = dense_ref[...].astype(F32)
    ones = width - width // LANES * LANES
    end = slice(width // LANES * LANES, width // LANES * LANES + LANES)
    sum_ref[:, end] += (iota((half, LANES), 1) == ones).astype(F32)
    for feat in range(feats):

        def fetch(at, carry):
            start = pl.multiple_of(at * UNROLL, UNROLL)
            window = near_ref.at[pl.ds(start, UNROLL), :]
            rows = [far_ref[pl.ds(place_ref[feat * half + start + k], 1), :] for k in range(UNROLL)]
            for k in range(UNROLL):
                window[k : k + 1, :] = rows[k]
            return carry

        lax.fori_loop(0, half // UNROLL, fetch, 0)
        start, spread = column_map(feat, dense_width, embed)
        sum_ref[:, start : start + 2 * LANES] += contract(near_ref[...].astype(BF16), spread, 1, 0)
    x_ref[...] = sum_ref[...].astype(BF16)


def send_kernel(feats, slots, stride, embed, dense_width, place_ref, dx_ref, rows_ref, far_ref, near_ref):
    half = near_ref.shape[0]
    third = stride // 3
    owners = far_ref.shape[0] // stride

    def clear(owner, carry):
        gap = stride - slots
        far_ref[pl.ds(pl.multiple_of(owner * stride + slots, 8), gap), :] = jnp.zeros((gap, LANES), F32)
        return carry

    lax.fori_loop(0, owners, clear, 0)
    for feat in range(feats):
        start, spread = column_map(feat, dense_width, embed)
        near_ref[...] = contract(dx_ref[:, start : start + 2 * LANES], spread, 1, 1)

        def put(at, carry):
            begin = pl.multiple_of(at * UNROLL, UNROLL)
            window = near_ref.at[pl.ds(begin, UNROLL), :]
            rows = [window[k : k + 1, :] for k in range(UNROLL)]
            for k in range(UNROLL):
                far_ref[pl.ds(place_ref[feat * half + begin + k], 1), :] = rows[k]
            return carry

        lax.fori_loop(0, half // UNROLL, put, 0)

    def pack(owner, carry):
        packed = jnp.zeros((third, LANES), F32)
        for piece in range(3):
            block = far_ref[pl.ds(pl.multiple_of(owner * stride + piece * third, 8), third), :]
            packed = packed + (block if piece == 0 else pltpu.roll(block, embed * piece, 1))
        rows_ref[pl.ds(pl.multiple_of(owner * third, 16), third), :] = packed.astype(BF16)
        return carry

    lax.fori_loop(0, owners, pack, 0)


def table_kernel(
    slots, stride, ids_ref, rows_ref, table_ref, first_ref, second_ref,
    grad_ref, first_new_ref, second_new_ref, table_new_ref, total_ref,
):
    embed, rows_own = table_ref.shape
    tall = round_up(embed, 8)
    parts = rows_own // 256
    wide = ids_ref.shape[1]
    third = stride // 3
    low_of = iota((256, wide), 0)
    lane = iota((1, wide), 1)
    total_ref[...] = jnp.zeros_like(total_ref)

    def step(owner, carry):
        ids = jnp.where(lane < slots, ids_ref[pl.ds(owner, 1), :], -1)
        high = lax.shift_right_arithmetic(ids, 8)
        pick = (low_of == (ids & 255)).astype(F32).astype(BF16)
        block = rows_ref[pl.ds(pl.multiple_of(owner * third, 16), third), :].astype(F32)
        pieces = [block if k == 0 else pltpu.roll(block, LANES - embed * k, 1) for k in range(3)]
        if wide > stride:
            pieces.append(jnp.zeros((wide - stride, LANES), F32))
        square = jnp.concatenate(pieces, axis=0)[:wide].T
        mine = jnp.where(iota((tall, wide), 0) < embed, square[:tall], 0.0)
        spread = [jnp.where(high == part, mine, 0.0) for part in range(parts)]
        total_ref[...] += contract(jnp.concatenate(spread, axis=0).astype(BF16), pick, 1, 1)
        return carry

    lax.fori_loop(0, ids_ref.shape[0], step, 0)
    for part in range(parts):
        here = slice(part * 256, part * 256 + 256)
        grad = total_ref[part * tall : part * tall + embed, :]
        one, two, new = adamw(table_ref[:, here], grad, first_ref[:, here], second_ref[:, here], 0.25)
        grad_ref[:, here] = grad
        first_new_ref[:, here] = one
        second_new_ref[:, here] = two
        table_new_ref[:, here] = new


def tiles(size):
    return [(at, min(256, size - at)) for at in range(0, size, 256)]


def towers_kernel(
    count_ref, bias_ref, x_ref, first_ref, second_ref, deep_ref, vec_ref, target_ref, valid_ref,
    one_ref, d_second_ref, d_first_ref, d_deep_ref, dx_ref, head_ref,
    pre_first_ref, layer_ref, pre_second_ref, two_ref, slope_ref, hidden_ref,
):
    half, wide = x_ref.shape
    hidden = deep_ref.shape[0]

    def lanes(x):
        total = x[:, :LANES]
        for at in range(LANES, x.shape[1], LANES):
            total = total + x[:, at : at + LANES]
        return total

    for at, size in tiles(wide):
        here = slice(at, at + size)
        base = x_ref[:, here].astype(F32)
        pre = contract(x_ref[...], first_ref[:, here], 1, 0) + vec_ref[0:1, here]
        layer = base * pre + base
        pre_first_ref[:, here] = pre
        layer_ref[:, here] = layer
        one_ref[:, here] = layer.astype(BF16)
    score = jnp.zeros((half, LANES), F32)
    for at, size in tiles(wide):
        here = slice(at, at + size)
        base = x_ref[:, here].astype(F32)
        pre = contract(one_ref[...], second_ref[:, here], 1, 0) + vec_ref[1:2, here]
        two = (base * pre + layer_ref[:, here]).astype(BF16)
        pre_second_ref[:, here] = pre
        two_ref[:, here] = two
        score = score + lanes(two.astype(F32) * vec_ref[3:4, here])
    for at, size in tiles(hidden):
        here = slice(at, at + size)
        pre = contract(x_ref[...], deep_ref[here, :], 1, 1) + vec_ref[2:3, here]
        gate = jax.nn.sigmoid(pre)
        out = (pre * gate).astype(BF16)
        hidden_ref[:, here] = out
        slope_ref[:, here] = gate * (1.0 + pre * (1.0 - gate))
        score = score + lanes(out.astype(F32) * vec_ref[4:5, here])
    logit = jnp.sum(score, axis=1, keepdims=True) + bias_ref[0, 0]
    target, valid = target_ref[...], valid_ref[...]
    softplus = jnp.maximum(logit, 0.0) + jnp.log1p(jnp.exp(-jnp.abs(logit)))
    loss = jnp.sum(valid * (softplus - target * logit), axis=0, keepdims=True)
    d_logit = valid * (jax.nn.sigmoid(logit) - target) / count_ref[0, 0]
    bias_grad = jnp.sum(d_logit, axis=0, keepdims=True)
    lane = iota((1, wide), 1)
    head_ref[...] = jnp.zeros_like(head_ref)
    head_ref[2:3, :] = jnp.where(lane == 0, bias_grad, jnp.where(lane == 1, loss, 0.0))
    for at, size in tiles(wide):
        here = slice(at, at + size)
        base = x_ref[:, here].astype(F32)
        d_second_ref[:, here] = (d_logit * vec_ref[3:4, here] * base).astype(BF16)
        head_ref[0:1, here] = jnp.sum(d_logit * two_ref[:, here].astype(F32), axis=0, keepdims=True)
    for at, size in tiles(hidden):
        here = slice(at, at + size)
        d_deep_ref[:, here] = (d_logit * vec_ref[4:5, here] * slope_ref[:, here]).astype(BF16)
        head_ref[1:2, here] = jnp.sum(d_logit * hidden_ref[:, here].astype(F32), axis=0, keepdims=True)
    for at, size in tiles(wide):
        here = slice(at, at + size)
        base = x_ref[:, here].astype(F32)
        d_two = d_logit * vec_ref[3:4, here]
        d_one = contract(d_second_ref[...], second_ref[here, :], 1, 1) + d_two
        d_first_ref[:, here] = (d_one * base).astype(BF16)
        layer_ref[:, here] = d_one * (1.0 + pre_first_ref[:, here]) + d_two * pre_second_ref[:, here]
    for at, size in tiles(wide):
        here = slice(at, at + size)
        dx = contract(d_first_ref[...], first_ref[here, :], 1, 1) + contract(d_deep_ref[...], deep_ref[:, here], 1, 0)
        dx_ref[:, here] = (dx + layer_ref[:, here]).astype(BF16)


def grads_kernel(
    deep_rows, core_ref, x_ref, one_ref, d_second_ref, d_first_ref, d_deep_ref, head_ref,
    keep_ref, give_ref, rest_ref, turned_ref,
):
    half, wide = x_ref.shape
    hidden = d_deep_ref.shape[1]
    towers, groups, pairs, rows, main = keep_ref.shape
    rows_c = rows - deep_rows
    even = core_ref[0, 0] == 0

    def share(value, tower, at, size, chunk, first):
        for group in range(groups):
            for pair in range(pairs):
                start = (group * pairs + pair) * 2 * chunk
                low, high = value[start : start + chunk], value[start + chunk : start + 2 * chunk]
                keep_ref[tower, group, pair, first : first + chunk, at : at + size] = jnp.where(even, low, high).astype(BF16)
                give_ref[tower, group, pair, first : first + chunk, at : at + size] = jnp.where(even, high, low).astype(BF16)

    rest_ref[...] = jnp.zeros_like(rest_ref)
    for tower, (left, right) in enumerate(((one_ref, d_second_ref), (x_ref, d_first_ref))):
        tower = 1 - tower
        turned_ref[...] = left[...].T
        for at, size in tiles(main):
            value = contract(turned_ref[...], right[:, at : at + size], 1, 0)
            share(value, tower, at, size, rows_c, 0)
            rest_ref[8 * tower : 8 * tower + 4, at : at + size] = value[main : main + 4]
        value = contract(turned_ref[...], right[:, main:wide], 1, 0)
        rest_ref[8 * tower : 8 * tower + 4, main:wide] = value[main : main + 4]
        rest_ref[8 * tower + 4 : 8 * tower + 7, :main] = value[:main].T[:3]
    bias = contract(turned_ref[main:wide, :], d_deep_ref[...], 1, 0)
    rest_ref[16:20, :hidden] = bias[:4]
    rest_ref[20:23, :] = head_ref[0:3, :]
    turned_ref[:hidden, :] = d_deep_ref[...].T
    for at, size in tiles(main):
        value = contract(turned_ref[:hidden, :], x_ref[:, at : at + size], 1, 0)
        for tower in range(towers):
            share(value[tower * (hidden // towers) : (tower + 1) * (hidden // towers)], tower, at, size, deep_rows, rows_c)


def cross_kernel(
    place_ref, near_ref, far_ref, rest_ref, weight_ref, first_ref, second_ref,
    grad_ref, first_new_ref, second_new_ref, new_ref, copy_ref,
):
    block = pl.program_id(0)
    width = weight_ref.shape[2]
    main = near_ref.shape[3]
    rows = 2 * near_ref.shape[2]
    even = (place_ref[0] & 1) == 0
    near, far = near_ref[0, 0].astype(F32), far_ref[0, 0].astype(F32)
    body = jnp.concatenate([jnp.where(even, near, far), jnp.where(even, far, near)], axis=0)
    lane = pl.multiple_of(jnp.minimum(block * rows, main - rows) // LANES * LANES, LANES)
    side = rest_ref[0, :, pl.ds(lane, LANES)]
    side = jnp.concatenate([side, jnp.zeros((LANES - 8, LANES), F32)], axis=0).T
    if rows < LANES:
        parts = [side[at : at + rows] for at in range(0, LANES, rows)]
        side = parts[0]
        for k, part in enumerate(parts):
            side = jnp.where(block % len(parts) == k, part, side)
    side = pltpu.roll(side, LANES - 4, 1)
    grad = jnp.concatenate([body, side], axis=1)
    last = jnp.concatenate([rest_ref[0], jnp.zeros((rows - 8, rest_ref.shape[2]), F32)], axis=0)
    grad = jnp.where(block == pl.num_programs(0) - 1, last, grad)[:, :width]
    one, two, new = adamw(weight_ref[:, 0, :], grad, first_ref[:, 0, :], second_ref[:, 0, :], 0.03)
    grad_ref[:, 0, :] = grad
    first_new_ref[:, 0, :] = one
    second_new_ref[:, 0, :] = two
    new_ref[:, 0, :] = new
    copy_ref[...] = new.astype(BF16)


def flip(x, axis, bit, size):
    return lax.ppermute(x, axis, [(i, i ^ bit) for i in range(size)])


def pick(x, axis, index):
    return lax.dynamic_index_in_dim(x, index, axis, keepdims=False)


def join(mine, other, axis, index):
    return jnp.where(index == 0, jnp.stack([mine, other], axis), jnp.stack([other, mine], axis))


def flip_far(x, batch, groups):
    return jnp.stack([x] + [flip(x, "batch", k * 4, batch) for k in range(1, groups)])


def in_order(parts, groups):
    far = lax.axis_index("batch") // 4
    return jnp.stack([pick(parts, 0, k ^ far) for k in range(groups)])


def local(
    dense_feats,
    category_ids,
    labels,
    valid_mask,
    embed_table,
    table_first,
    table_second,
    cross_weight,
    cross_first,
    cross_second,
    deep_weight,
    deep_first,
    deep_second,
    vectors,
    vector_first,
    vector_second,
):
    towers, batch = lax.axis_size("tower"), lax.axis_size("batch")
    owners = towers * batch
    tower, place = lax.axis_index("tower"), lax.axis_index("batch")
    core, near, far = place & 1, (place >> 1) & 1, place >> 2
    groups = batch // 4
    rows_own, embed = embed_table.shape
    examples, feats = category_ids.shape
    half = examples // towers
    width = cross_weight.shape[1]
    deep_rows = deep_weight.shape[0]
    hidden = deep_rows * owners
    dense_width = dense_feats.shape[1]
    wide = round_up(width, LANES)
    slots = half * feats // owners
    third = round_up(-(-slots // 3), 16)
    stride = 3 * third
    shift = rows_own.bit_length() - 1
    asked_wide = round_up(max(slots + 1, stride), LANES)

    def mine(x, dim):
        return lax.dynamic_slice_in_dim(x, tower * half, half, dim)

    ids = mine(category_ids.T, 1)
    valid = mine(valid_mask, 0)
    target = mine(labels, 0).astype(F32)
    dense = jnp.pad(mine(dense_feats, 0), ((0, 0), (0, LANES - dense_width)))

    asked, slot = pl.pallas_call(
        functools.partial(slots_kernel, shift, slots, stride),
        out_shape=(
            jax.ShapeDtypeStruct((owners, asked_wide), jnp.int32),
            jax.ShapeDtypeStruct((feats * half // LANES, LANES), jnp.int32),
        ),
        in_specs=[in_vmem()] * 2,
        out_specs=(in_vmem(), in_vmem()),
        compiler_params=params(32),
        name="slots",
    )(ids, valid.reshape(1, half))
    slot = slot.reshape(-1)
    arrived = lax.all_to_all(asked, ("tower", "batch"), split_axis=0, concat_axis=0, tiled=True)
    count = jnp.sum(arrived[:, slots]).astype(F32)
    table_t = embed_table.T
    found = pl.pallas_call(
        functools.partial(lookup_kernel, slots, stride),
        out_shape=jax.ShapeDtypeStruct((owners * third, LANES), BF16),
        in_specs=[in_vmem()] * 2,
        out_specs=in_vmem(),
        scratch_shapes=[pltpu.VMEM((rows_own // 256 * round_up(embed, 8), 256), F32)],
        compiler_params=params(32),
        name="lookup",
    )(arrived, table_t)
    returned = lax.all_to_all(found, ("tower", "batch"), split_axis=0, concat_axis=0, tiled=True)
    inputs = pl.pallas_call(
        functools.partial(inputs_kernel, feats, stride, embed, dense_width),
        out_shape=jax.ShapeDtypeStruct((half, wide), BF16),
        in_specs=[in_smem(), in_vmem(), in_vmem()],
        out_specs=in_vmem(),
        scratch_shapes=[
            pltpu.VMEM((owners * stride, LANES), F32),
            pltpu.VMEM((half, LANES), F32),
            pltpu.VMEM((half, wide), F32),
        ],
        compiler_params=params(48),
        name="inputs",
    )(slot, returned, dense)

    own_low = jnp.pad(cross_weight[0].astype(BF16), ((0, wide - width), (0, wide - width)))
    halves = own_low.reshape(2, wide // 2, wide)
    got = flip(pick(halves, 0, core), "tower", 1, towers)
    other_low = join(got, flip(got, "batch", 1, batch), 0, core).reshape(wide, wide)
    cross_low = (
        jnp.where(tower == 0, own_low, other_low),
        jnp.where(tower == 0, other_low, own_low),
    )
    deep_own = jnp.pad(deep_weight.astype(BF16), ((0, 0), (0, wide - width)))
    deep_low = in_order(flip_far(deep_own, batch, groups), groups)
    deep_low = join(deep_low, flip(deep_low, "batch", 2, batch), 1, near)
    deep_low = join(deep_low, flip(deep_low, "tower", 1, towers), 0, tower)
    deep_low = join(deep_low, flip(deep_low, "batch", 1, batch), 3, core).reshape(hidden, wide)

    def widen(x):
        return jnp.pad(x, (0, wide - x.shape[0]))

    vec = jnp.stack(
        [
            widen(vectors[:width]),
            widen(vectors[width : 2 * width]),
            widen(vectors[2 * width : 2 * width + hidden]),
            widen(vectors[2 * width + hidden : 3 * width + hidden]).astype(BF16).astype(F32),
            widen(vectors[3 * width + hidden : 3 * width + 2 * hidden]).astype(BF16).astype(F32),
        ]
        + [jnp.zeros((wide,), F32)] * 3
    )
    low = jax.ShapeDtypeStruct((half, wide), BF16)
    low_deep = jax.ShapeDtypeStruct((half, hidden), BF16)
    one_low, d_second, d_first, d_deep, d_inputs, heads = pl.pallas_call(
        towers_kernel,
        out_shape=(low, low, low, low_deep, low, jax.ShapeDtypeStruct((8, wide), F32)),
        in_specs=[in_smem()] * 2 + [in_vmem()] * 7,
        out_specs=(in_vmem(),) * 6,
        scratch_shapes=[
            pltpu.VMEM((half, wide), F32),
            pltpu.VMEM((half, wide), F32),
            pltpu.VMEM((half, wide), F32),
            pltpu.VMEM((half, wide), BF16),
            pltpu.VMEM((half, hidden), F32),
            pltpu.VMEM((half, hidden), BF16),
        ],
        compiler_params=params(56),
        name="towers",
    )(
        count.reshape(1, 1), vectors[-1:].reshape(1, 1), inputs, cross_low[0], cross_low[1], deep_low, vec,
        target.reshape(half, 1), valid.astype(F32).reshape(half, 1),
    )
    main = width // LANES * LANES
    rows_c = main // batch
    parts = jax.ShapeDtypeStruct((towers, groups, 2, rows_c + deep_rows, main), BF16)
    keep, give, rest = pl.pallas_call(
        functools.partial(grads_kernel, deep_rows),
        out_shape=(parts, parts, jax.ShapeDtypeStruct((24, wide), F32)),
        in_specs=[in_smem()] + [in_vmem()] * 6,
        out_specs=(in_vmem(),) * 3,
        scratch_shapes=[pltpu.VMEM((wide, half), BF16)],
        compiler_params=params(56),
        name="grads",
    )(core.reshape(1, 1), inputs, one_low, d_second, d_first, d_deep, heads)
    got = flip(give, "batch", 1, batch)

    sent = pl.pallas_call(
        functools.partial(send_kernel, feats, slots, stride, embed, dense_width),
        out_shape=jax.ShapeDtypeStruct((owners * third, LANES), BF16),
        in_specs=[in_smem(), in_vmem()],
        out_specs=in_vmem(),
        scratch_shapes=[
            pltpu.VMEM((owners * stride, LANES), F32),
            pltpu.VMEM((half, LANES), F32),
        ],
        compiler_params=params(48),
        name="send",
    )(slot, d_inputs)
    back = lax.all_to_all(sent, ("tower", "batch"), split_axis=0, concat_axis=0, tiled=True)
    shape_t = jax.ShapeDtypeStruct((embed, rows_own), F32)
    table_grad, table_one, table_two, table_new = pl.pallas_call(
        functools.partial(table_kernel, slots, stride),
        out_shape=(shape_t,) * 4,
        in_specs=[in_vmem()] * 5,
        out_specs=(in_vmem(),) * 4,
        scratch_shapes=[pltpu.VMEM((rows_own // 256 * round_up(embed, 8), 256), F32)],
        compiler_params=params(32),
        name="table",
    )(arrived, back, table_t, table_first.T, table_second.T)

    for bit in [1, 2] + [4 << k for k in range(groups.bit_length() - 1)]:
        rest = rest + flip(rest, "batch", bit, batch)
    rest = rest + flip(rest, "tower", 1, towers)

    mid = groups // 2
    other, beyond = 1 - tower, 1 - near
    keep_one, got_one, keep_two, got_two = keep[:, :mid], got[:, :mid], keep[:, mid:], got[:, mid:]
    from_tower = flip(pick(keep_one, 0, other) + pick(got_one, 0, other), "tower", 1, towers)
    from_near = flip(pick(keep_two, 2, beyond) + pick(got_two, 2, beyond), "batch", 2, batch)
    one = pick(keep_one, 0, tower) + pick(got_one, 0, tower) + from_tower
    two = pick(keep_two, 2, near) + pick(got_two, 2, near) + from_near
    one = pick(one, 1, near) + flip(pick(one, 1, beyond), "batch", 2, batch)
    two = pick(two, 0, tower) + flip(pick(two, 0, other), "tower", 1, towers)
    both = jnp.concatenate([one, two], axis=0)
    summed = pick(both, 0, far).astype(F32)
    for k in range(1, groups):
        summed = summed + flip(pick(both, 0, far ^ k), "batch", k * 4, batch).astype(F32)
    tail = lax.dynamic_slice_in_dim(rest[16 : 16 + width - main], (tower * batch + place) * deep_rows, deep_rows, 1)
    deep_grad = jnp.concatenate([summed[rows_c:], tail.T], axis=1)
    chunk = flip_far(summed[:rows_c].astype(BF16), batch, groups)
    chunk = jnp.stack([chunk, flip(chunk, "batch", 2, batch)])
    partner = flip(chunk, "batch", 1, batch)
    side = pick(rest[:16].reshape(2, 8, wide), 0, tower)[None]
    blocks = batch // 2
    rows = 2 * rows_c

    def relative(block, at):
        other = jnp.minimum(block, blocks - 1) ^ (at[0] >> 1)
        return (other & 1, other >> 1, 0, 0)

    piece = pl.BlockSpec((1, 1, rows_c, main), relative)
    slab = pl.BlockSpec((rows, 1, width), lambda block, at: (block, 0, 0))
    shape_c = jax.ShapeDtypeStruct((width, 1, width), F32)
    cross_out = pl.pallas_call(
        cross_kernel,
        grid_spec=pltpu.PrefetchScalarGridSpec(
            num_scalar_prefetch=1,
            grid=(blocks + 1,),
            in_specs=[piece, piece, pl.BlockSpec((1, 8, wide), lambda block, at: (0, 0, 0)), slab, slab, slab],
            out_specs=(slab, slab, slab, slab, pl.BlockSpec((rows, width), lambda block, at: (block, 0))),
        ),
        out_shape=(shape_c,) * 4 + (jax.ShapeDtypeStruct((width, width), BF16),),
        compiler_params=params(48),
        name="cross",
    )(
        place.reshape(1), chunk, partner, side,
        cross_weight.transpose(1, 0, 2), cross_first.transpose(1, 0, 2), cross_second.transpose(1, 0, 2),
    )
    cross_grad, cross_one, cross_two, cross_new = (x.transpose(1, 0, 2) for x in cross_out[:4])
    vector_grad = jnp.concatenate(
        [rest[3, :width], rest[11, :width], rest[19, :hidden], rest[20, :width], rest[21, :hidden], rest[22, :1]]
    )
    loss_sum = rest[22, 1]
    deep_one, deep_two, deep_new = adamw(deep_weight, deep_grad, deep_first, deep_second, 0.03)
    vector_one, vector_two, vector_new = adamw(vectors, vector_grad, vector_first, vector_second, 0.03)
    return (
        loss_sum,
        count,
        cross_grad,
        cross_one,
        cross_two,
        cross_new,
        cross_out[4][None],
        deep_grad,
        deep_one,
        deep_two,
        deep_new,
        deep_new.astype(BF16),
        table_grad.T,
        table_one.T,
        table_two.T,
        table_new.T,
        vector_grad,
        vector_one,
        vector_two,
        vector_new,
    )


def solution(mesh):
    both = P(("tower", "batch"), None)
    cross = P("tower", None, None)
    return jax.shard_map(
        local,
        mesh=mesh,
        in_specs=(
            P("batch", None),
            P("batch", None),
            P("batch"),
            P("batch"),
            both,
            both,
            both,
            cross,
            cross,
            cross,
            both,
            both,
            both,
            P(),
            P(),
            P(),
        ),
        out_specs=(P(), P()) + (cross,) * 5 + (both,) * 9 + (P(),) * 4,
        check_vma=False,
    )
```

time: 1120 us -> 360 us (0.32)
  waiting for transfers between devices: 458 us -> 75.2 us
  local copies, waits for them, and re-layouts: 379 us -> 35.1 us
  Pallas kernels: 0 us -> 132 us
  other arithmetic: 117 us -> 32 us
  matrix products: 47.8 us -> 0 us
  blocking collectives: 73.9 us -> 28.3 us
  starting transfers between devices: 16.3 us -> 47.7 us
  between operations: 16.1 us -> 3.53 us
    gather x4 -> x0, local copies, waits for them, and re-layouts: 216 us -> none  [the longest x1 73.7 us: local(): asked = my_ids[order].reshape(owners, slots)]
    all_gather x4 -> x0, waiting for transfers between devices: 204 us -> none  [the longest x1 64.1 us: local(): lax.all_gather(cross_weight.astype(jnp.bfloat16), 'tower', axis=0, tiled=...]
    pallas_call x0 -> x8, Pallas kernels: none -> 132 us  [the longest x1 23.9 us: local(): pl.pallas_call(functools.partial(send_kernel, feats, slots, stride, embed...]
    reduce_scatter x2 -> x0, waiting for transfers between devices: 107 us -> none  [the longest x1 70.3 us: local(): lax.psum_scatter(deep_local, ('tower', 'batch'), scatter_dimension=0, til...]
    unnamed x55 -> x63, local copies, waits for them, and re-layouts: 90.5 us -> 6.56 us
    unnamed x9 -> x0, waiting for transfers between devices: 76.2 us -> none
    psum x2 -> x0, blocking collectives: 73.9 us -> none  [the longest x1 40.1 us: local(): lax.psum((vector_local, loss_part), ('tower', 'batch'))]
    scatter-add x1 -> x0, other arithmetic: 71.7 us -> none  [local(): jnp.zeros_like(embed_table).at[local_rows].add(got_back.reshape(-1, embed))]
  transfers between devices with their start and end apart: 11 -> 28, of which waited for: 10 -> 13; matrix products, arithmetic and copies ran while one was open for 16% -> 15% of each run, Pallas kernels for 0% -> 16%
where the time goes in v1:
time: 360 us; the launch traced here: 354 us
  Pallas kernels  132 us (37%)
  waiting for transfers between devices  75.2 us (21%)
  starting transfers between devices  47.7 us (13%)
  local copies, waits for them, and re-layouts  35.1 us (10%)
  other arithmetic  32 us (9%)
  blocking collectives  28.3 us (8%)
    ppermute x26, waiting for transfers between devices, flip(): return lax.ppermute(x, axis, [(i, i ^ bit) for i in range(size)])  56.2 us
    ppermute x26, starting transfers between devices, flip(): return lax.ppermute(x, axis, [(i, i ^ bit) for i in range(size)])  39.4 us
    all_to_all x1, blocking collectives, local(): lax.all_to_all(asked, ('tower', 'batch'), split_axis=0, concat_axis=0, ti...  28.3 us
    pallas_call x1, Pallas kernels, local(): pl.pallas_call(functools.partial(send_kernel, feats, slots, stride, embed...  23.9 us
    pallas_call x1, Pallas kernels, local(): pl.pallas_call(cross_kernel, grid_spec=pltpu.PrefetchScalarGridSpec(num_s...  23.8 us
    pallas_call x1, Pallas kernels, local(): pl.pallas_call(functools.partial(inputs_kernel, feats, stride, embed, den...  21.1 us
    all_to_all x1, waiting for transfers between devices, local(): lax.all_to_all(found, ('tower', 'batch'), split_axis=0, concat_axis=0, ti...  19 us
    pallas_call x1, Pallas kernels, local(): pl.pallas_call(towers_kernel, out_shape=(low, low, low, low_deep, low, ja...  16.9 us
  transfers between devices with their start and end apart: 28, of which 13 were waited for; matrix products, arithmetic and copies ran while one was open for 15% of the time, Pallas kernels for 16%

profile of v1, /device:TPU:0, one launch (start us, length us, event | category | flops | bytes accessed | tf_op | source)
XLA Modules:
  0.0 353.9 jit_solution(7896661504631927566)
XLA Ops:
  1.7 3.1 collective-permute-start.2
  18.0 2.7 collective-permute-done.5
  23.3 7.2 %slots.1 = (s32[32,512]{1,0:T(8,128)S(1)}, s32[104,128]{1,0:T(8,128)S(1)}) custom-call(s32[26,512]{1,0:T(8,128)S(1)} %dynamic-slice_bitcast_fusion.3.ids_ref, s32[1,512]{1,0:T(1,128)S(1)} %bitcast.126), custom_call_target="tpu_custom_call" | custom-call | tf_op jit(solution)/shard_map/slots/pallas_call | solution.py:448
  30.6 28.3 %all_to_all.33 = s32[32,1,512]{2,1,0:T(1,128)S(1)} all-to-all(s32[32,1,512]{2,1,0:T(1,128)S(1)} %copy.76), channel_id=1, replica_groups=mesh['tower'=2,'batch'=16] {'tower','batch'}, dimensions={0} | all-to-all | bytes 131072 | tf_op jit(solution)/shard_map/all_to_all | solution.py:460
  58.9 15.9 %lookup.1 = bf16[4608,128]{1,0:T(8,128)(2,1)} custom-call(s32[32,512]{1,0:T(8,128)S(1)} %bitcast.118, f32[39,2048]{1,0:T(8,128)S(1)} %bitcast.116), custom_call_target="tpu_custom_call" | custom-call | tf_op jit(solution)/shard_map/lookup/pallas_call | solution.py:463
  74.8 5.4 %all-to-all-start.1 = ((bf16[32,144,128]{2,1,0:T(8,128)(2,1)}), bf16[32,144,128]{2,1,0:T(8,128)(2,1)S(1)}, u32[]{:S(2)}, u32[]{:S(2)}) async-start(bf16[32,144,128]{2,1,0:T(8,128)(2,1)} %bitcast.6), calls=%async_computation.1 | async-start | bytes 2359296 | tf_op jit(solution)/shard_map/all_to_all | solution.py:472
  91.2 19.0 %all-to-all-done.1 = bf16[32,144,128]{2,1,0:T(8,128)(2,1)S(1)} async-done(((bf16[32,144,128]{2,1,0:T(8,128)(2,1)}), bf16[32,144,128]{2,1,0:T(8,128)(2,1)S(1)}, u32[]{:S(2)}, u32[]{:S(2)}) %all-to-all-start.1) | async-done | bytes 1179680 | tf_op jit(solution)/shard_map/all_to_all | solution.py:472
  110.2 21.1 %inputs.1.x_ref = bf16[512,1152]{1,0:T(8,128)(2,1)S(1)} custom-call(s32[13312]{0:T(1024)S(1)} %bitcast.123, bf16[4608,128]{1,0:T(8,128)(2,1)S(1)} %bitcast.114, bf16[512,128]{1,0:T(8,128)(2,1)S(1)} %pad.31.dense_ref), custom_call_target="tpu_custom_call" | custom-call | tf_op jit(solution)/shard_map/inputs/pallas_call | solution.py:473
  131.3 3.4 maximum_select_fusion
  135.0 3.5 bitcast_select_fusion
  138.5 16.9 %towers.1 = (bf16[512,1152]{1,0:T(8,128)(2,1)}, bf16[512,1152]{1,0:T(8,128)(2,1)}, bf16[512,1152]{1,0:T(8,128)(2,1)}, bf16[512,1024]{1,0:T(8,128)(2,1)}, bf16[512,1152]{1,0:T(8,128)(2,1)}, /*index=5*/f32[8,1152]{1,0:T(8,128)}) custom-call(f32[1,1]{1,0:T(1,128)} %bitcast.8.count_ref, f32[1,1]{1,0:T(1,128)} %bitcast.9.bias_ref, bf16[512,1152]{1,0:T(8,128)(2,1)} %copy-done.2, ...), custom_call_target="tpu_custom_call" | custom-call | tf_op jit(solution)/shard_map/towers/pallas_call | solution.py:516
  155.4 10.1 %grads.1 = (bf16[2,4,2,96,1024]{4,3,2,1,0:T(8,128)(2,1)}, bf16[2,4,2,96,1024]{4,3,2,1,0:T(8,128)(2,1)}, f32[24,1152]{1,0:T(8,128)}) custom-call(s32[1,1]{1,0:T(1,128)} %bitcast.core_ref, bf16[512,1152]{1,0:T(8,128)(2,1)} %copy-done.2, bf16[512,1152]{1,0:T(8,128)(2,1)} %get-tuple-element.42.one_ref, bf16[512,1152]{1,0:T(8,128)(2,1)} %get-tuple-element.43.d_second_ref, ...), custom_call_target="tpu_custom_call" | custom-call | tf_op jit(solution)/shard_map/grads/pallas_call | solution.py:538
  168.0 3.5 %collective-permute-done.13 = bf16[2,4,2,96,1024]{4,3,2,1,0:T(8,128)(2,1)} collective-permute-done((bf16[2,4,2,96,1024]{4,3,2,1,0:T(8,128)(2,1)}, bf16[2,4,2,96,1024]{4,3,2,1,0:T(8,128)(2,1)}, u32[]{:S(2)}, u32[]{:S(2)}) %collective-permute-start.13) | collective-permute-done | bytes 3145760 | tf_op jit(solution)/shard_map/ppermute | solution.py:383
  171.5 3.4 fusion.23
  181.8 13.8 %collective-permute-done.16 = bf16[2,2,96,1024]{3,2,1,0:T(8,128)(2,1)S(1)} collective-permute-done((bf16[2,2,96,1024]{3,2,1,0:T(8,128)(2,1)S(1)}, bf16[2,2,96,1024]{3,2,1,0:T(8,128)(2,1)S(1)}, u32[]{:S(2)}, u32[]{:S(2)}) %collective-permute-start.16) | collective-permute-done | bytes 786464 | tf_op jit(solution)/shard_map/ppermute | solution.py:383
  203.8 23.9 %send.1 = bf16[4608,128]{1,0:T(8,128)(2,1)} custom-call(s32[13312]{0:T(1024)S(1)} %bitcast.124, bf16[512,1152]{1,0:T(8,128)(2,1)S(1)} %copy-done.4), custom_call_target="tpu_custom_call" | custom-call | tf_op jit(solution)/shard_map/send/pallas_call | solution.py:549
  227.7 2.9 all-to-all-start.2
  247.5 17.9 %collective-permute-done.10 = f32[24,1152]{1,0:T(8,128)S(1)} collective-permute-done((f32[24,1152]{1,0:T(8,128)S(1)}, f32[24,1152]{1,0:T(8,128)S(1)}, u32[]{:S(2)}, u32[]{:S(2)}) %collective-permute-start.10) | collective-permute-done | bytes 110624 | tf_op jit(solution)/shard_map/ppermute | solution.py:383
  267.8 4.7 %collective-permute-start.11 = (f32[24,1152]{1,0:T(8,128)S(1)}, f32[24,1152]{1,0:T(8,128)S(1)}, u32[]{:S(2)}, u32[]{:S(2)}) collective-permute-start(f32[24,1152]{1,0:T(8,128)S(1)} %copy.86), channel_id=1, source_target_pairs={{0,8},{1,9},{2,10},{3,11},{4,12},{5,13},{6,14},{7,15},{8,0},{9,1},... | collective-permute-start | bytes 331784 | tf_op jit(solution)/shard_map/ppermute | solution.py:383
  274.3 7.2 %collective-permute-start.21 = (bf16[64,1024]{1,0:T(8,128)(2,1)S(1)}, bf16[64,1024]{1,0:T(8,128)(2,1)S(1)}, u32[]{:S(2)}, u32[]{:S(2)}) collective-permute-start(bf16[64,1024]{1,0:T(8,128)(2,1)S(1)} %slice.117), channel_id=1, source_target_pairs={{0,4},{1,5},{2,6},{3,7},{4,0},{5,1},{6,2},{7,3},{8,12},{9,13},{10,... | collective-permute-start | bytes 393224 | tf_op jit(solution)/shard_map/ppermute | solution.py:383
  285.7 8.0 %collective-permute-done.22 = bf16[64,1024]{1,0:T(8,128)(2,1)S(1)} collective-permute-done((bf16[64,1024]{1,0:T(8,128)(2,1)S(1)}, bf16[64,1024]{1,0:T(8,128)(2,1)S(1)}, u32[]{:S(2)}, u32[]{:S(2)}) %collective-permute-start.22) | collective-permute-done | bytes 131104 | tf_op jit(solution)/shard_map/ppermute | solution.py:383
  300.2 3.1 collective-permute-done.12
  314.4 13.2 %table.1 = (f32[39,2048]{1,0:T(8,128)}, f32[39,2048]{1,0:T(8,128)}, f32[39,2048]{1,0:T(8,128)}, f32[39,2048]{1,0:T(8,128)}) custom-call(s32[32,512]{1,0:T(8,128)S(1)} %bitcast.120, bf16[4608,128]{1,0:T(8,128)(2,1)S(1)} %bitcast.115, f32[39,2048]{1,0:T(8,128)S(1)} %bitcast.117, f32[39,2048]{1,0:T(8,128)S(1)} %bitcast.121, f32[39,2048]{1,0:T(8,128)S(1)} %bitcast.122), custom_call_target="tpu_custom_call" | custom-call | tf_op jit(solution)/shard_map/table/pallas_call | solution.py:563
  328.5 23.8 %cross.1 = (f32[1027,1,1027]{2,1,0:T(1,128)}, f32[1027,1,1027]{2,1,0:T(1,128)}, f32[1027,1,1027]{2,1,0:T(1,128)}, f32[1027,1,1027]{2,1,0:T(1,128)}, bf16[1027,1027]{1,0:T(8,128)(2,1)}) custom-call(s32[1]{0:T(128)} %bitcast.32.place_ref, bf16[2,4,64,1024]{3,2,1,0:T(8,128)(2,1)S(1)} %pad_maximum_fusion.near_ref, ...), custom_call_target="tpu_custom_call" | custom-call | tf_op jit(solution)/shard_map/cross/pallas_call | solution.py:606
  (190 shorter events, 88.5 us)
Async XLA Ops:
  1.7 9.7 %collective-permute-start.2 = (bf16[32,1152]{1,0:T(8,128)(2,1)S(1)}, bf16[32,1152]{1,0:T(8,128)(2,1)S(1)}, u32[]{:S(2)}, u32[]{:S(2)}) collective-permute-start(bf16[32,1152]{1,0:T(8,128)(2,1)S(1)} %get-tuple-element.94), channel_id=1, source_target_pairs={{0,4},{1,5},{2,6},{3,7},{4,0},{5,1},{6,2},{7,3},{8,12},{9,13},{10,... | collective-permute-start | bytes 221192 | tf_op jit(solution)/shard_map/ppermute | solution.py:383
  4.7 7.8 %collective-permute-start.3 = (bf16[32,1152]{1,0:T(8,128)(2,1)S(1)}, bf16[32,1152]{1,0:T(8,128)(2,1)S(1)}, u32[]{:S(2)}, u32[]{:S(2)}) collective-permute-start(bf16[32,1152]{1,0:T(8,128)(2,1)S(1)} %get-tuple-element.94), channel_id=1, source_target_pairs={{0,8},{1,9},{2,10},{3,11},{4,12},{5,13},{6,14},{7,15},{8,0},{9,1},... | collective-permute-start | bytes 221192 | tf_op jit(solution)/shard_map/ppermute | solution.py:383
  13.8 7.0 %collective-permute-start.5 = (bf16[4,32,1152]{2,1,0:T(8,128)(2,1)S(1)}, bf16[4,32,1152]{2,1,0:T(8,128)(2,1)S(1)}, u32[]{:S(2)}, u32[]{:S(2)}) collective-permute-start(bf16[4,32,1152]{2,1,0:T(8,128)(2,1)S(1)} %get-tuple-element.88), channel_id=1, source_target_pairs={{0,2},{1,3},{2,0},{3,1},{4,6},{5,7},{6,4},{7,5},{8,10},{9,11},{10,... | collective-permute-start | bytes 884744 | tf_op jit(solution)/shard_map/ppermute | solution.py:383
  16.5 65.6 %collective-permute-start = (bf16[576,1152]{1,0:T(8,128)(2,1)}, bf16[576,1152]{1,0:T(8,128)(2,1)}, u32[]{:S(2)}, u32[]{:S(2)}) collective-permute-start(bf16[576,1152]{1,0:T(8,128)(2,1)} %dynamic-slice_bitcast_fusion), channel_id=1, source_target_pairs={{0,16},{16,0},{1,17},{17,1},{2,18},{18,2},{3,19},{19,3},{4,20},{20... | collective-permute-start | bytes 3981320 | tf_op jit(solution)/shard_map/ppermute | solution.py:383
  21.7 58.8 %collective-permute-start.6 = (bf16[4,2,32,1152]{3,2,0,1:T(8,128)(2,1)}, bf16[4,2,32,1152]{3,2,0,1:T(8,128)(2,1)S(1)}, u32[]{:S(2)}, u32[]{:S(2)}) collective-permute-start(bf16[4,2,32,1152]{3,2,0,1:T(8,128)(2,1)} %maximum_select_fusion.5), channel_id=1, source_target_pairs={{0,16},{16,0},{1,17},{17,1},{2,18},{18,2},{3,19},{19,3},{4,20},{20... | collective-permute-start | bytes 1769480 | tf_op jit(solution)/shard_map/ppermute | solution.py:383
  74.8 35.4 %all-to-all-start.1 = ((bf16[32,144,128]{2,1,0:T(8,128)(2,1)}), bf16[32,144,128]{2,1,0:T(8,128)(2,1)S(1)}, u32[]{:S(2)}, u32[]{:S(2)}) async-start(bf16[32,144,128]{2,1,0:T(8,128)(2,1)} %bitcast.6), calls=%async_computation.1 | async-start | bytes 2359296 | tf_op jit(solution)/shard_map/all_to_all | solution.py:472
  82.1 49.2 %collective-permute-start.1 = (bf16[576,1152]{1,0:T(8,128)(2,1)}, bf16[576,1152]{1,0:T(8,128)(2,1)}, u32[]{:S(2)}, u32[]{:S(2)}) collective-permute-start(bf16[576,1152]{1,0:T(8,128)(2,1)} %collective-permute-done), channel_id=1, source_target_pairs={{0,1},{1,0},{2,3},{3,2},{4,5},{5,4},{6,7},{7,6},{8,9},{9,8},{10,11... | collective-permute-start | bytes 3981320 | tf_op jit(solution)/shard_map/ppermute | solution.py:383
  176.0 19.6 %collective-permute-start.16 = (bf16[2,2,96,1024]{3,2,1,0:T(8,128)(2,1)S(1)}, bf16[2,2,96,1024]{3,2,1,0:T(8,128)(2,1)S(1)}, u32[]{:S(2)}, u32[]{:S(2)}) collective-permute-start(bf16[2,2,96,1024]{3,2,1,0:T(8,128)(2,1)S(1)} %fusion.3), channel_id=1, source_target_pairs={{0,2},{1,3},{2,0},{3,1},{4,6},{5,7},{6,4},{7,5},{8,10},{9,11},{10,... | collective-permute-start | bytes 2359304 | tf_op jit(solution)/shard_map/ppermute | solution.py:383
  181.3 20.3 %collective-permute-start.14 = (bf16[2,2,96,1024]{3,2,1,0:T(8,128)(2,1)}, bf16[2,2,96,1024]{3,2,1,0:T(8,128)(2,1)}, u32[]{:S(2)}, u32[]{:S(2)}) collective-permute-start(bf16[2,2,96,1024]{3,2,1,0:T(8,128)(2,1)} %add_bitcast_fusion), channel_id=1, source_target_pairs={{0,16},{16,0},{1,17},{17,1},{2,18},{18,2},{3,19},{19,3},{4,20},{20... | collective-permute-start | bytes 2359304 | tf_op jit(solution)/shard_map/ppermute | solution.py:383
  197.9 35.5 %collective-permute-start.17 = (bf16[2,96,1024]{2,1,0:T(8,128)(2,1)}, bf16[2,96,1024]{2,1,0:T(8,128)(2,1)}, u32[]{:S(2)}, u32[]{:S(2)}) collective-permute-start(bf16[2,96,1024]{2,1,0:T(8,128)(2,1)} %dynamic-slice_bitcast_fusion.1), channel_id=1, source_target_pairs={{0,16},{16,0},{1,17},{17,1},{2,18},{18,2},{3,19},{19,3},{4,20},{20... | collective-permute-start | bytes 1179656 | tf_op jit(solution)/shard_map/ppermute | solution.py:383
  203.7 30.7 %collective-permute-start.15 = (bf16[2,96,1024]{2,1,0:T(8,128)(2,1)}, bf16[2,96,1024]{2,1,0:T(8,128)(2,1)}, u32[]{:S(2)}, u32[]{:S(2)}) collective-permute-start(bf16[2,96,1024]{2,1,0:T(8,128)(2,1)} %dynamic-slice_bitcast_fusion.2), channel_id=1, source_target_pairs={{0,2},{1,3},{2,0},{3,1},{4,6},{5,7},{6,4},{7,5},{8,10},{9,11},{10,... | collective-permute-start | bytes 1179656 | tf_op jit(solution)/shard_map/ppermute | solution.py:383
  203.7 26.8 %collective-permute-start.8 = (f32[24,1152]{1,0:T(8,128)S(1)}, f32[24,1152]{1,0:T(8,128)}, u32[]{:S(2)}, u32[]{:S(2)}) collective-permute-start(f32[24,1152]{1,0:T(8,128)S(1)} %copy-done.23), channel_id=1, source_target_pairs={{0,1},{1,0},{2,3},{3,2},{4,5},{5,4},{6,7},{7,6},{8,9},{9,8},{10,11... | collective-permute-start | bytes 331784 | tf_op jit(solution)/shard_map/ppermute | solution.py:383
  227.7 86.8 %all-to-all-start.2 = ((bf16[32,144,128]{2,1,0:T(8,128)(2,1)}), bf16[32,144,128]{2,1,0:T(8,128)(2,1)S(1)}, u32[]{:S(2)}, u32[]{:S(2)}) async-start(bf16[32,144,128]{2,1,0:T(8,128)(2,1)} %bitcast.62), calls=%async_computation.2 | async-start | bytes 2359296 | tf_op jit(solution)/shard_map/all_to_all | solution.py:561
  231.6 10.5 %collective-permute-start.9 = (f32[24,1152]{1,0:T(8,128)S(1)}, f32[24,1152]{1,0:T(8,128)}, u32[]{:S(2)}, u32[]{:S(2)}) collective-permute-start(f32[24,1152]{1,0:T(8,128)S(1)} %add.181), channel_id=1, source_target_pairs={{0,2},{1,3},{2,0},{3,1},{4,6},{5,7},{6,4},{7,5},{8,10},{9,11},{10,... | collective-permute-start | bytes 331784 | tf_op jit(solution)/shard_map/ppermute | solution.py:383
  236.5 35.9 %collective-permute-start.18 = (bf16[96,1024]{1,0:T(8,128)(2,1)}, bf16[96,1024]{1,0:T(8,128)(2,1)}, u32[]{:S(2)}, u32[]{:S(2)}) collective-permute-start(bf16[96,1024]{1,0:T(8,128)(2,1)} %get-tuple-element.79), channel_id=1, source_target_pairs={{0,4},{1,5},{2,6},{3,7},{4,0},{5,1},{6,2},{7,3},{8,12},{9,13},{10,... | collective-permute-start | bytes 589832 | tf_op jit(solution)/shard_map/ppermute | solution.py:383
  238.1 34.8 %collective-permute-start.19 = (bf16[96,1024]{1,0:T(8,128)(2,1)}, bf16[96,1024]{1,0:T(8,128)(2,1)}, u32[]{:S(2)}, u32[]{:S(2)}) collective-permute-start(bf16[96,1024]{1,0:T(8,128)(2,1)} %get-tuple-element.80), channel_id=1, source_target_pairs={{0,8},{1,9},{2,10},{3,11},{4,12},{5,13},{6,14},{7,15},{8,0},{9,1},... | collective-permute-start | bytes 589832 | tf_op jit(solution)/shard_map/ppermute | solution.py:383
  240.6 32.3 %collective-permute-start.20 = (bf16[96,1024]{1,0:T(8,128)(2,1)S(1)}, bf16[96,1024]{1,0:T(8,128)(2,1)}, u32[]{:S(2)}, u32[]{:S(2)}) collective-permute-start(bf16[96,1024]{1,0:T(8,128)(2,1)S(1)} %get-tuple-element.81), channel_id=1, source_target_pairs={{0,12},{1,13},{2,14},{3,15},{4,8},{5,9},{6,10},{7,11},{8,4},{9,5},... | collective-permute-start | bytes 589832 | tf_op jit(solution)/shard_map/ppermute | solution.py:383
  245.6 19.9 %collective-permute-start.10 = (f32[24,1152]{1,0:T(8,128)S(1)}, f32[24,1152]{1,0:T(8,128)S(1)}, u32[]{:S(2)}, u32[]{:S(2)}) collective-permute-start(f32[24,1152]{1,0:T(8,128)S(1)} %copy.84), channel_id=1, source_target_pairs={{0,4},{1,5},{2,6},{3,7},{4,0},{5,1},{6,2},{7,3},{8,12},{9,13},{10,... | collective-permute-start | bytes 331784 | tf_op jit(solution)/shard_map/ppermute | solution.py:383
  267.8 28.3 %collective-permute-start.11 = (f32[24,1152]{1,0:T(8,128)S(1)}, f32[24,1152]{1,0:T(8,128)S(1)}, u32[]{:S(2)}, u32[]{:S(2)}) collective-permute-start(f32[24,1152]{1,0:T(8,128)S(1)} %copy.86), channel_id=1, source_target_pairs={{0,8},{1,9},{2,10},{3,11},{4,12},{5,13},{6,14},{7,15},{8,0},{9,1},... | collective-permute-start | bytes 331784 | tf_op jit(solution)/shard_map/ppermute | solution.py:383
  274.3 11.4 %collective-permute-start.21 = (bf16[64,1024]{1,0:T(8,128)(2,1)S(1)}, bf16[64,1024]{1,0:T(8,128)(2,1)S(1)}, u32[]{:S(2)}, u32[]{:S(2)}) collective-permute-start(bf16[64,1024]{1,0:T(8,128)(2,1)S(1)} %slice.117), channel_id=1, source_target_pairs={{0,4},{1,5},{2,6},{3,7},{4,0},{5,1},{6,2},{7,3},{8,12},{9,13},{10,... | collective-permute-start | bytes 393224 | tf_op jit(solution)/shard_map/ppermute | solution.py:383
  281.5 12.2 %collective-permute-start.22 = (bf16[64,1024]{1,0:T(8,128)(2,1)S(1)}, bf16[64,1024]{1,0:T(8,128)(2,1)S(1)}, u32[]{:S(2)}, u32[]{:S(2)}) collective-permute-start(bf16[64,1024]{1,0:T(8,128)(2,1)S(1)} %slice.117), channel_id=1, source_target_pairs={{0,8},{1,9},{2,10},{3,11},{4,12},{5,13},{6,14},{7,15},{8,0},{9,1},... | collective-permute-start | bytes 393224 | tf_op jit(solution)/shard_map/ppermute | solution.py:383
  281.5 12.2 %collective-permute-start.23 = (bf16[64,1024]{1,0:T(8,128)(2,1)S(1)}, bf16[64,1024]{1,0:T(8,128)(2,1)S(1)}, u32[]{:S(2)}, u32[]{:S(2)}) collective-permute-start(bf16[64,1024]{1,0:T(8,128)(2,1)S(1)} %slice.117), channel_id=1, source_target_pairs={{0,12},{1,13},{2,14},{3,15},{4,8},{5,9},{6,10},{7,11},{8,4},{9,5},... | collective-permute-start | bytes 393224 | tf_op jit(solution)/shard_map/ppermute | solution.py:383
  294.7 15.5 %collective-permute-start.24 = (bf16[4,64,1024]{2,1,0:T(8,128)(2,1)}, bf16[4,64,1024]{2,1,0:T(8,128)(2,1)}, u32[]{:S(2)}, u32[]{:S(2)}) collective-permute-start(bf16[4,64,1024]{2,1,0:T(8,128)(2,1)} %get-tuple-element.85), channel_id=1, source_target_pairs={{0,2},{1,3},{2,0},{3,1},{4,6},{5,7},{6,4},{7,5},{8,10},{9,11},{10,... | collective-permute-start | bytes 1572872 | tf_op jit(solution)/shard_map/ppermute | solution.py:383
  311.6 16.9 %collective-permute-start.25 = (bf16[2,4,64,1024]{3,2,1,0:T(8,128)(2,1)S(1)}, bf16[2,4,64,1024]{3,2,1,0:T(8,128)(2,1)}, u32[]{:S(2)}, u32[]{:S(2)}) collective-permute-start(bf16[2,4,64,1024]{3,2,1,0:T(8,128)(2,1)S(1)} %pad_maximum_fusion.near_ref), channel_id=1, source_target_pairs={{0,1},{1,0},{2,3},{3,2},{4,5},{5,4},{6,7},{7,6},{8,9},{9,8},{10,11... | collective-permute-start | bytes 3145736 | tf_op jit(solution)/shard_map/ppermute | solution.py:383
  (35 other events, 339.1 us)

commit v2 on v1

--- a/solution.py
+++ b/solution.py
@@ -9,7 +9,7 @@
 
 STEP = 5
 LANES = 128
-UNROLL = 64
+CHUNK = 128
 BF16 = jnp.bfloat16
 F32 = jnp.float32
 
@@ -48,6 +48,10 @@
 
 def params(mib):
     return pltpu.CompilerParams(vmem_limit_bytes=mib * 2**20)
+
+
+def takes(micros):
+    return pl.CostEstimate(flops=0, bytes_accessed=micros * 3_000_000, transcendentals=0)
 
 
 def slots_kernel(shift, slots, stride, ids_ref, valid_ref, asked_ref, place_ref):
@@ -115,20 +119,20 @@
         rows_ref[pl.ds(pl.multiple_of(owner * third, 16), third), :] = packed.astype(BF16)
         return carry
 
-    lax.fori_loop(0, ids_ref.shape[0], step, 0)
-
-
-def column_map(feat, dense_width, embed):
+    lax.fori_loop(0, ids_ref.shape[0], step, 0, unroll=4)
+
+
+def column_map(feat, dense_width, embed, turned):
     start = dense_width + embed * feat
     tile = start // LANES
-    lane = iota((LANES, 2 * LANES), 0)
-    column = iota((LANES, 2 * LANES), 1)
+    shape = (2 * LANES, LANES) if turned else (LANES, 2 * LANES)
+    column, lane = iota(shape, 1 - turned), iota(shape, turned)
     hit = (column == lane + (start - tile * LANES)) & (lane < embed)
-    return tile * LANES, hit.astype(F32).astype(BF16)
-
-
-def inputs_kernel(feats, stride, embed, dense_width, place_ref, rows_ref, dense_ref, x_ref, far_ref, near_ref, sum_ref):
-    half = near_ref.shape[0]
+    return pl.multiple_of(tile * LANES, LANES), hit.astype(F32).astype(BF16)
+
+
+def inputs_kernel(feats, stride, embed, dense_width, place_ref, rows_ref, dense_ref, x_ref, far_ref, even_ref, odd_ref, sum_ref):
+    half = even_ref.shape[0]
     third = stride // 3
     width = dense_width + embed * feats
 
@@ -139,30 +143,44 @@
             far_ref[pl.ds(pl.multiple_of(owner * stride + piece * third, 16), third), :] = rolled
         return carry
 
-    lax.fori_loop(0, far_ref.shape[0] // stride, unpack, 0)
+    lax.fori_loop(0, far_ref.shape[0] // stride, unpack, 0, unroll=4)
     sum_ref[...] = jnp.zeros_like(sum_ref)
     sum_ref[:, :LANES] = dense_ref[...].astype(F32)
     ones = width - width // LANES * LANES
     end = slice(width // LANES * LANES, width // LANES * LANES + LANES)
     sum_ref[:, end] += (iota((half, LANES), 1) == ones).astype(F32)
-    for feat in range(feats):
-
-        def fetch(at, carry):
-            start = pl.multiple_of(at * UNROLL, UNROLL)
-            window = near_ref.at[pl.ds(start, UNROLL), :]
-            rows = [far_ref[pl.ds(place_ref[feat * half + start + k], 1), :] for k in range(UNROLL)]
-            for k in range(UNROLL):
-                window[k : k + 1, :] = rows[k]
-            return carry
-
-        lax.fori_loop(0, half // UNROLL, fetch, 0)
-        start, spread = column_map(feat, dense_width, embed)
-        sum_ref[:, start : start + 2 * LANES] += contract(near_ref[...].astype(BF16), spread, 1, 0)
+    odd_ref[...] = jnp.zeros_like(odd_ref)
+
+    def add(ref, at, spread):
+        start, spread = spread
+        here = slice(at, at + CHUNK)
+        sum_ref[here, pl.ds(start, 2 * LANES)] += contract(ref[here, :].astype(BF16), spread, 1, 0)
+
+    def fetch(feat, ref, at):
+        rows = [far_ref[pl.ds(place_ref[feat * half + at + k], 1), :] for k in range(CHUNK)]
+        for k in range(CHUNK):
+            ref[at + k : at + k + 1, :] = rows[k]
+
+    def step(pair, carry):
+        spread = column_map(jnp.maximum(2 * pair - 1, 0), dense_width, embed, 0)
+        for at in range(0, half, CHUNK):
+            add(odd_ref, at, spread)
+            fetch(2 * pair, even_ref, at)
+        spread = column_map(2 * pair, dense_width, embed, 0)
+        for at in range(0, half, CHUNK):
+            add(even_ref, at, spread)
+            fetch(2 * pair + 1, odd_ref, at)
+        return carry
+
+    lax.fori_loop(0, feats // 2, step, 0)
+    spread = column_map(feats - 1, dense_width, embed, 0)
+    for at in range(0, half, CHUNK):
+        add(odd_ref, at, spread)
     x_ref[...] = sum_ref[...].astype(BF16)
 
 
-def send_kernel(feats, slots, stride, embed, dense_width, place_ref, dx_ref, rows_ref, far_ref, near_ref):
-    half = near_ref.shape[0]
+def send_kernel(feats, slots, stride, embed, dense_width, place_ref, dx_ref, rows_ref, far_ref, even_ref, odd_ref):
+    half = even_ref.shape[0]
     third = stride // 3
     owners = far_ref.shape[0] // stride
 
@@ -171,20 +189,34 @@
         far_ref[pl.ds(pl.multiple_of(owner * stride + slots, 8), gap), :] = jnp.zeros((gap, LANES), F32)
         return carry
 
-    lax.fori_loop(0, owners, clear, 0)
-    for feat in range(feats):
-        start, spread = column_map(feat, dense_width, embed)
-        near_ref[...] = contract(dx_ref[:, start : start + 2 * LANES], spread, 1, 1)
-
-        def put(at, carry):
-            begin = pl.multiple_of(at * UNROLL, UNROLL)
-            window = near_ref.at[pl.ds(begin, UNROLL), :]
-            rows = [window[k : k + 1, :] for k in range(UNROLL)]
-            for k in range(UNROLL):
-                far_ref[pl.ds(place_ref[feat * half + begin + k], 1), :] = rows[k]
-            return carry
-
-        lax.fori_loop(0, half // UNROLL, put, 0)
+    lax.fori_loop(0, owners, clear, 0, unroll=8)
+
+    def cut(ref, at, spread):
+        start, spread = spread
+        here = slice(at, at + CHUNK)
+        ref[here, :] = contract(dx_ref[here, pl.ds(start, 2 * LANES)], spread, 1, 0)
+
+    def put(feat, ref, at):
+        rows = [ref[at + k : at + k + 1, :] for k in range(CHUNK)]
+        for k in range(CHUNK):
+            far_ref[pl.ds(place_ref[feat * half + at + k], 1), :] = rows[k]
+
+    spread = column_map(0, dense_width, embed, 1)
+    for at in range(0, half, CHUNK):
+        cut(even_ref, at, spread)
+
+    def step(pair, carry):
+        spread = column_map(2 * pair + 1, dense_width, embed, 1)
+        for at in range(0, half, CHUNK):
+            cut(odd_ref, at, spread)
+            put(2 * pair, even_ref, at)
+        spread = column_map(jnp.minimum(2 * pair + 2, feats - 1), dense_width, embed, 1)
+        for at in range(0, half, CHUNK):
+            cut(even_ref, at, spread)
+            put(2 * pair + 1, odd_ref, at)
+        return carry
+
+    lax.fori_loop(0, feats // 2, step, 0)
 
     def pack(owner, carry):
         packed = jnp.zeros((third, LANES), F32)
@@ -194,7 +226,7 @@
         rows_ref[pl.ds(pl.multiple_of(owner * third, 16), third), :] = packed.astype(BF16)
         return carry
 
-    lax.fori_loop(0, owners, pack, 0)
+    lax.fori_loop(0, owners, pack, 0, unroll=4)
 
 
 def table_kernel(
@@ -224,7 +256,7 @@
         total_ref[...] += contract(jnp.concatenate(spread, axis=0).astype(BF16), pick, 1, 1)
         return carry
 
-    lax.fori_loop(0, ids_ref.shape[0], step, 0)
+    lax.fori_loop(0, ids_ref.shape[0], step, 0, unroll=4)
     for part in range(parts):
         here = slice(part * 256, part * 256 + 256)
         grad = total_ref[part * tall : part * tall + embed, :]
@@ -240,12 +272,35 @@
 
 
 def towers_kernel(
-    count_ref, bias_ref, x_ref, first_ref, second_ref, deep_ref, vec_ref, target_ref, valid_ref,
+    spot_ref, count_ref, bias_ref, x_ref, vec_ref, target_ref, valid_ref,
+    own_ref, half_ref, half_core_ref, deep_ref, deep_core_ref,
     one_ref, d_second_ref, d_first_ref, d_deep_ref, dx_ref, head_ref,
-    pre_first_ref, layer_ref, pre_second_ref, two_ref, slope_ref, hidden_ref,
+    cross_ref, all_deep_ref, pre_first_ref, layer_ref, pre_second_ref, two_ref, slope_ref, hidden_ref, arrival,
 ):
     half, wide = x_ref.shape
-    hidden = deep_ref.shape[0]
+    pairs, _, deep_rows = deep_ref.shape[:3]
+    hidden = 4 * pairs * deep_rows
+    tower, core = spot_ref[0], spot_ref[3]
+    middle = half_ref.shape[0]
+    copies = []
+    for k, (source, target) in enumerate(
+        (
+            (own_ref, cross_ref.at[tower, pl.ds(0, 2 * middle), :]),
+            (half_ref, cross_ref.at[1 - tower, pl.ds(pl.multiple_of(core * middle, 16), middle), :]),
+            (half_core_ref, cross_ref.at[1 - tower, pl.ds(pl.multiple_of((1 - core) * middle, 16), middle), :]),
+            (deep_ref.at[:, 0], all_deep_ref.at[0, :, core]),
+            (deep_ref.at[:, 1], all_deep_ref.at[1, :, core]),
+            (deep_core_ref.at[:, 0], all_deep_ref.at[0, :, 1 - core]),
+            (deep_core_ref.at[:, 1], all_deep_ref.at[1, :, 1 - core]),
+        )
+    ):
+        copies.append(pltpu.make_async_copy(source, target, arrival.at[k]))
+        copies[-1].start()
+
+    def deep_block(at, size):
+        per = 2 * deep_rows
+        block = all_deep_ref[at // (hidden // 2), pl.ds(at % (hidden // 2) // per, size // per)]
+        return block.reshape(size, wide)
 
     def lanes(x):
         total = x[:, :LANES]
@@ -253,10 +308,14 @@
             total = total + x[:, at : at + LANES]
         return total
 
+    if 2 * middle < wide:
+        cross_ref[:, 2 * middle :, :] = jnp.zeros((2, wide - 2 * middle, wide), BF16)
+    for copy in copies[:3]:
+        copy.wait()
     for at, size in tiles(wide):
         here = slice(at, at + size)
         base = x_ref[:, here].astype(F32)
-        pre = contract(x_ref[...], first_ref[:, here], 1, 0) + vec_ref[0:1, here]
+        pre = contract(x_ref[...], cross_ref[0, :, here], 1, 0) + vec_ref[0:1, here]
         layer = base * pre + base
         pre_first_ref[:, here] = pre
         layer_ref[:, here] = layer
@@ -265,14 +324,16 @@
     for at, size in tiles(wide):
         here = slice(at, at + size)
         base = x_ref[:, here].astype(F32)
-        pre = contract(one_ref[...], second_ref[:, here], 1, 0) + vec_ref[1:2, here]
+        pre = contract(one_ref[...], cross_ref[1, :, here], 1, 0) + vec_ref[1:2, here]
         two = (base * pre + layer_ref[:, here]).astype(BF16)
         pre_second_ref[:, here] = pre
         two_ref[:, here] = two
         score = score + lanes(two.astype(F32) * vec_ref[3:4, here])
+    for copy in copies[3:]:
+        copy.wait()
     for at, size in tiles(hidden):
         here = slice(at, at + size)
-        pre = contract(x_ref[...], deep_ref[here, :], 1, 1) + vec_ref[2:3, here]
+        pre = contract(x_ref[...], deep_block(at, size), 1, 1) + vec_ref[2:3, here]
         gate = jax.nn.sigmoid(pre)
         out = (pre * gate).astype(BF16)
         hidden_ref[:, here] = out
@@ -300,32 +361,41 @@
         here = slice(at, at + size)
         base = x_ref[:, here].astype(F32)
         d_two = d_logit * vec_ref[3:4, here]
-        d_one = contract(d_second_ref[...], second_ref[here, :], 1, 1) + d_two
+        d_one = contract(d_second_ref[...], cross_ref[1, here, :], 1, 1) + d_two
         d_first_ref[:, here] = (d_one * base).astype(BF16)
         layer_ref[:, here] = d_one * (1.0 + pre_first_ref[:, here]) + d_two * pre_second_ref[:, here]
     for at, size in tiles(wide):
         here = slice(at, at + size)
-        dx = contract(d_first_ref[...], first_ref[here, :], 1, 1) + contract(d_deep_ref[...], deep_ref[:, here], 1, 0)
+        columns = all_deep_ref[:, :, :, :, here].reshape(hidden, size)
+        dx = contract(d_first_ref[...], cross_ref[0, here, :], 1, 1) + contract(d_deep_ref[...], columns, 1, 0)
         dx_ref[:, here] = (dx + layer_ref[:, here]).astype(BF16)
 
 
 def grads_kernel(
-    deep_rows, core_ref, x_ref, one_ref, d_second_ref, d_first_ref, d_deep_ref, head_ref,
+    deep_rows, spot_ref, x_ref, one_ref, d_second_ref, d_first_ref, d_deep_ref, head_ref,
     keep_ref, give_ref, rest_ref, turned_ref,
 ):
     half, wide = x_ref.shape
     hidden = d_deep_ref.shape[1]
-    towers, groups, pairs, rows, main = keep_ref.shape
+    mid, rows, main = keep_ref.shape[3:]
+    towers, groups, pairs = 2, 2 * mid, 2
     rows_c = rows - deep_rows
-    even = core_ref[0, 0] == 0
+    even = spot_ref[3] == 0
 
     def share(value, tower, at, size, chunk, first):
+        by_tower = tower ^ spot_ref[0]
         for group in range(groups):
+            by_far = group ^ spot_ref[1]
+            upper = by_far // mid
             for pair in range(pairs):
+                by_near = pair ^ spot_ref[2]
+                one = by_tower + upper * (by_near - by_tower)
+                two = by_near + upper * (by_tower - by_near)
                 start = (group * pairs + pair) * 2 * chunk
                 low, high = value[start : start + chunk], value[start + chunk : start + 2 * chunk]
-                keep_ref[tower, group, pair, first : first + chunk, at : at + size] = jnp.where(even, low, high).astype(BF16)
-                give_ref[tower, group, pair, first : first + chunk, at : at + size] = jnp.where(even, high, low).astype(BF16)
+                place = (upper, one, two, by_far % mid, slice(first, first + chunk), slice(at, at + size))
+                keep_ref[place] = jnp.where(even, low, high).astype(BF16)
+                give_ref[place] = jnp.where(even, high, low).astype(BF16)
 
     rest_ref[...] = jnp.zeros_like(rest_ref)
     for tower, (left, right) in enumerate(((one_ref, d_second_ref), (x_ref, d_first_ref))):
@@ -334,13 +404,19 @@
         for at, size in tiles(main):
             value = contract(turned_ref[...], right[:, at : at + size], 1, 0)
             share(value, tower, at, size, rows_c, 0)
-            rest_ref[8 * tower : 8 * tower + 4, at : at + size] = value[main : main + 4]
+            rest_ref[16 * tower : 16 * tower + 3, at : at + size] = value[main : main + 3]
+            rest_ref[6 + tower : 7 + tower, at : at + size] = value[main + 3 : main + 4]
         value = contract(turned_ref[...], right[:, main:wide], 1, 0)
-        rest_ref[8 * tower : 8 * tower + 4, main:wide] = value[main : main + 4]
-        rest_ref[8 * tower + 4 : 8 * tower + 7, :main] = value[:main].T[:3]
+        rest_ref[16 * tower : 16 * tower + 3, main:wide] = value[main : main + 3]
+        rest_ref[6 + tower : 7 + tower, main:wide] = value[main + 3 : main + 4]
+        rest_ref[16 * tower + 3 : 16 * tower + 6, :main] = value[:main].T[:3]
     bias = contract(turned_ref[main:wide, :], d_deep_ref[...], 1, 0)
-    rest_ref[16:20, :hidden] = bias[:4]
-    rest_ref[20:23, :] = head_ref[0:3, :]
+    rest_ref[8:12, :hidden] = bias[:4]
+    rest_ref[12:15, :] = head_ref[0:3, :]
+    mine, other = rest_ref[0:8, :], rest_ref[16:24, :]
+    swap = (iota((8, wide), 0) < 6) & (iota((8, wide), 1) >= wide * (1 - spot_ref[0]))
+    rest_ref[0:8, :] = jnp.where(swap, other, mine)
+    rest_ref[16:24, :] = jnp.where(swap, mine, other)
     turned_ref[:hidden, :] = d_deep_ref[...].T
     for at, size in tiles(main):
         value = contract(turned_ref[:hidden, :], x_ref[:, at : at + size], 1, 0)
@@ -355,28 +431,36 @@
     block = pl.program_id(0)
     width = weight_ref.shape[2]
     main = near_ref.shape[3]
-    rows = 2 * near_ref.shape[2]
+    half = near_ref.shape[2]
+    rows = 2 * half
     even = (place_ref[0] & 1) == 0
-    near, far = near_ref[0, 0].astype(F32), far_ref[0, 0].astype(F32)
-    body = jnp.concatenate([jnp.where(even, near, far), jnp.where(even, far, near)], axis=0)
-    lane = pl.multiple_of(jnp.minimum(block * rows, main - rows) // LANES * LANES, LANES)
-    side = rest_ref[0, :, pl.ds(lane, LANES)]
-    side = jnp.concatenate([side, jnp.zeros((LANES - 8, LANES), F32)], axis=0).T
-    if rows < LANES:
+
+    def update(at, columns, grad):
+        here = (slice(at, at + grad.shape[0]), 0, columns)
+        one, two, new = adamw(weight_ref[here], grad, first_ref[here], second_ref[here], 0.03)
+        grad_ref[here] = grad
+        first_new_ref[here] = one
+        second_new_ref[here] = two
+        new_ref[here] = new
+        copy_ref[slice(at, at + grad.shape[0]), columns] = new.astype(BF16)
+
+    @pl.when(block < pl.num_programs(0) - 1)
+    def _():
+        near, far = near_ref[0, 0].astype(F32), far_ref[0, 0].astype(F32)
+        update(0, slice(0, main), jnp.where(even, near, far))
+        update(half, slice(0, main), jnp.where(even, far, near))
+        lane = pl.multiple_of(block * rows // LANES * LANES, LANES)
+        side = rest_ref[0, :, pl.ds(lane, LANES)]
+        side = jnp.concatenate([side, jnp.zeros((LANES - 8, LANES), F32)], axis=0).T
         parts = [side[at : at + rows] for at in range(0, LANES, rows)]
         side = parts[0]
         for k, part in enumerate(parts):
             side = jnp.where(block % len(parts) == k, part, side)
-    side = pltpu.roll(side, LANES - 4, 1)
-    grad = jnp.concatenate([body, side], axis=1)
-    last = jnp.concatenate([rest_ref[0], jnp.zeros((rows - 8, rest_ref.shape[2]), F32)], axis=0)
-    grad = jnp.where(block == pl.num_programs(0) - 1, last, grad)[:, :width]
-    one, two, new = adamw(weight_ref[:, 0, :], grad, first_ref[:, 0, :], second_ref[:, 0, :], 0.03)
-    grad_ref[:, 0, :] = grad
-    first_new_ref[:, 0, :] = one
-    second_new_ref[:, 0, :] = two
-    new_ref[:, 0, :] = new
-    copy_ref[...] = new.astype(BF16)
+        update(0, slice(main, width), side[:, 3 : 3 + width - main])
+
+    @pl.when(block == pl.num_programs(0) - 1)
+    def _():
+        update(0, slice(0, width), rest_ref[0, :, :width])
 
 
 def flip(x, axis, bit, size):
@@ -423,6 +507,7 @@
     tower, place = lax.axis_index("tower"), lax.axis_index("batch")
     core, near, far = place & 1, (place >> 1) & 1, place >> 2
     groups = batch // 4
+    spot = jnp.stack([tower, far, near, core])
     rows_own, embed = embed_table.shape
     examples, feats = category_ids.shape
     half = examples // towers
@@ -458,8 +543,14 @@
     )(ids, valid.reshape(1, half))
     slot = slot.reshape(-1)
     arrived = lax.all_to_all(asked, ("tower", "batch"), split_axis=0, concat_axis=0, tiled=True)
+    middle = round_up(-(-width // 2), 16)
+    own_low = jnp.pad(cross_weight[0].astype(BF16), ((0, 2 * middle - width), (0, wide - width)))
+    deep_own = jnp.pad(deep_weight.astype(BF16), ((0, 0), (0, wide - width)))
+    own_low, deep_own, arrived = lax.optimization_barrier((own_low, deep_own, arrived))
     count = jnp.sum(arrived[:, slots]).astype(F32)
     table_t = embed_table.T
+    deep_parts = flip_far(deep_own, batch, groups)
+    got_low = flip(lax.dynamic_slice_in_dim(own_low, core * middle, middle, 0), "tower", 1, towers)
     found = pl.pallas_call(
         functools.partial(lookup_kernel, slots, stride),
         out_shape=jax.ShapeDtypeStruct((owners * third, LANES), BF16),
@@ -469,34 +560,11 @@
         compiler_params=params(32),
         name="lookup",
     )(arrived, table_t)
+    deep_parts, found = lax.optimization_barrier((deep_parts, found))
     returned = lax.all_to_all(found, ("tower", "batch"), split_axis=0, concat_axis=0, tiled=True)
-    inputs = pl.pallas_call(
-        functools.partial(inputs_kernel, feats, stride, embed, dense_width),
-        out_shape=jax.ShapeDtypeStruct((half, wide), BF16),
-        in_specs=[in_smem(), in_vmem(), in_vmem()],
-        out_specs=in_vmem(),
-        scratch_shapes=[
-            pltpu.VMEM((owners * stride, LANES), F32),
-            pltpu.VMEM((half, LANES), F32),
-            pltpu.VMEM((half, wide), F32),
-        ],
-        compiler_params=params(48),
-        name="inputs",
-    )(slot, returned, dense)
-
-    own_low = jnp.pad(cross_weight[0].astype(BF16), ((0, wide - width), (0, wide - width)))
-    halves = own_low.reshape(2, wide // 2, wide)
-    got = flip(pick(halves, 0, core), "tower", 1, towers)
-    other_low = join(got, flip(got, "batch", 1, batch), 0, core).reshape(wide, wide)
-    cross_low = (
-        jnp.where(tower == 0, own_low, other_low),
-        jnp.where(tower == 0, other_low, own_low),
-    )
-    deep_own = jnp.pad(deep_weight.astype(BF16), ((0, 0), (0, wide - width)))
-    deep_low = in_order(flip_far(deep_own, batch, groups), groups)
-    deep_low = join(deep_low, flip(deep_low, "batch", 2, batch), 1, near)
-    deep_low = join(deep_low, flip(deep_low, "tower", 1, towers), 0, tower)
-    deep_low = join(deep_low, flip(deep_low, "batch", 1, batch), 3, core).reshape(hidden, wide)
+    deep_low = in_order(deep_parts, groups)
+    deep_low = join(deep_low, flip(deep_low, "tower", 1, towers), 1, tower)
+    deep_low = join(deep_low, flip(deep_low, "batch", 2, batch), 1, near).reshape(batch // 2, towers, deep_rows, wide)
 
     def widen(x):
         return jnp.pad(x, (0, wide - x.shape[0]))
@@ -511,30 +579,71 @@
         ]
         + [jnp.zeros((wide,), F32)] * 3
     )
+    target = target.reshape(half, 1)
+    valid = valid.astype(F32).reshape(half, 1)
+    returned, own_low, got_low, deep_low, vec, target, valid = lax.optimization_barrier(
+        (returned, own_low, got_low, deep_low, vec, target, valid)
+    )
+    got_core = flip(got_low, "batch", 1, batch)
+    deep_core = flip(deep_low, "batch", 1, batch)
+    inputs = pl.pallas_call(
+        functools.partial(inputs_kernel, feats, stride, embed, dense_width),
+        out_shape=jax.ShapeDtypeStruct((half, wide), BF16),
+        in_specs=[in_smem(), in_vmem(), in_vmem()],
+        out_specs=in_vmem(),
+        scratch_shapes=[
+            pltpu.VMEM((owners * stride, LANES), F32),
+            pltpu.VMEM((half, LANES), F32),
+            pltpu.VMEM((half, LANES), F32),
+            pltpu.VMEM((half, wide), F32),
+        ],
+        compiler_params=params(48),
+        name="inputs",
+    )(slot, returned, dense)
+
     low = jax.ShapeDtypeStruct((half, wide), BF16)
     low_deep = jax.ShapeDtypeStruct((half, hidden), BF16)
     one_low, d_second, d_first, d_deep, d_inputs, heads = pl.pallas_call(
         towers_kernel,
         out_shape=(low, low, low, low_deep, low, jax.ShapeDtypeStruct((8, wide), F32)),
-        in_specs=[in_smem()] * 2 + [in_vmem()] * 7,
+        in_specs=[in_smem()] * 3 + [in_vmem()] * 4 + [pl.BlockSpec(memory_space=pl.ANY)] * 5,
         out_specs=(in_vmem(),) * 6,
         scratch_shapes=[
+            pltpu.VMEM((2, wide, wide), BF16),
+            pltpu.VMEM((2, batch // 2, 2, deep_rows, wide), BF16),
             pltpu.VMEM((half, wide), F32),
             pltpu.VMEM((half, wide), F32),
             pltpu.VMEM((half, wide), F32),
             pltpu.VMEM((half, wide), BF16),
             pltpu.VMEM((half, hidden), F32),
             pltpu.VMEM((half, hidden), BF16),
+            pltpu.SemaphoreType.DMA((7,)),
         ],
         compiler_params=params(56),
         name="towers",
     )(
-        count.reshape(1, 1), vectors[-1:].reshape(1, 1), inputs, cross_low[0], cross_low[1], deep_low, vec,
-        target.reshape(half, 1), valid.astype(F32).reshape(half, 1),
+        spot, count.reshape(1, 1), vectors[-1:].reshape(1, 1), inputs, vec, target, valid,
+        own_low, got_low, got_core, deep_low, deep_core,
+    )
+    sent = pl.pallas_call(
+        functools.partial(send_kernel, feats, slots, stride, embed, dense_width),
+        out_shape=jax.ShapeDtypeStruct((owners * third, LANES), BF16),
+        in_specs=[in_smem(), in_vmem()],
+        out_specs=in_vmem(),
+        scratch_shapes=[
+            pltpu.VMEM((owners * stride, LANES), F32),
+            pltpu.VMEM((half, LANES), F32),
+            pltpu.VMEM((half, LANES), F32),
+        ],
+        compiler_params=params(48),
+        name="send",
+    )(slot, d_inputs)
+    sent, inputs, one_low, d_second, d_first, d_deep, heads = lax.optimization_barrier(
+        (sent, inputs, one_low, d_second, d_first, d_deep, heads)
     )
     main = width // LANES * LANES
     rows_c = main // batch
-    parts = jax.ShapeDtypeStruct((towers, groups, 2, rows_c + deep_rows, main), BF16)
+    parts = jax.ShapeDtypeStruct((2, 2, 2, groups // 2, rows_c + deep_rows, main), BF16)
     keep, give, rest = pl.pallas_call(
         functools.partial(grads_kernel, deep_rows),
         out_shape=(parts, parts, jax.ShapeDtypeStruct((24, wide), F32)),
@@ -543,21 +652,23 @@
         scratch_shapes=[pltpu.VMEM((wide, half), BF16)],
         compiler_params=params(56),
         name="grads",
-    )(core.reshape(1, 1), inputs, one_low, d_second, d_first, d_deep, heads)
+    )(spot, inputs, one_low, d_second, d_first, d_deep, heads)
     got = flip(give, "batch", 1, batch)
-
-    sent = pl.pallas_call(
-        functools.partial(send_kernel, feats, slots, stride, embed, dense_width),
-        out_shape=jax.ShapeDtypeStruct((owners * third, LANES), BF16),
-        in_specs=[in_smem(), in_vmem()],
-        out_specs=in_vmem(),
-        scratch_shapes=[
-            pltpu.VMEM((owners * stride, LANES), F32),
-            pltpu.VMEM((half, LANES), F32),
-        ],
-        compiler_params=params(48),
-        name="send",
-    )(slot, d_inputs)
+    rest = rest + flip(rest, "batch", 1, batch)
+
+    def by_tower(x):
+        return flip(x, "tower", 1, towers)
+
+    def by_near(x):
+        return flip(x, "batch", 2, batch)
+
+    to_one, rest = lax.optimization_barrier(([keep[k, 1] + got[k, 1] for k in range(2)], rest))
+    from_one = [by_tower(to_one[0]), by_near(to_one[1])]
+    rest = rest[:16] + by_tower(jnp.concatenate([rest[16:22], rest[6:16]]))
+    from_one, rest = lax.optimization_barrier((from_one, rest))
+    rest = rest + by_near(rest)
+    for bit in [4 << k for k in range(groups.bit_length() - 1)]:
+        rest = rest + flip(rest, "batch", bit, batch)
     back = lax.all_to_all(sent, ("tower", "batch"), split_axis=0, concat_axis=0, tiled=True)
     shape_t = jax.ShapeDtypeStruct((embed, rows_own), F32)
     table_grad, table_one, table_two, table_new = pl.pallas_call(
@@ -570,29 +681,41 @@
         name="table",
     )(arrived, back, table_t, table_first.T, table_second.T)
 
-    for bit in [1, 2] + [4 << k for k in range(groups.bit_length() - 1)]:
-        rest = rest + flip(rest, "batch", bit, batch)
-    rest = rest + flip(rest, "tower", 1, towers)
-
-    mid = groups // 2
-    other, beyond = 1 - tower, 1 - near
-    keep_one, got_one, keep_two, got_two = keep[:, :mid], got[:, :mid], keep[:, mid:], got[:, mid:]
-    from_tower = flip(pick(keep_one, 0, other) + pick(got_one, 0, other), "tower", 1, towers)
-    from_near = flip(pick(keep_two, 2, beyond) + pick(got_two, 2, beyond), "batch", 2, batch)
-    one = pick(keep_one, 0, tower) + pick(got_one, 0, tower) + from_tower
-    two = pick(keep_two, 2, near) + pick(got_two, 2, near) + from_near
-    one = pick(one, 1, near) + flip(pick(one, 1, beyond), "batch", 2, batch)
-    two = pick(two, 0, tower) + flip(pick(two, 0, other), "tower", 1, towers)
-    both = jnp.concatenate([one, two], axis=0)
-    summed = pick(both, 0, far).astype(F32)
-    for k in range(1, groups):
-        summed = summed + flip(pick(both, 0, far ^ k), "batch", k * 4, batch).astype(F32)
-    tail = lax.dynamic_slice_in_dim(rest[16 : 16 + width - main], (tower * batch + place) * deep_rows, deep_rows, 1)
-    deep_grad = jnp.concatenate([summed[rows_c:], tail.T], axis=1)
+    from_one, rest, table_grad, table_one, table_two, table_new = lax.optimization_barrier(
+        (from_one, rest, table_grad, table_one, table_two, table_new)
+    )
+    to_two = lax.optimization_barrier([keep[k, 0, 1] + got[k, 0, 1] + from_one[k][1] for k in range(2)])
+    from_two = [by_near(to_two[0]), by_tower(to_two[1])]
+    from_two = lax.optimization_barrier(from_two)
+    both = [keep[k, 0, 0] + got[k, 0, 0] + from_one[k][0] + from_two[k] for k in range(2)]
+    both = lax.optimization_barrier([part[k] for part in both for k in range(groups // 2)])
+    from_far = [flip(both[k], "batch", k * 4, batch) for k in range(1, groups)]
+    from_far = lax.optimization_barrier(from_far)
+    summed = both[0].astype(F32)
+    for part in from_far:
+        summed = summed + part.astype(F32)
     chunk = flip_far(summed[:rows_c].astype(BF16), batch, groups)
-    chunk = jnp.stack([chunk, flip(chunk, "batch", 2, batch)])
+    across = flip(chunk, "batch", 2, batch)
+    vector_grad = jnp.concatenate(
+        [rest[6, :width], rest[7, :width], rest[11, :hidden], rest[12, :width], rest[13, :hidden], rest[14, :1]]
+    )
+    vector_one, vector_two, vector_new = adamw(vectors, vector_grad, vector_first, vector_second, 0.03)
+    tail = lax.dynamic_slice_in_dim(rest[8 : 8 + width - main], (tower * batch + place) * deep_rows, deep_rows, 1).T
+    deep_grad = jnp.concatenate([summed[rows_c:], tail], axis=1)
+    deep_one, deep_two, deep_new = adamw(deep_weight, deep_grad, deep_first, deep_second, 0.03)
+    deep_copy = deep_new.astype(BF16)
+    side = rest[:8][None]
+    (
+        across, side, vector_grad, vector_one, vector_two, vector_new,
+        deep_grad, deep_one, deep_two, deep_new, deep_copy,
+    ) = lax.optimization_barrier(
+        (
+            across, side, vector_grad, vector_one, vector_two, vector_new,
+            deep_grad, deep_one, deep_two, deep_new, deep_copy,
+        )
+    )
+    chunk = jnp.stack([chunk, across])
     partner = flip(chunk, "batch", 1, batch)
-    side = pick(rest[:16].reshape(2, 8, wide), 0, tower)[None]
     blocks = batch // 2
     rows = 2 * rows_c
 
@@ -619,12 +742,7 @@
         cross_weight.transpose(1, 0, 2), cross_first.transpose(1, 0, 2), cross_second.transpose(1, 0, 2),
     )
     cross_grad, cross_one, cross_two, cross_new = (x.transpose(1, 0, 2) for x in cross_out[:4])
-    vector_grad = jnp.concatenate(
-        [rest[3, :width], rest[11, :width], rest[19, :hidden], rest[20, :width], rest[21, :hidden], rest[22, :1]]
-    )
-    loss_sum = rest[22, 1]
-    deep_one, deep_two, deep_new = adamw(deep_weight, deep_grad, deep_first, deep_second, 0.03)
-    vector_one, vector_two, vector_new = adamw(vectors, vector_grad, vector_first, vector_second, 0.03)
+    loss_sum = rest[14, 1]
     return (
         loss_sum,
         count,
@@ -637,7 +755,7 @@
         deep_one,
         deep_two,
         deep_new,
-        deep_new.astype(BF16),
+        deep_copy,
         table_grad.T,
         table_one.T,
         table_two.T,

time: 360 us -> 299 us (0.83); the launches traced: 354 us -> 298 us
  waiting for transfers between devices: 75.2 us -> 113 us
  blocking collectives: 28.3 us -> 0 us
  Pallas kernels: 132 us -> 108 us
  other arithmetic: 32 us -> 10.7 us
  local copies, waits for them, and re-layouts: 35.1 us -> 16 us
    ppermute x26, waiting for transfers between devices: 56.2 us -> 110 us  [flip(): return lax.ppermute(x, axis, [(i, i ^ bit) for i in range(size)])]
    all_to_all x1 -> x0, blocking collectives: 28.3 us -> none  [local(): lax.all_to_all(asked, ('tower', 'batch'), split_axis=0, concat_axis=0, ti...]
    all_to_all x1, waiting for transfers between devices: 19 us -> 0.01 us  [local(): lax.all_to_all(found, ('tower', 'batch'), split_axis=0, concat_axis=0, ti...]
    slice x10 -> x8, local copies, waits for them, and re-layouts: 8.62 us -> 0.66 us  [the longest x1 0.58 us: local(): rest[14, :1]]
    select_n x6 -> x3, other arithmetic: 7.89 us -> 0.45 us  [join(): jnp.where(index == 0, jnp.stack([mine, other], axis), jnp.stack([other, m...]
    ppermute x26, starting transfers between devices: 39.4 us -> 32 us  [flip(): return lax.ppermute(x, axis, [(i, i ^ bit) for i in range(size)])]
    all_to_all x0 -> x1, starting transfers between devices: none -> 7.3 us  [local(): lax.all_to_all(asked, ('tower', 'batch'), split_axis=0, concat_axis=0, ti...]
    pallas_call x1, Pallas kernels: 23.9 us -> 16.8 us  [local(): pl.pallas_call(functools.partial(send_kernel, feats, slots, stride, embed...]
  transfers between devices with their start and end apart: 28 -> 29, of which waited for: 13 -> 16; matrix products, arithmetic and copies ran while one was open for 15% -> 6% of each run, Pallas kernels for 16% -> 12%
where the time goes in v2:
time: 299 us; the launch traced here: 298 us
  waiting for transfers between devices  113 us (38%)
  Pallas kernels  108 us (36%)
  starting transfers between devices  47.7 us (16%)
  local copies, waits for them, and re-layouts  16 us (5%)
  other arithmetic  10.7 us (4%)
  between operations  3.05 us (1%)
    ppermute x26, waiting for transfers between devices, flip(): return lax.ppermute(x, axis, [(i, i ^ bit) for i in range(size)])  110 us
    ppermute x26, starting transfers between devices, flip(): return lax.ppermute(x, axis, [(i, i ^ bit) for i in range(size)])  32 us
    pallas_call x1, Pallas kernels, local(): pl.pallas_call(cross_kernel, grid_spec=pltpu.PrefetchScalarGridSpec(num_s...  22 us
    pallas_call x1, Pallas kernels, local(): pl.pallas_call(towers_kernel, out_shape=(low, low, low, low_deep, low, ja...  17.3 us
    pallas_call x1, Pallas kernels, local(): pl.pallas_call(functools.partial(inputs_kernel, feats, stride, embed, den...  17.1 us
    pallas_call x1, Pallas kernels, local(): pl.pallas_call(functools.partial(send_kernel, feats, slots, stride, embed...  16.8 us
    pallas_call x1, Pallas kernels, local(): pl.pallas_call(functools.partial(grads_kernel, deep_rows), out_shape=(par...  10.2 us
    pallas_call x1, Pallas kernels, local(): pl.pallas_call(functools.partial(lookup_kernel, slots, stride), out_shape...  9.48 us
  transfers between devices with their start and end apart: 29, of which 16 were waited for; matrix products, arithmetic and copies ran while one was open for 6% of the time, Pallas kernels for 12%

profile of v2, /device:TPU:0, one launch (start us, length us, event | category | flops | bytes accessed | tf_op | source)
XLA Modules:
  0.0 298.1 jit_solution(1872029068964717874)
XLA Ops:
  1.6 7.2 %slots.1 = (s32[32,512]{1,0:T(8,128)S(1)}, s32[104,128]{1,0:T(8,128)S(1)}) custom-call(s32[26,512]{1,0:T(8,128)S(1)} %dynamic-slice_bitcast_fusion.ids_ref, s32[1,512]{1,0:T(1,128)S(1)} %bitcast.119), custom_call_target="tpu_custom_call" | custom-call | tf_op jit(solution)/shard_map/slots/pallas_call | solution.py:533
  9.5 7.3 %all-to-all-start = ((s32[32,1,512]{2,1,0:T(1,128)}), s32[32,1,512]{2,1,0:T(1,128)S(1)}, u32[]{:S(2)}, u32[]{:S(2)}) async-start(s32[32,1,512]{2,1,0:T(1,128)} %copy.47), calls=%async_computation | async-start | bytes 131072 | tf_op jit(solution)/shard_map/all_to_all | solution.py:545
  28.6 9.5 %lookup.1 = bf16[4608,128]{1,0:T(8,128)(2,1)} custom-call(s32[32,512]{1,0:T(8,128)S(1)} %bitcast.111, f32[39,2048]{1,0:T(8,128)S(1)} %bitcast.109), custom_call_target="tpu_custom_call" | custom-call | tf_op jit(solution)/shard_map/lookup/pallas_call | solution.py:554
  38.2 3.7 %all-to-all-start.1 = ((bf16[32,144,128]{2,1,0:T(8,128)(2,1)}), bf16[32,144,128]{2,1,0:T(8,128)(2,1)S(1)}, u32[]{:S(2)}, u32[]{:S(2)}) async-start(bf16[32,144,128]{2,1,0:T(8,128)(2,1)} %bitcast.16), calls=%async_computation.1 | async-start | bytes 2359296 | tf_op jit(solution)/shard_map/all_to_all | solution.py:564
  46.6 14.5 %collective-permute-done.4 = bf16[4,32,1152]{2,1,0:T(8,128)(2,1)S(1)} collective-permute-done((bf16[4,32,1152]{2,1,0:T(8,128)(2,1)S(1)}, bf16[4,32,1152]{2,1,0:T(8,128)(2,1)S(1)}, u32[]{:S(2)}, u32[]{:S(2)}) %collective-permute-start.4) | collective-permute-done | bytes 294944 | tf_op jit(solution)/shard_map/ppermute | solution.py:467
  64.2 13.6 %collective-permute-done.5 = bf16[4,2,32,1152]{3,2,0,1:T(8,128)(2,1)S(1)} collective-permute-done((bf16[4,2,32,1152]{3,2,0,1:T(8,128)(2,1)S(1)}, bf16[4,2,32,1152]{3,2,0,1:T(8,128)(2,1)S(1)}, u32[]{:S(2)}, u32[]{:S(2)}) %collective-permute-start.5) | collective-permute-done | bytes 589856 | tf_op jit(solution)/shard_map/ppermute | solution.py:467
  78.2 11.7 %collective-permute-done.3.half_ref = bf16[528,1152]{1,0:T(8,128)(2,1)} collective-permute-done((bf16[528,1152]{1,0:T(8,128)(2,1)}, bf16[528,1152]{1,0:T(8,128)(2,1)}, u32[]{:S(2)}, u32[]{:S(2)}) %collective-permute-start.3) | collective-permute-done | bytes 1216544 | tf_op jit(solution)/shard_map/ppermute | solution.py:467
  94.9 17.1 %inputs.1.x_ref = bf16[512,1152]{1,0:T(8,128)(2,1)S(1)} custom-call(s32[13312]{0:T(1024)S(1)} %bitcast.116, bf16[4608,128]{1,0:T(8,128)(2,1)S(1)} %bitcast.107, bf16[512,128]{1,0:T(8,128)(2,1)S(1)} %pad.38.dense_ref), custom_call_target="tpu_custom_call" | custom-call | tf_op jit(solution)/shard_map/inputs/pallas_call | solution.py:589
  113.0 17.3 %towers.1 = (bf16[512,1152]{1,0:T(8,128)(2,1)}, bf16[512,1152]{1,0:T(8,128)(2,1)}, bf16[512,1152]{1,0:T(8,128)(2,1)}, bf16[512,1024]{1,0:T(8,128)(2,1)}, bf16[512,1152]{1,0:T(8,128)(2,1)}, /*index=5*/f32[8,1152]{1,0:T(8,128)}) custom-call(s32[4]{0:T(128)} %pad_add_fusion.spot_ref, f32[1,1]{1,0:T(1,128)} %bitcast.9.count_ref, f32[1,1]{1,0:T(1,128)} %bitcast.10.bias_ref, ...), custom_call_target="tpu_custom_call" | custom-call | tf_op jit(solution)/shard_map/towers/pallas_call | solution.py:606
  131.6 16.8 %send.1 = bf16[4608,128]{1,0:T(8,128)(2,1)} custom-call(s32[13312]{0:T(1024)S(1)} %bitcast.117, bf16[512,1152]{1,0:T(8,128)(2,1)S(1)} %copy-done.4), custom_call_target="tpu_custom_call" | custom-call | tf_op jit(solution)/shard_map/send/pallas_call | solution.py:628
  148.4 10.2 %grads.1 = (bf16[2,2,2,2,96,1024]{5,4,3,2,1,0:T(8,128)(2,1)}, bf16[2,2,2,2,96,1024]{5,4,3,2,1,0:T(8,128)(2,1)}, f32[24,1152]{1,0:T(8,128)}) custom-call(s32[4]{0:T(128)} %pad_add_fusion.spot_ref, bf16[512,1152]{1,0:T(8,128)(2,1)} %copy-done.2, bf16[512,1152]{1,0:T(8,128)(2,1)} %get-tuple-element.115.one_ref, ...), custom_call_target="tpu_custom_call" | custom-call | tf_op jit(solution)/shard_map/grads/pallas_call | solution.py:647
  158.6 4.7 %all-to-all-start.2 = ((bf16[32,144,128]{2,1,0:T(8,128)(2,1)}), bf16[32,144,128]{2,1,0:T(8,128)(2,1)S(1)}, u32[]{:S(2)}, u32[]{:S(2)}) async-start(bf16[32,144,128]{2,1,0:T(8,128)(2,1)} %bitcast.28), calls=%async_computation.2 | async-start | bytes 2359296 | tf_op jit(solution)/shard_map/all_to_all | solution.py:672
  170.8 26.5 %collective-permute-done.12 = f32[16,1152]{1,0:T(8,128)S(1)} collective-permute-done((f32[16,1152]{1,0:T(8,128)S(1)}, f32[16,1152]{1,0:T(8,128)S(1)}, u32[]{:S(2)}, u32[]{:S(2)}) %collective-permute-start.12) | collective-permute-done | bytes 73760 | tf_op jit(solution)/shard_map/ppermute | solution.py:467
  199.7 2.9 collective-permute-done.13
  204.1 2.9 collective-permute-done.14
  209.5 7.8 %table.1 = (f32[39,2048]{1,0:T(8,128)}, f32[39,2048]{1,0:T(8,128)}, f32[39,2048]{1,0:T(8,128)}, f32[39,2048]{1,0:T(8,128)}) custom-call(s32[32,512]{1,0:T(8,128)S(1)} %bitcast.113, bf16[4608,128]{1,0:T(8,128)(2,1)S(1)} %bitcast.108, f32[39,2048]{1,0:T(8,128)S(1)} %bitcast.110, f32[39,2048]{1,0:T(8,128)S(1)} %bitcast.114, f32[39,2048]{1,0:T(8,128)S(1)} %bitcast.115), custom_call_target="tpu_custom_call" | custom-call | tf_op jit(solution)/shard_map/table/pallas_call | solution.py:674
  222.5 5.2 %collective-permute-done.16 = bf16[2,96,1024]{2,1,0:T(8,128)(2,1)S(1)} collective-permute-done((bf16[2,96,1024]{2,1,0:T(8,128)(2,1)S(1)}, bf16[2,96,1024]{2,1,0:T(8,128)(2,1)S(1)}, u32[]{:S(2)}, u32[]{:S(2)}) %collective-permute-start.16) | collective-permute-done | bytes 393248 | tf_op jit(solution)/shard_map/ppermute | solution.py:467
  235.8 4.1 %collective-permute-done.18 = bf16[96,1024]{1,0:T(8,128)(2,1)S(1)} collective-permute-done((bf16[96,1024]{1,0:T(8,128)(2,1)S(1)}, bf16[96,1024]{1,0:T(8,128)(2,1)S(1)}, u32[]{:S(2)}, u32[]{:S(2)}) %collective-permute-start.18) | collective-permute-done | bytes 196640 | tf_op jit(solution)/shard_map/ppermute | solution.py:467
  239.9 5.5 %collective-permute-done.19 = bf16[96,1024]{1,0:T(8,128)(2,1)S(1)} collective-permute-done((bf16[96,1024]{1,0:T(8,128)(2,1)S(1)}, bf16[96,1024]{1,0:T(8,128)(2,1)S(1)}, u32[]{:S(2)}, u32[]{:S(2)}) %collective-permute-start.19) | collective-permute-done | bytes 196640 | tf_op jit(solution)/shard_map/ppermute | solution.py:467
  245.6 3.5 %collective-permute-start.21 = (bf16[64,1024]{1,0:T(8,128)(2,1)S(1)}, bf16[64,1024]{1,0:T(8,128)(2,1)S(1)}, u32[]{:S(2)}, u32[]{:S(2)}) collective-permute-start(bf16[64,1024]{1,0:T(8,128)(2,1)S(1)} %slice.234), channel_id=1, source_target_pairs={{0,4},{1,5},{2,6},{3,7},{4,0},{5,1},{6,2},{7,3},{8,12},{9,13},{10,... | collective-permute-start | bytes 393224 | tf_op jit(solution)/shard_map/ppermute | solution.py:467
  253.0 7.5 %collective-permute-done.22 = bf16[64,1024]{1,0:T(8,128)(2,1)S(1)} collective-permute-done((bf16[64,1024]{1,0:T(8,128)(2,1)S(1)}, bf16[64,1024]{1,0:T(8,128)(2,1)S(1)}, u32[]{:S(2)}, u32[]{:S(2)}) %collective-permute-start.22) | collective-permute-done | bytes 131104 | tf_op jit(solution)/shard_map/ppermute | solution.py:467
  262.5 9.6 %collective-permute-done.24 = bf16[4,64,1024]{2,1,0:T(8,128)(2,1)S(1)} collective-permute-done((bf16[4,64,1024]{2,1,0:T(8,128)(2,1)S(1)}, bf16[4,64,1024]{2,1,0:T(8,128)(2,1)S(1)}, u32[]{:S(2)}, u32[]{:S(2)}) %collective-permute-start.24) | collective-permute-done | bytes 524320 | tf_op jit(solution)/shard_map/ppermute | solution.py:467
  272.3 2.6 collective-permute-done.25.far_ref
  275.0 22.0 %cross.1 = (f32[1027,1,1027]{2,1,0:T(1,128)}, f32[1027,1,1027]{2,1,0:T(1,128)}, f32[1027,1,1027]{2,1,0:T(1,128)}, f32[1027,1,1027]{2,1,0:T(1,128)}, bf16[1027,1027]{1,0:T(8,128)(2,1)}) custom-call(s32[1]{0:T(128)} %bitcast.33.place_ref, bf16[2,4,64,1024]{3,2,1,0:T(8,128)(2,1)S(1)} %pad_maximum_fusion.near_ref, ...), custom_call_target="tpu_custom_call" | custom-call | tf_op jit(solution)/shard_map/cross/pallas_call | solution.py:729
  (160 shorter events, 61.4 us)
Async XLA Ops:
  9.5 14.7 %all-to-all-start = ((s32[32,1,512]{2,1,0:T(1,128)}), s32[32,1,512]{2,1,0:T(1,128)S(1)}, u32[]{:S(2)}, u32[]{:S(2)}) async-start(s32[32,1,512]{2,1,0:T(1,128)} %copy.47), calls=%async_computation | async-start | bytes 131072 | tf_op jit(solution)/shard_map/all_to_all | solution.py:545
  24.2 13.9 %collective-permute-start.2 = (bf16[32,1152]{1,0:T(8,128)(2,1)S(1)}, bf16[32,1152]{1,0:T(8,128)(2,1)S(1)}, u32[]{:S(2)}, u32[]{:S(2)}) collective-permute-start(bf16[32,1152]{1,0:T(8,128)(2,1)S(1)} %pad.32), channel_id=1, source_target_pairs={{0,12},{1,13},{2,14},{3,15},{4,8},{5,9},{6,10},{7,11},{8,4},{9,5},... | collective-permute-start | bytes 221192 | tf_op jit(solution)/shard_map/ppermute | solution.py:467
  25.7 12.4 %collective-permute-start.1 = (bf16[32,1152]{1,0:T(8,128)(2,1)S(1)}, bf16[32,1152]{1,0:T(8,128)(2,1)S(1)}, u32[]{:S(2)}, u32[]{:S(2)}) collective-permute-start(bf16[32,1152]{1,0:T(8,128)(2,1)S(1)} %pad.32), channel_id=1, source_target_pairs={{0,8},{1,9},{2,10},{3,11},{4,12},{5,13},{6,14},{7,15},{8,0},{9,1},... | collective-permute-start | bytes 221192 | tf_op jit(solution)/shard_map/ppermute | solution.py:467
  26.1 12.1 %collective-permute-start = (bf16[32,1152]{1,0:T(8,128)(2,1)S(1)}, bf16[32,1152]{1,0:T(8,128)(2,1)S(1)}, u32[]{:S(2)}, u32[]{:S(2)}) collective-permute-start(bf16[32,1152]{1,0:T(8,128)(2,1)S(1)} %pad.32), channel_id=1, source_target_pairs={{0,4},{1,5},{2,6},{3,7},{4,0},{5,1},{6,2},{7,3},{8,12},{9,13},{10,... | collective-permute-start | bytes 221192 | tf_op jit(solution)/shard_map/ppermute | solution.py:467
  38.2 51.7 %all-to-all-start.1 = ((bf16[32,144,128]{2,1,0:T(8,128)(2,1)}), bf16[32,144,128]{2,1,0:T(8,128)(2,1)S(1)}, u32[]{:S(2)}, u32[]{:S(2)}) async-start(bf16[32,144,128]{2,1,0:T(8,128)(2,1)} %bitcast.16), calls=%async_computation.1 | async-start | bytes 2359296 | tf_op jit(solution)/shard_map/all_to_all | solution.py:564
  42.1 19.0 %collective-permute-start.4 = (bf16[4,32,1152]{2,1,0:T(8,128)(2,1)S(1)}, bf16[4,32,1152]{2,1,0:T(8,128)(2,1)S(1)}, u32[]{:S(2)}, u32[]{:S(2)}) collective-permute-start(bf16[4,32,1152]{2,1,0:T(8,128)(2,1)S(1)} %get-tuple-element.194), channel_id=1, source_target_pairs={{0,16},{16,0},{1,17},{17,1},{2,18},{18,2},{3,19},{19,3},{4,20},{20... | collective-permute-start | bytes 884744 | tf_op jit(solution)/shard_map/ppermute | solution.py:467
  46.3 43.6 %collective-permute-start.3 = (bf16[528,1152]{1,0:T(8,128)(2,1)}, bf16[528,1152]{1,0:T(8,128)(2,1)}, u32[]{:S(2)}, u32[]{:S(2)}) collective-permute-start(bf16[528,1152]{1,0:T(8,128)(2,1)} %constant_dynamic-slice_fusion.5), channel_id=1, source_target_pairs={{0,16},{16,0},{1,17},{17,1},{2,18},{18,2},{3,19},{19,3},{4,20},{20... | collective-permute-start | bytes 3649544 | tf_op jit(solution)/shard_map/ppermute | solution.py:467
  61.1 16.6 %collective-permute-start.5 = (bf16[4,2,32,1152]{3,2,0,1:T(8,128)(2,1)S(1)}, bf16[4,2,32,1152]{3,2,0,1:T(8,128)(2,1)S(1)}, u32[]{:S(2)}, u32[]{:S(2)}) collective-permute-start(bf16[4,2,32,1152]{3,2,0,1:T(8,128)(2,1)S(1)} %maximum_select_fusion.2), channel_id=1, source_target_pairs={{0,2},{1,3},{2,0},{3,1},{4,6},{5,7},{6,4},{7,5},{8,10},{9,11},{10,... | collective-permute-start | bytes 1769480 | tf_op jit(solution)/shard_map/ppermute | solution.py:467
  89.9 23.1 %collective-permute-start.6 = (bf16[528,1152]{1,0:T(8,128)(2,1)}, bf16[528,1152]{1,0:T(8,128)(2,1)}, u32[]{:S(2)}, u32[]{:S(2)}) collective-permute-start(bf16[528,1152]{1,0:T(8,128)(2,1)} %collective-permute-done.3.half_ref), channel_id=1, source_target_pairs={{0,1},{1,0},{2,3},{3,2},{4,5},{5,4},{6,7},{7,6},{8,9},{9,8},{10,11... | collective-permute-start | bytes 3649544 | tf_op jit(solution)/shard_map/ppermute | solution.py:467
  89.9 23.1 %collective-permute-start.7 = (bf16[8,2,32,1152]{3,2,1,0:T(8,128)(2,1)S(1)}, bf16[8,2,32,1152]{3,2,1,0:T(8,128)(2,1)}, u32[]{:S(2)}, u32[]{:S(2)}) collective-permute-start(bf16[8,2,32,1152]{3,2,1,0:T(8,128)(2,1)S(1)} %bitcast.124), channel_id=1, source_target_pairs={{0,1},{1,0},{2,3},{3,2},{4,5},{5,4},{6,7},{7,6},{8,9},{9,8},{10,11... | collective-permute-start | bytes 3538952 | tf_op jit(solution)/shard_map/ppermute | solution.py:467
  158.6 50.8 %all-to-all-start.2 = ((bf16[32,144,128]{2,1,0:T(8,128)(2,1)}), bf16[32,144,128]{2,1,0:T(8,128)(2,1)S(1)}, u32[]{:S(2)}, u32[]{:S(2)}) async-start(bf16[32,144,128]{2,1,0:T(8,128)(2,1)} %bitcast.28), calls=%async_computation.2 | async-start | bytes 2359296 | tf_op jit(solution)/shard_map/all_to_all | solution.py:672
  166.8 30.5 %collective-permute-start.10 = (bf16[2,2,96,1024]{3,2,1,0:T(8,128)(2,1)S(1)}, bf16[2,2,96,1024]{3,2,1,0:T(8,128)(2,1)S(1)}, u32[]{:S(2)}, u32[]{:S(2)}) collective-permute-start(bf16[2,2,96,1024]{3,2,1,0:T(8,128)(2,1)S(1)} %get-tuple-element.123), channel_id=1, source_target_pairs={{0,16},{16,0},{1,17},{17,1},{2,18},{18,2},{3,19},{19,3},{4,20},{20... | collective-permute-start | bytes 2359304 | tf_op jit(solution)/shard_map/ppermute | solution.py:467
  168.7 28.7 %collective-permute-start.11 = (bf16[2,2,96,1024]{3,2,1,0:T(8,128)(2,1)S(1)}, bf16[2,2,96,1024]{3,2,1,0:T(8,128)(2,1)S(1)}, u32[]{:S(2)}, u32[]{:S(2)}) collective-permute-start(bf16[2,2,96,1024]{3,2,1,0:T(8,128)(2,1)S(1)} %get-tuple-element.124), channel_id=1, source_target_pairs={{0,2},{1,3},{2,0},{3,1},{4,6},{5,7},{6,4},{7,5},{8,10},{9,11},{10,... | collective-permute-start | bytes 2359304 | tf_op jit(solution)/shard_map/ppermute | solution.py:467
  170.2 27.1 %collective-permute-start.12 = (f32[16,1152]{1,0:T(8,128)S(1)}, f32[16,1152]{1,0:T(8,128)S(1)}, u32[]{:S(2)}, u32[]{:S(2)}) collective-permute-start(f32[16,1152]{1,0:T(8,128)S(1)} %pad_maximum_fusion.5), channel_id=1, source_target_pairs={{0,16},{16,0},{1,17},{17,1},{2,18},{18,2},{3,19},{19,3},{4,20},{20... | collective-permute-start | bytes 221192 | tf_op jit(solution)/shard_map/ppermute | solution.py:467
  207.0 10.2 %collective-permute-start.15 = (f32[16,1152]{1,0:T(8,128)S(1)}, f32[16,1152]{1,0:T(8,128)S(1)}, u32[]{:S(2)}, u32[]{:S(2)}) collective-permute-start(f32[16,1152]{1,0:T(8,128)S(1)} %add.164), channel_id=1, source_target_pairs={{0,8},{1,9},{2,10},{3,11},{4,12},{5,13},{6,14},{7,15},{8,0},{9,1},... | collective-permute-start | bytes 221192 | tf_op jit(solution)/shard_map/ppermute | solution.py:467
  219.5 8.2 %collective-permute-start.16 = (bf16[2,96,1024]{2,1,0:T(8,128)(2,1)S(1)}, bf16[2,96,1024]{2,1,0:T(8,128)(2,1)S(1)}, u32[]{:S(2)}, u32[]{:S(2)}) collective-permute-start(bf16[2,96,1024]{2,1,0:T(8,128)(2,1)S(1)} %get-tuple-element.137), channel_id=1, source_target_pairs={{0,2},{1,3},{2,0},{3,1},{4,6},{5,7},{6,4},{7,5},{8,10},{9,11},{10,... | collective-permute-start | bytes 1179656 | tf_op jit(solution)/shard_map/ppermute | solution.py:467
  221.1 7.9 %collective-permute-start.17 = (bf16[2,96,1024]{2,1,0:T(8,128)(2,1)S(1)}, bf16[2,96,1024]{2,1,0:T(8,128)(2,1)}, u32[]{:S(2)}, u32[]{:S(2)}) collective-permute-start(bf16[2,96,1024]{2,1,0:T(8,128)(2,1)S(1)} %get-tuple-element.138), channel_id=1, source_target_pairs={{0,16},{16,0},{1,17},{17,1},{2,18},{18,2},{3,19},{19,3},{4,20},{20... | collective-permute-start | bytes 1179656 | tf_op jit(solution)/shard_map/ppermute | solution.py:467
  230.7 9.2 %collective-permute-start.18 = (bf16[96,1024]{1,0:T(8,128)(2,1)S(1)}, bf16[96,1024]{1,0:T(8,128)(2,1)S(1)}, u32[]{:S(2)}, u32[]{:S(2)}) collective-permute-start(bf16[96,1024]{1,0:T(8,128)(2,1)S(1)} %get-tuple-element.142), channel_id=1, source_target_pairs={{0,4},{1,5},{2,6},{3,7},{4,0},{5,1},{6,2},{7,3},{8,12},{9,13},{10,... | collective-permute-start | bytes 589832 | tf_op jit(solution)/shard_map/ppermute | solution.py:467
  232.4 13.0 %collective-permute-start.19 = (bf16[96,1024]{1,0:T(8,128)(2,1)S(1)}, bf16[96,1024]{1,0:T(8,128)(2,1)S(1)}, u32[]{:S(2)}, u32[]{:S(2)}) collective-permute-start(bf16[96,1024]{1,0:T(8,128)(2,1)S(1)} %get-tuple-element.143), channel_id=1, source_target_pairs={{0,8},{1,9},{2,10},{3,11},{4,12},{5,13},{6,14},{7,15},{8,0},{9,1},... | collective-permute-start | bytes 589832 | tf_op jit(solution)/shard_map/ppermute | solution.py:467
  232.7 12.6 %collective-permute-start.20 = (bf16[96,1024]{1,0:T(8,128)(2,1)S(1)}, bf16[96,1024]{1,0:T(8,128)(2,1)S(1)}, u32[]{:S(2)}, u32[]{:S(2)}) collective-permute-start(bf16[96,1024]{1,0:T(8,128)(2,1)S(1)} %get-tuple-element.144), channel_id=1, source_target_pairs={{0,12},{1,13},{2,14},{3,15},{4,8},{5,9},{6,10},{7,11},{8,4},{9,5},... | collective-permute-start | bytes 589832 | tf_op jit(solution)/shard_map/ppermute | solution.py:467
  245.6 7.4 %collective-permute-start.21 = (bf16[64,1024]{1,0:T(8,128)(2,1)S(1)}, bf16[64,1024]{1,0:T(8,128)(2,1)S(1)}, u32[]{:S(2)}, u32[]{:S(2)}) collective-permute-start(bf16[64,1024]{1,0:T(8,128)(2,1)S(1)} %slice.234), channel_id=1, source_target_pairs={{0,4},{1,5},{2,6},{3,7},{4,0},{5,1},{6,2},{7,3},{8,12},{9,13},{10,... | collective-permute-start | bytes 393224 | tf_op jit(solution)/shard_map/ppermute | solution.py:467
  249.0 11.4 %collective-permute-start.22 = (bf16[64,1024]{1,0:T(8,128)(2,1)S(1)}, bf16[64,1024]{1,0:T(8,128)(2,1)S(1)}, u32[]{:S(2)}, u32[]{:S(2)}) collective-permute-start(bf16[64,1024]{1,0:T(8,128)(2,1)S(1)} %slice.234), channel_id=1, source_target_pairs={{0,8},{1,9},{2,10},{3,11},{4,12},{5,13},{6,14},{7,15},{8,0},{9,1},... | collective-permute-start | bytes 393224 | tf_op jit(solution)/shard_map/ppermute | solution.py:467
  249.0 11.4 %collective-permute-start.23 = (bf16[64,1024]{1,0:T(8,128)(2,1)S(1)}, bf16[64,1024]{1,0:T(8,128)(2,1)S(1)}, u32[]{:S(2)}, u32[]{:S(2)}) collective-permute-start(bf16[64,1024]{1,0:T(8,128)(2,1)S(1)} %slice.234), channel_id=1, source_target_pairs={{0,12},{1,13},{2,14},{3,15},{4,8},{5,9},{6,10},{7,11},{8,4},{9,5},... | collective-permute-start | bytes 393224 | tf_op jit(solution)/shard_map/ppermute | solution.py:467
  260.6 11.6 %collective-permute-start.24 = (bf16[4,64,1024]{2,1,0:T(8,128)(2,1)S(1)}, bf16[4,64,1024]{2,1,0:T(8,128)(2,1)S(1)}, u32[]{:S(2)}, u32[]{:S(2)}) collective-permute-start(bf16[4,64,1024]{2,1,0:T(8,128)(2,1)S(1)} %get-tuple-element.187), channel_id=1, source_target_pairs={{0,2},{1,3},{2,0},{3,1},{4,6},{5,7},{6,4},{7,5},{8,10},{9,11},{10,... | collective-permute-start | bytes 1572872 | tf_op jit(solution)/shard_map/ppermute | solution.py:467
  (29 other events, 357.0 us)

commit v3 on v2

--- a/solution.py
+++ b/solution.py
@@ -54,9 +54,16 @@
     return pl.CostEstimate(flops=0, bytes_accessed=micros * 3_000_000, transcendentals=0)
 
 
-def slots_kernel(shift, slots, stride, ids_ref, valid_ref, asked_ref, place_ref):
+def slots_kernel(shift, slots, stride, groups, ids_ref, valid_ref, table_ref, asked_ref, place_ref, low_ref):
     feats, half = ids_ref.shape
     owners = asked_ref.shape[0]
+    embed, rows_own = table_ref.shape
+    real = jnp.sum(valid_ref[...].astype(F32), axis=1, keepdims=True)
+    high_real = jnp.floor(real * (1.0 / 64.0))
+    spare = (low_ref.shape[0] - embed, rows_own)
+    lane = iota(spare, 1)
+    counts = jnp.where(lane == 0, high_real, jnp.where(lane == 1, real - 64.0 * high_real, 0.0))
+    low_ref[...] = jnp.concatenate([table_ref[...], counts], axis=0).astype(BF16)
     before = (iota((half, half), 0) < iota((half, half), 1)).astype(BF16)
     owner_of = iota((owners, half), 0)
     slot_of = iota((slots, half), 0)
@@ -65,6 +72,8 @@
     for feat in range(feats):
         ids = ids_ref[feat : feat + 1, :]
         owner = lax.shift_right_logical(ids, shift)
+        plane = lax.shift_right_logical(owner, (4 * groups).bit_length() - 1) * 4 + (owner & 3)
+        owner = plane * groups + (lax.shift_right_logical(owner, 2) & (groups - 1))
         row = ids & ((1 << shift) - 1)
         hit = (owner_of == owner).astype(F32)
         earlier = contract(hit.astype(BF16), before, 1, 0) + base
@@ -84,42 +93,51 @@
     tall = round_up(slots, LANES)
     if tall > slots:
         rows = jnp.concatenate([rows, jnp.zeros((tall - slots, owners), F32)], axis=0)
-    count = jnp.sum(valid_ref[...])
     wide = asked_ref.shape[1]
     flat = rows.T
     if wide > tall:
         flat = jnp.concatenate([flat, jnp.zeros((owners, wide - tall), F32)], axis=1)
-    asked_ref[...] = jnp.where(iota((owners, wide), 1) < slots, flat.astype(jnp.int32), count)
-
-
-def lookup_kernel(slots, stride, ids_ref, table_ref, rows_ref, blocks_ref):
-    embed, rows_own = table_ref.shape
-    tall = round_up(embed, 8)
+    asked_ref[...] = flat.astype(jnp.int32)
+
+
+def lookup_kernel(embed, stride, spot_ref, ids_ref, *refs):
+    tables, (rows_ref, blocks_ref) = refs[:-2], refs[-2:]
+    groups = len(tables)
+    tall, rows_own = tables[0].shape
     parts = rows_own // 256
     wide = ids_ref.shape[1]
     third = stride // 3
-    blocks_ref[...] = jnp.zeros_like(blocks_ref)
-    for part in range(parts):
-        blocks_ref[part * tall : part * tall + embed, :] = table_ref[:, part * 256 : part * 256 + 256]
-    blocks = blocks_ref[...].astype(BF16)
+    count = jnp.zeros((1, 1), F32)
+    for k, table_ref in enumerate(tables):
+        table = table_ref[...].astype(F32)
+        count = count + 64.0 * table[embed : embed + 1, 0:1] + table[embed : embed + 1, 1:2]
+        table = jnp.where(iota((tall, rows_own), 0) < embed, table, 0.0)
+        block = jnp.concatenate([table[:, part * 256 : part * 256 + 256] for part in range(parts)], axis=0)
+        blocks_ref[spot_ref[1] ^ k] = block.astype(BF16)
     low_of = iota((256, wide), 0)
-
-    def step(owner, carry):
-        ids = ids_ref[pl.ds(owner, 1), :]
-        high = lax.shift_right_logical(ids, 8)
-        pick = (low_of == (ids & 255)).astype(F32).astype(BF16)
-        found = contract(blocks, pick, 1, 0)
-        mine = jnp.zeros((tall, wide), F32)
-        for part in range(parts):
-            mine = jnp.where(high == part, found[part * tall : part * tall + tall], mine)
-        square = jnp.concatenate([mine, jnp.zeros((LANES - tall, wide), F32)], axis=0).T
-        packed = square[:third]
-        for piece in (1, 2):
-            packed = packed + pltpu.roll(square[piece * third : piece * third + third], embed * piece, 1)
-        rows_ref[pl.ds(pl.multiple_of(owner * third, 16), third), :] = packed.astype(BF16)
+    high_count = jnp.floor(count * (1.0 / 64.0))
+    row, lane = iota((third, LANES), 0), iota((third, LANES), 1)
+    counts = jnp.where(lane == LANES - 2, high_count, jnp.where(lane == LANES - 1, count - 64.0 * high_count, 0.0))
+    counts = jnp.where(row == 0, counts, 0.0)
+
+    def step(peer, carry):
+        for group in range(groups):
+            block = peer * groups + group
+            ids = ids_ref[pl.ds(block, 1), :]
+            high = lax.shift_right_logical(ids, 8)
+            pick = (low_of == (ids & 255)).astype(F32).astype(BF16)
+            found = contract(blocks_ref[group], pick, 1, 0)
+            mine = jnp.zeros((tall, wide), F32)
+            for part in range(parts):
+                mine = jnp.where(high == part, found[part * tall : part * tall + tall], mine)
+            square = jnp.concatenate([mine, jnp.zeros((LANES - tall, wide), F32)], axis=0).T
+            packed = square[:third] if group else square[:third] + counts
+            for piece in (1, 2):
+                packed = packed + pltpu.roll(square[piece * third : piece * third + third], embed * piece, 1)
+            rows_ref[pl.ds(pl.multiple_of(block * third, 16), third), :] = packed.astype(BF16)
         return carry
 
-    lax.fori_loop(0, ids_ref.shape[0], step, 0, unroll=4)
+    lax.fori_loop(0, ids_ref.shape[0] // groups, step, 0)
 
 
 def column_map(feat, dense_width, embed, turned):
@@ -131,7 +149,9 @@
     return pl.multiple_of(tile * LANES, LANES), hit.astype(F32).astype(BF16)
 
 
-def inputs_kernel(feats, stride, embed, dense_width, place_ref, rows_ref, dense_ref, x_ref, far_ref, even_ref, odd_ref, sum_ref):
+def inputs_kernel(
+    feats, stride, groups, embed, dense_width, place_ref, rows_ref, dense_ref, x_ref, count_ref, far_ref, even_ref, odd_ref, sum_ref
+):
     half = even_ref.shape[0]
     third = stride // 3
     width = dense_width + embed * feats
@@ -143,7 +163,13 @@
             far_ref[pl.ds(pl.multiple_of(owner * stride + piece * third, 16), third), :] = rolled
         return carry
 
-    lax.fori_loop(0, far_ref.shape[0] // stride, unpack, 0, unroll=4)
+    owners = far_ref.shape[0] // stride
+    lax.fori_loop(0, owners, unpack, 0, unroll=4)
+    counts = jnp.zeros((16, LANES), F32)
+    for peer in range(owners // groups):
+        start = peer * groups * third
+        counts = counts + rows_ref[start : start + 16, :].astype(F32)
+    count_ref[...] = 64.0 * counts[0:1, LANES - 2 : LANES - 1] + counts[0:1, LANES - 1 : LANES]
     sum_ref[...] = jnp.zeros_like(sum_ref)
     sum_ref[:, :LANES] = dense_ref[...].astype(F32)
     ones = width - width // LANES * LANES
@@ -229,37 +255,50 @@
     lax.fori_loop(0, owners, pack, 0, unroll=4)
 
 
-def table_kernel(
-    slots, stride, ids_ref, rows_ref, table_ref, first_ref, second_ref,
-    grad_ref, first_new_ref, second_new_ref, table_new_ref, total_ref,
-):
-    embed, rows_own = table_ref.shape
+def table_kernel(embed, slots, stride, spot_ref, ids_ref, rows_ref, own_ref, other_ref, total_ref):
+    groups, size = total_ref.shape[:2]
     tall = round_up(embed, 8)
-    parts = rows_own // 256
+    parts = size // tall
     wide = ids_ref.shape[1]
     third = stride // 3
     low_of = iota((256, wide), 0)
     lane = iota((1, wide), 1)
     total_ref[...] = jnp.zeros_like(total_ref)
 
-    def step(owner, carry):
-        ids = jnp.where(lane < slots, ids_ref[pl.ds(owner, 1), :], -1)
-        high = lax.shift_right_arithmetic(ids, 8)
-        pick = (low_of == (ids & 255)).astype(F32).astype(BF16)
-        block = rows_ref[pl.ds(pl.multiple_of(owner * third, 16), third), :].astype(F32)
-        pieces = [block if k == 0 else pltpu.roll(block, LANES - embed * k, 1) for k in range(3)]
-        if wide > stride:
-            pieces.append(jnp.zeros((wide - stride, LANES), F32))
-        square = jnp.concatenate(pieces, axis=0)[:wide].T
-        mine = jnp.where(iota((tall, wide), 0) < embed, square[:tall], 0.0)
-        spread = [jnp.where(high == part, mine, 0.0) for part in range(parts)]
-        total_ref[...] += contract(jnp.concatenate(spread, axis=0).astype(BF16), pick, 1, 1)
+    def step(peer, carry):
+        for group in range(groups):
+            at = peer * groups + group
+            ids = jnp.where(lane < slots, ids_ref[pl.ds(at, 1), :], -1)
+            high = lax.shift_right_arithmetic(ids, 8)
+            pick = (low_of == (ids & 255)).astype(F32).astype(BF16)
+            block = rows_ref[pl.ds(pl.multiple_of(at * third, 16), third), :].astype(F32)
+            pieces = [block if k == 0 else pltpu.roll(block, LANES - embed * k, 1) for k in range(3)]
+            if wide > stride:
+                pieces.append(jnp.zeros((wide - stride, LANES), F32))
+            square = jnp.concatenate(pieces, axis=0)[:wide].T
+            mine = jnp.where(iota((tall, wide), 0) < embed, square[:tall], 0.0)
+            spread = [jnp.where(high == part, mine, 0.0) for part in range(parts)]
+            total_ref[group] += contract(jnp.concatenate(spread, axis=0).astype(BF16), pick, 1, 1)
         return carry
 
-    lax.fori_loop(0, ids_ref.shape[0], step, 0, unroll=4)
-    for part in range(parts):
+    lax.fori_loop(0, ids_ref.shape[0] // groups, step, 0)
+    own_ref[...] = total_ref[spot_ref[1]]
+    for k in range(1, groups):
+        other_ref[k - 1] = total_ref[spot_ref[1] ^ k].astype(BF16)
+
+
+def update_kernel(*refs):
+    own_ref, table_ref, first_ref, second_ref = refs[:4]
+    others = refs[4:-4]
+    grad_ref, first_new_ref, second_new_ref, table_new_ref = refs[-4:]
+    embed, rows_own = table_ref.shape
+    tall = round_up(embed, 8)
+    total = own_ref[...]
+    for ref in others:
+        total = total + ref[...].astype(F32)
+    for part in range(rows_own // 256):
         here = slice(part * 256, part * 256 + 256)
-        grad = total_ref[part * tall : part * tall + embed, :]
+        grad = total[part * tall : part * tall + embed, :]
         one, two, new = adamw(table_ref[:, here], grad, first_ref[:, here], second_ref[:, here], 0.25)
         grad_ref[:, here] = grad
         first_new_ref[:, here] = one
@@ -272,34 +311,32 @@
 
 
 def towers_kernel(
-    spot_ref, count_ref, bias_ref, x_ref, vec_ref, target_ref, valid_ref,
-    own_ref, half_ref, half_core_ref, deep_ref, deep_core_ref,
+    spot_ref, count_ref, bias_ref, x_ref, vec_ref, labels_ref,
+    own_ref, half_ref, half_core_ref, here_ref, here_core_ref, near_ref, near_core_ref,
     one_ref, d_second_ref, d_first_ref, d_deep_ref, dx_ref, head_ref,
     cross_ref, all_deep_ref, pre_first_ref, layer_ref, pre_second_ref, two_ref, slope_ref, hidden_ref, arrival,
 ):
     half, wide = x_ref.shape
-    pairs, _, deep_rows = deep_ref.shape[:3]
-    hidden = 4 * pairs * deep_rows
-    tower, core = spot_ref[0], spot_ref[3]
+    groups, _, deep_rows = here_ref.shape[:3]
+    hidden = 8 * groups * deep_rows
+    tower, near, core = spot_ref[0], spot_ref[2], spot_ref[3]
     middle = half_ref.shape[0]
+    moves = [(own_ref, cross_ref.at[tower, pl.ds(0, 2 * middle), :])]
+    for ref, at_core in ((half_ref, core), (half_core_ref, 1 - core)):
+        moves.append((ref, cross_ref.at[1 - tower, pl.ds(pl.multiple_of(at_core * middle, 16), middle), :]))
+    for ref, at_near, at_core in (
+        (here_ref, near, core), (here_core_ref, near, 1 - core), (near_ref, 1 - near, core), (near_core_ref, 1 - near, 1 - core)
+    ):
+        for k in range(2):
+            moves.append((ref.at[:, k], all_deep_ref.at[k, :, at_near, at_core]))
     copies = []
-    for k, (source, target) in enumerate(
-        (
-            (own_ref, cross_ref.at[tower, pl.ds(0, 2 * middle), :]),
-            (half_ref, cross_ref.at[1 - tower, pl.ds(pl.multiple_of(core * middle, 16), middle), :]),
-            (half_core_ref, cross_ref.at[1 - tower, pl.ds(pl.multiple_of((1 - core) * middle, 16), middle), :]),
-            (deep_ref.at[:, 0], all_deep_ref.at[0, :, core]),
-            (deep_ref.at[:, 1], all_deep_ref.at[1, :, core]),
-            (deep_core_ref.at[:, 0], all_deep_ref.at[0, :, 1 - core]),
-            (deep_core_ref.at[:, 1], all_deep_ref.at[1, :, 1 - core]),
-        )
-    ):
+    for k, (source, target) in enumerate(moves):
         copies.append(pltpu.make_async_copy(source, target, arrival.at[k]))
         copies[-1].start()
 
     def deep_block(at, size):
-        per = 2 * deep_rows
-        block = all_deep_ref[at // (hidden // 2), pl.ds(at % (hidden // 2) // per, size // per)]
+        tower, at = at // (hidden // 2), at % (hidden // 2)
+        block = all_deep_ref[tower, pl.ds(at // (4 * deep_rows), size // (4 * deep_rows))]
         return block.reshape(size, wide)
 
     def lanes(x):
@@ -340,7 +377,8 @@
         slope_ref[:, here] = gate * (1.0 + pre * (1.0 - gate))
         score = score + lanes(out.astype(F32) * vec_ref[4:5, here])
     logit = jnp.sum(score, axis=1, keepdims=True) + bias_ref[0, 0]
-    target, valid = target_ref[...], valid_ref[...]
+    labels = jnp.concatenate([labels_ref[...], jnp.zeros((6, half), jnp.int32)], axis=0).astype(F32).T
+    target, valid = labels[:, 0:1], labels[:, 1:2]
     softplus = jnp.maximum(logit, 0.0) + jnp.log1p(jnp.exp(-jnp.abs(logit)))
     loss = jnp.sum(valid * (softplus - target * logit), axis=0, keepdims=True)
     d_logit = valid * (jax.nn.sigmoid(logit) - target) / count_ref[0, 0]
@@ -366,7 +404,7 @@
         layer_ref[:, here] = d_one * (1.0 + pre_first_ref[:, here]) + d_two * pre_second_ref[:, here]
     for at, size in tiles(wide):
         here = slice(at, at + size)
-        columns = all_deep_ref[:, :, :, :, here].reshape(hidden, size)
+        columns = all_deep_ref[:, :, :, :, :, here].reshape(hidden, size)
         dx = contract(d_first_ref[...], cross_ref[0, here, :], 1, 1) + contract(d_deep_ref[...], columns, 1, 0)
         dx_ref[:, here] = (dx + layer_ref[:, here]).astype(BF16)
 
@@ -520,51 +558,62 @@
     third = round_up(-(-slots // 3), 16)
     stride = 3 * third
     shift = rows_own.bit_length() - 1
-    asked_wide = round_up(max(slots + 1, stride), LANES)
+    asked_wide = round_up(stride, LANES)
 
     def mine(x, dim):
         return lax.dynamic_slice_in_dim(x, tower * half, half, dim)
 
     ids = mine(category_ids.T, 1)
     valid = mine(valid_mask, 0)
-    target = mine(labels, 0).astype(F32)
+    target = mine(labels, 0)
     dense = jnp.pad(mine(dense_feats, 0), ((0, 0), (0, LANES - dense_width)))
 
-    asked, slot = pl.pallas_call(
-        functools.partial(slots_kernel, shift, slots, stride),
+    table_t = embed_table.T
+    tall = round_up(embed, 8)
+    asked, slot, table_low = pl.pallas_call(
+        functools.partial(slots_kernel, shift, slots, stride, groups),
         out_shape=(
             jax.ShapeDtypeStruct((owners, asked_wide), jnp.int32),
             jax.ShapeDtypeStruct((feats * half // LANES, LANES), jnp.int32),
+            jax.ShapeDtypeStruct((tall, rows_own), BF16),
         ),
-        in_specs=[in_vmem()] * 2,
-        out_specs=(in_vmem(), in_vmem()),
+        in_specs=[in_vmem()] * 3,
+        out_specs=(in_vmem(),) * 3,
         compiler_params=params(32),
         name="slots",
-    )(ids, valid.reshape(1, half))
+    )(ids, valid.reshape(1, half), table_t)
     slot = slot.reshape(-1)
-    arrived = lax.all_to_all(asked, ("tower", "batch"), split_axis=0, concat_axis=0, tiled=True)
+    planes = [[t * batch + z * 4 + k for t in range(towers) for k in range(4)] for z in range(groups)]
+
+    def in_plane(x):
+        return lax.all_to_all(
+            x, ("tower", "batch"), split_axis=0, concat_axis=0, axis_index_groups=planes, tiled=True
+        )
+
+    tables = [table_low] + [flip(table_low, "batch", k * 4, batch) for k in range(1, groups)]
+
+    main = width // LANES * LANES
+    rows_c = main // batch
     middle = round_up(-(-width // 2), 16)
     own_low = jnp.pad(cross_weight[0].astype(BF16), ((0, 2 * middle - width), (0, wide - width)))
     deep_own = jnp.pad(deep_weight.astype(BF16), ((0, 0), (0, wide - width)))
-    own_low, deep_own, arrived = lax.optimization_barrier((own_low, deep_own, arrived))
-    count = jnp.sum(arrived[:, slots]).astype(F32)
-    table_t = embed_table.T
-    deep_parts = flip_far(deep_own, batch, groups)
+    asked, deep_own = lax.optimization_barrier((asked, deep_own))
+    arrived = in_plane(asked)
+    deep_pair = join(deep_own, flip(deep_own, "tower", 1, towers), 0, tower)
+    tables[1:], own_low, arrived = lax.optimization_barrier((tables[1:], own_low, arrived))
     got_low = flip(lax.dynamic_slice_in_dim(own_low, core * middle, middle, 0), "tower", 1, towers)
+    weights = flip_far(deep_pair, batch, groups)
     found = pl.pallas_call(
-        functools.partial(lookup_kernel, slots, stride),
+        functools.partial(lookup_kernel, embed, stride),
         out_shape=jax.ShapeDtypeStruct((owners * third, LANES), BF16),
-        in_specs=[in_vmem()] * 2,
+        in_specs=[in_smem()] + [in_vmem()] * (1 + groups),
         out_specs=in_vmem(),
-        scratch_shapes=[pltpu.VMEM((rows_own // 256 * round_up(embed, 8), 256), F32)],
+        scratch_shapes=[pltpu.VMEM((groups, rows_own // 256 * tall, 256), BF16)],
         compiler_params=params(32),
         name="lookup",
-    )(arrived, table_t)
-    deep_parts, found = lax.optimization_barrier((deep_parts, found))
-    returned = lax.all_to_all(found, ("tower", "batch"), split_axis=0, concat_axis=0, tiled=True)
-    deep_low = in_order(deep_parts, groups)
-    deep_low = join(deep_low, flip(deep_low, "tower", 1, towers), 1, tower)
-    deep_low = join(deep_low, flip(deep_low, "batch", 2, batch), 1, near).reshape(batch // 2, towers, deep_rows, wide)
+    )(spot, arrived, *tables)
+    returned = in_plane(found)
+    weights = in_order(weights, groups)
 
     def widen(x):
         return jnp.pad(x, (0, wide - x.shape[0]))
@@ -579,18 +628,15 @@
         ]
         + [jnp.zeros((wide,), F32)] * 3
     )
-    target = target.reshape(half, 1)
-    valid = valid.astype(F32).reshape(half, 1)
-    returned, own_low, got_low, deep_low, vec, target, valid = lax.optimization_barrier(
-        (returned, own_low, got_low, deep_low, vec, target, valid)
-    )
+    returned, own_low, got_low, weights, vec = lax.optimization_barrier((returned, own_low, got_low, weights, vec))
     got_core = flip(got_low, "batch", 1, batch)
-    deep_core = flip(deep_low, "batch", 1, batch)
-    inputs = pl.pallas_call(
-        functools.partial(inputs_kernel, feats, stride, embed, dense_width),
-        out_shape=jax.ShapeDtypeStruct((half, wide), BF16),
+    weights_core = flip(weights, "batch", 1, batch)
+    weights_near = flip(weights, "batch", 2, batch)
+    inputs, count = pl.pallas_call(
+        functools.partial(inputs_kernel, feats, stride, groups, embed, dense_width),
+        out_shape=(jax.ShapeDtypeStruct((half, wide), BF16), jax.ShapeDtypeStruct((1, 1), F32)),
         in_specs=[in_smem(), in_vmem(), in_vmem()],
-        out_specs=in_vmem(),
+        out_specs=(in_vmem(), in_vmem()),
         scratch_shapes=[
             pltpu.VMEM((owners * stride, LANES), F32),
             pltpu.VMEM((half, LANES), F32),
@@ -601,30 +647,54 @@
         name="inputs",
     )(slot, returned, dense)
 
+    inputs, count, weights_near = lax.optimization_barrier((inputs, count, weights_near))
+    weights_both = flip(weights_near, "batch", 1, batch)
     low = jax.ShapeDtypeStruct((half, wide), BF16)
     low_deep = jax.ShapeDtypeStruct((half, hidden), BF16)
     one_low, d_second, d_first, d_deep, d_inputs, heads = pl.pallas_call(
         towers_kernel,
         out_shape=(low, low, low, low_deep, low, jax.ShapeDtypeStruct((8, wide), F32)),
-        in_specs=[in_smem()] * 3 + [in_vmem()] * 4 + [pl.BlockSpec(memory_space=pl.ANY)] * 5,
+        in_specs=[in_smem()] * 3 + [in_vmem()] * 3 + [pl.BlockSpec(memory_space=pl.ANY)] * 7,
         out_specs=(in_vmem(),) * 6,
         scratch_shapes=[
             pltpu.VMEM((2, wide, wide), BF16),
-            pltpu.VMEM((2, batch // 2, 2, deep_rows, wide), BF16),
+            pltpu.VMEM((2, groups, 2, 2, deep_rows, wide), BF16),
             pltpu.VMEM((half, wide), F32),
             pltpu.VMEM((half, wide), F32),
             pltpu.VMEM((half, wide), F32),
             pltpu.VMEM((half, wide), BF16),
             pltpu.VMEM((half, hidden), F32),
             pltpu.VMEM((half, hidden), BF16),
-            pltpu.SemaphoreType.DMA((7,)),
+            pltpu.SemaphoreType.DMA((11,)),
         ],
         compiler_params=params(56),
         name="towers",
     )(
-        spot, count.reshape(1, 1), vectors[-1:].reshape(1, 1), inputs, vec, target, valid,
-        own_low, got_low, got_core, deep_low, deep_core,
+        spot, count, vectors[-1:].reshape(1, 1), inputs, vec, jnp.stack([target, valid]),
+        own_low, got_low, got_core, weights, weights_core, weights_near, weights_both,
     )
+    parts = jax.ShapeDtypeStruct((2, 2, 2, groups // 2, rows_c + deep_rows, main), BF16)
+    keep, give, rest = pl.pallas_call(
+        functools.partial(grads_kernel, deep_rows),
+        out_shape=(parts, parts, jax.ShapeDtypeStruct((24, wide), F32)),
+        in_specs=[in_smem()] + [in_vmem()] * 6,
+        out_specs=(in_vmem(),) * 3,
+        scratch_shapes=[pltpu.VMEM((wide, half), BF16)],
+        compiler_params=params(56),
+        name="grads",
+    )(spot, inputs, one_low, d_second, d_first, d_deep, heads)
+    got = flip(give, "batch", 1, batch)
+    rest = rest + flip(rest, "batch", 1, batch)
+
+    def by_tower(x):
+        return flip(x, "tower", 1, towers)
+
+    def by_near(x):
+        return flip(x, "batch", 2, batch)
+
+    to_one, rest, d_inputs = lax.optimization_barrier(([keep[k, 1] + got[k, 1] for k in range(2)], rest, d_inputs))
+    from_one = [by_tower(to_one[0]), by_near(to_one[1])]
+    rest = rest[:16] + by_tower(jnp.concatenate([rest[16:22], rest[6:16]]))
     sent = pl.pallas_call(
         functools.partial(send_kernel, feats, slots, stride, embed, dense_width),
         out_shape=jax.ShapeDtypeStruct((owners * third, LANES), BF16),
@@ -638,63 +708,34 @@
         compiler_params=params(48),
         name="send",
     )(slot, d_inputs)
-    sent, inputs, one_low, d_second, d_first, d_deep, heads = lax.optimization_barrier(
-        (sent, inputs, one_low, d_second, d_first, d_deep, heads)
-    )
-    main = width // LANES * LANES
-    rows_c = main // batch
-    parts = jax.ShapeDtypeStruct((2, 2, 2, groups // 2, rows_c + deep_rows, main), BF16)
-    keep, give, rest = pl.pallas_call(
-        functools.partial(grads_kernel, deep_rows),
-        out_shape=(parts, parts, jax.ShapeDtypeStruct((24, wide), F32)),
-        in_specs=[in_smem()] + [in_vmem()] * 6,
-        out_specs=(in_vmem(),) * 3,
-        scratch_shapes=[pltpu.VMEM((wide, half), BF16)],
-        compiler_params=params(56),
-        name="grads",
-    )(spot, inputs, one_low, d_second, d_first, d_deep, heads)
-    got = flip(give, "batch", 1, batch)
-    rest = rest + flip(rest, "batch", 1, batch)
-
-    def by_tower(x):
-        return flip(x, "tower", 1, towers)
-
-    def by_near(x):
-        return flip(x, "batch", 2, batch)
-
-    to_one, rest = lax.optimization_barrier(([keep[k, 1] + got[k, 1] for k in range(2)], rest))
-    from_one = [by_tower(to_one[0]), by_near(to_one[1])]
-    rest = rest[:16] + by_tower(jnp.concatenate([rest[16:22], rest[6:16]]))
-    from_one, rest = lax.optimization_barrier((from_one, rest))
+    from_one, rest, sent = lax.optimization_barrier((from_one, rest, sent))
+    back = in_plane(sent)
+    to_two = lax.optimization_barrier([keep[k, 0, 1] + got[k, 0, 1] + from_one[k][1] for k in range(2)])
+    from_two = [by_near(to_two[0]), by_tower(to_two[1])]
     rest = rest + by_near(rest)
     for bit in [4 << k for k in range(groups.bit_length() - 1)]:
         rest = rest + flip(rest, "batch", bit, batch)
-    back = lax.all_to_all(sent, ("tower", "batch"), split_axis=0, concat_axis=0, tiled=True)
-    shape_t = jax.ShapeDtypeStruct((embed, rows_own), F32)
-    table_grad, table_one, table_two, table_new = pl.pallas_call(
-        functools.partial(table_kernel, slots, stride),
-        out_shape=(shape_t,) * 4,
-        in_specs=[in_vmem()] * 5,
-        out_specs=(in_vmem(),) * 4,
-        scratch_shapes=[pltpu.VMEM((rows_own // 256 * round_up(embed, 8), 256), F32)],
-        compiler_params=params(32),
-        name="table",
-    )(arrived, back, table_t, table_first.T, table_second.T)
-
-    from_one, rest, table_grad, table_one, table_two, table_new = lax.optimization_barrier(
-        (from_one, rest, table_grad, table_one, table_two, table_new)
-    )
-    to_two = lax.optimization_barrier([keep[k, 0, 1] + got[k, 0, 1] + from_one[k][1] for k in range(2)])
-    from_two = [by_near(to_two[0]), by_tower(to_two[1])]
-    from_two = lax.optimization_barrier(from_two)
+    from_two, rest, back = lax.optimization_barrier((from_two, rest, back))
+    blocks_t = (rows_own // 256 * tall, 256)
     both = [keep[k, 0, 0] + got[k, 0, 0] + from_one[k][0] + from_two[k] for k in range(2)]
     both = lax.optimization_barrier([part[k] for part in both for k in range(groups // 2)])
     from_far = [flip(both[k], "batch", k * 4, batch) for k in range(1, groups)]
-    from_far = lax.optimization_barrier(from_far)
+    both, back = lax.optimization_barrier((both, back))
+    table_own, table_other = pl.pallas_call(
+        functools.partial(table_kernel, embed, slots, stride),
+        out_shape=(jax.ShapeDtypeStruct(blocks_t, F32), jax.ShapeDtypeStruct((groups - 1,) + blocks_t, BF16)),
+        in_specs=[in_smem()] + [in_vmem()] * 2,
+        out_specs=(in_vmem(),) * 2,
+        scratch_shapes=[pltpu.VMEM((groups,) + blocks_t, F32)],
+        compiler_params=params(32),
+        name="table",
+    )(spot, arrived, back)
+    from_far, table_own, table_other = lax.optimization_barrier((from_far, table_own, table_other))
     summed = both[0].astype(F32)
     for part in from_far:
         summed = summed + part.astype(F32)
     chunk = flip_far(summed[:rows_c].astype(BF16), batch, groups)
+    table_got = [flip(table_other[k - 1], "batch", k * 4, batch) for k in range(1, groups)]
     across = flip(chunk, "batch", 2, batch)
     vector_grad = jnp.concatenate(
         [rest[6, :width], rest[7, :width], rest[11, :hidden], rest[12, :width], rest[13, :hidden], rest[14, :1]]
@@ -705,13 +746,22 @@
     deep_one, deep_two, deep_new = adamw(deep_weight, deep_grad, deep_first, deep_second, 0.03)
     deep_copy = deep_new.astype(BF16)
     side = rest[:8][None]
+    shape_t = jax.ShapeDtypeStruct((embed, rows_own), F32)
+    table_grad, table_one, table_two, table_new = pl.pallas_call(
+        update_kernel,
+        out_shape=(shape_t,) * 4,
+        in_specs=[in_vmem()] * (3 + groups),
+        out_specs=(in_vmem(),) * 4,
+        compiler_params=params(32),
+        name="update",
+    )(table_own, table_t, table_first.T, table_second.T, *table_got)
     (
         across, side, vector_grad, vector_one, vector_two, vector_new,
-        deep_grad, deep_one, deep_two, deep_new, deep_copy,
+        deep_grad, deep_one, deep_two, deep_new, deep_copy, table_grad, table_one, table_two, table_new,
     ) = lax.optimization_barrier(
         (
             across, side, vector_grad, vector_one, vector_two, vector_new,
-            deep_grad, deep_one, deep_two, deep_new, deep_copy,
+            deep_grad, deep_one, deep_two, deep_new, deep_copy, table_grad, table_one, table_two, table_new,
         )
     )
     chunk = jnp.stack([chunk, across])
@@ -745,7 +795,7 @@
     loss_sum = rest[14, 1]
     return (
         loss_sum,
-        count,
+        count[0, 0],
         cross_grad,
         cross_one,
         cross_two,

time: 299 us -> 271 us (0.906)
  waiting for transfers between devices: 113 us -> 79.7 us
  other arithmetic: 10.7 us -> 14.9 us
  starting transfers between devices: 47.7 us -> 51.9 us
  local copies, waits for them, and re-layouts: 16 us -> 12.4 us
    ppermute x26 -> x33, waiting for transfers between devices: 110 us -> 70 us  [flip(): return lax.ppermute(x, axis, [(i, i ^ bit) for i in range(size)])]
    ppermute x26 -> x33, starting transfers between devices: 32 us -> 40.9 us  [flip(): return lax.ppermute(x, axis, [(i, i ^ bit) for i in range(size)])]
    all_to_all x3, waiting for transfers between devices: 2.22 us -> 9.65 us  [in_plane(): lax.all_to_all(x, ('tower', 'batch'), split_axis=0, concat_axis=0, axis_i...]
    all_to_all x3, starting transfers between devices: 15.7 us -> 11 us  [in_plane(): lax.all_to_all(x, ('tower', 'batch'), split_axis=0, concat_axis=0, axis_i...]
    pallas_call x4 -> x5, Pallas kernels: 41.6 us -> 42.8 us  [the longest x1 17.4 us: local(): pl.pallas_call(functools.partial(inputs_kernel, feats, stride, groups, em...]
    unnamed x49 -> x48, local copies, waits for them, and re-layouts: 6.15 us -> 6.18 us
  transfers between devices with their start and end apart: 29 -> 36, of which waited for: 16 -> 16; matrix products, arithmetic and copies ran while one was open for 6% -> 6% of each run, Pallas kernels for 12% -> 13%
where the time goes in v3:
time: 271 us; the launch traced here: 270 us
  Pallas kernels  110 us (41%)
  waiting for transfers between devices  79.7 us (29%)
  starting transfers between devices  51.9 us (19%)
  other arithmetic  14.9 us (5%)
  local copies, waits for them, and re-layouts  12.4 us (5%)
    ppermute x33, waiting for transfers between devices, flip(): return lax.ppermute(x, axis, [(i, i ^ bit) for i in range(size)])  70 us
    ppermute x33, starting transfers between devices, flip(): return lax.ppermute(x, axis, [(i, i ^ bit) for i in range(size)])  40.9 us
    pallas_call x1, Pallas kernels, local(): pl.pallas_call(cross_kernel, grid_spec=pltpu.PrefetchScalarGridSpec(num_s...  22 us
    pallas_call x1, Pallas kernels, local(): pl.pallas_call(towers_kernel, out_shape=(low, low, low, low_deep, low, ja...  18 us
    pallas_call x1, Pallas kernels, local(): pl.pallas_call(functools.partial(inputs_kernel, feats, stride, groups, em...  17.4 us
    pallas_call x1, Pallas kernels, local(): pl.pallas_call(functools.partial(send_kernel, feats, slots, stride, embed...  16.6 us
    all_to_all x3, starting transfers between devices, in_plane(): lax.all_to_all(x, ('tower', 'batch'), split_axis=0, concat_axis=0, axis_i...  11 us
    pallas_call x1, Pallas kernels, local(): pl.pallas_call(functools.partial(grads_kernel, deep_rows), out_shape=(par...  10.5 us
  transfers between devices with their start and end apart: 36, of which 16 were waited for; matrix products, arithmetic and copies ran while one was open for 6% of the time, Pallas kernels for 13%

profile of v3, /device:TPU:0, one launch (start us, length us, event | category | flops | bytes accessed | tf_op | source)
XLA Modules:
  0.0 270.3 jit_solution(6184408184350204463)
XLA Ops:
  2.6 7.2 %slots.1 = (s32[32,512]{1,0:T(8,128)S(1)}, s32[104,128]{1,0:T(8,128)S(1)}, bf16[40,2048]{1,0:T(8,128)(2,1)S(1)}) custom-call(s32[26,512]{1,0:T(8,128)S(1)} %dynamic-slice_bitcast_fusion.ids_ref, s32[1,512]{1,0:T(1,128)S(1)} %bitcast.111, f32[39,2048]{1,0:T(8,128)S(1)} %bitcast.105), custom_call_target="tpu_custom_call" | custom-call | tf_op jit(solution)/shard_map/slots/pallas_call | solution.py:573
  9.8 5.1 %collective-permute-start.2 = (bf16[40,2048]{1,0:T(8,128)(2,1)S(1)}, bf16[40,2048]{1,0:T(8,128)(2,1)S(1)}, u32[]{:S(2)}, u32[]{:S(2)}) collective-permute-start(bf16[40,2048]{1,0:T(8,128)(2,1)S(1)} %get-tuple-element.101.refs_0_), channel_id=1, source_target_pairs={{0,12},{1,13},{2,14},{3,15},{4,8},{5,9},{6,10},{7,11},{8,4},{9,5},... | collective-permute-start | bytes 491528 | tf_op jit(solution)/shard_map/ppermute | solution.py:505
  17.2 3.9 %all-to-all-start = ((s32[8,4,512]{2,1,0:T(4,128)}), s32[8,4,512]{2,1,0:T(4,128)S(1)}, u32[]{:S(2)}, u32[]{:S(2)}) async-start(s32[8,4,512]{2,1,0:T(4,128)} %all_to_all.24), calls=%async_computation | async-start | bytes 131072 | tf_op jit(solution)/shard_map/all_to_all | solution.py:589
  32.4 10.0 %lookup.1 = bf16[4608,128]{1,0:T(8,128)(2,1)} custom-call(s32[4]{0:T(128)S(1)} %pad_add_fusion.1.spot_ref, s32[32,512]{1,0:T(8,128)S(1)} %all_to_all.26.ids_ref, bf16[40,2048]{1,0:T(8,128)(2,1)S(1)} %get-tuple-element.101.refs_0_, bf16[40,2048]{1,0:T(8,128)(2,1)S(1)} %collective-permute-done.refs_1_, bf16[40,2048]{1,0:T(8,128)(2,1)S(1)} %collective-permute-done.1.refs_2_, ...), custom_call_target="tpu_custom_call" | custom-call | tf_op jit(solution)/shard_map/lookup/pallas_call | solution.py:606
  42.4 3.6 %all-to-all-start.1 = ((bf16[8,576,128]{2,1,0:T(8,128)(2,1)}), bf16[8,576,128]{2,1,0:T(8,128)(2,1)S(1)}, u32[]{:S(2)}, u32[]{:S(2)}) async-start(bf16[8,576,128]{2,1,0:T(8,128)(2,1)} %bitcast.9), calls=%async_computation.1 | async-start | bytes 2359296 | tf_op jit(solution)/shard_map/all_to_all | solution.py:589
  50.5 4.2 %collective-permute-done.7 = bf16[2,32,1152]{2,1,0:T(8,128)(2,1)S(1)} collective-permute-done((bf16[2,32,1152]{2,1,0:T(8,128)(2,1)S(1)}, bf16[2,32,1152]{2,1,0:T(8,128)(2,1)S(1)}, u32[]{:S(2)}, u32[]{:S(2)}) %collective-permute-start.7) | collective-permute-done | bytes 147488 | tf_op jit(solution)/shard_map/ppermute | solution.py:505
  54.7 6.1 %collective-permute-done.6 = bf16[2,32,1152]{2,1,0:T(8,128)(2,1)S(1)} collective-permute-done((bf16[2,32,1152]{2,1,0:T(8,128)(2,1)S(1)}, bf16[2,32,1152]{2,1,0:T(8,128)(2,1)S(1)}, u32[]{:S(2)}, u32[]{:S(2)}) %collective-permute-start.6) | collective-permute-done | bytes 147488 | tf_op jit(solution)/shard_map/ppermute | solution.py:505
  61.1 9.6 %all-to-all-done.1 = bf16[8,576,128]{2,1,0:T(8,128)(2,1)S(1)} async-done(((bf16[8,576,128]{2,1,0:T(8,128)(2,1)}), bf16[8,576,128]{2,1,0:T(8,128)(2,1)S(1)}, u32[]{:S(2)}, u32[]{:S(2)}) %all-to-all-start.1) | async-done | bytes 1179680 | tf_op jit(solution)/shard_map/all_to_all | solution.py:589
  72.7 17.4 %inputs.1 = (bf16[512,1152]{1,0:T(8,128)(2,1)S(1)}, f32[1,1]{1,0:T(1,128)}) custom-call(s32[13312]{0:T(1024)S(1)} %bitcast.109, bf16[4608,128]{1,0:T(8,128)(2,1)S(1)} %bitcast.104, bf16[512,128]{1,0:T(8,128)(2,1)S(1)} %pad.38.dense_ref), custom_call_target="tpu_custom_call" | custom-call | tf_op jit(solution)/shard_map/inputs/pallas_call | solution.py:635
  94.5 18.0 %towers.1 = (bf16[512,1152]{1,0:T(8,128)(2,1)}, bf16[512,1152]{1,0:T(8,128)(2,1)}, bf16[512,1152]{1,0:T(8,128)(2,1)}, bf16[512,1024]{1,0:T(8,128)(2,1)}, bf16[512,1152]{1,0:T(8,128)(2,1)}, /*index=5*/f32[8,1152]{1,0:T(8,128)}) custom-call(s32[4]{0:T(128)} %copy-done.8, f32[1,1]{1,0:T(1,128)} %get-tuple-element.115.count_ref, f32[1,1]{1,0:T(1,128)} %bitcast.18.bias_ref, ...), custom_call_target="tpu_custom_call" | custom-call | tf_op jit(solution)/shard_map/towers/pallas_call | solution.py:654
  112.6 10.5 %grads.1 = (bf16[2,2,2,2,96,1024]{5,4,3,2,1,0:T(8,128)(2,1)}, bf16[2,2,2,2,96,1024]{5,4,3,2,1,0:T(8,128)(2,1)}, f32[24,1152]{1,0:T(8,128)}) custom-call(s32[4]{0:T(128)} %copy-done.8, bf16[512,1152]{1,0:T(8,128)(2,1)} %copy-done.2, bf16[512,1152]{1,0:T(8,128)(2,1)} %get-tuple-element.120.one_ref, bf16[512,1152]{1,0:T(8,128)(2,1)} %get-tuple-element.121.d_second_ref, ...), custom_call_target="tpu_custom_call" | custom-call | tf_op jit(solution)/shard_map/grads/pallas_call | solution.py:677
  123.6 5.5 %collective-permute-done.13 = f32[24,1152]{1,0:T(8,128)S(1)} collective-permute-done((f32[24,1152]{1,0:T(8,128)}, f32[24,1152]{1,0:T(8,128)S(1)}, u32[]{:S(2)}, u32[]{:S(2)}) %collective-permute-start.13) | collective-permute-done | bytes 110624 | tf_op jit(solution)/shard_map/ppermute | solution.py:505
  135.5 16.6 %send.1 = bf16[4608,128]{1,0:T(8,128)(2,1)} custom-call(s32[13312]{0:T(1024)S(1)} %bitcast.110, bf16[512,1152]{1,0:T(8,128)(2,1)S(1)} %copy-done.5), custom_call_target="tpu_custom_call" | custom-call | tf_op jit(solution)/shard_map/send/pallas_call | solution.py:698
  154.2 3.6 %all-to-all-start.2 = ((bf16[8,576,128]{2,1,0:T(8,128)(2,1)}), bf16[8,576,128]{2,1,0:T(8,128)(2,1)S(1)}, u32[]{:S(2)}, u32[]{:S(2)}) async-start(bf16[8,576,128]{2,1,0:T(8,128)(2,1)} %bitcast.26), calls=%async_computation.2 | async-start | bytes 2359296 | tf_op jit(solution)/shard_map/all_to_all | solution.py:589
  164.1 19.4 %collective-permute-done.19 = f32[16,1152]{1,0:T(8,128)S(1)} collective-permute-done((f32[16,1152]{1,0:T(8,128)S(1)}, f32[16,1152]{1,0:T(8,128)S(1)}, u32[]{:S(2)}, u32[]{:S(2)}) %collective-permute-start.19) | collective-permute-done | bytes 73760 | tf_op jit(solution)/shard_map/ppermute | solution.py:505
  184.5 3.5 %collective-permute-done.20 = f32[16,1152]{1,0:T(8,128)S(1)} collective-permute-done((f32[16,1152]{1,0:T(8,128)S(1)}, f32[16,1152]{1,0:T(8,128)S(1)}, u32[]{:S(2)}, u32[]{:S(2)}) %collective-permute-start.20) | collective-permute-done | bytes 73760 | tf_op jit(solution)/shard_map/ppermute | solution.py:505
  189.9 4.2 %collective-permute-done.21 = f32[16,1152]{1,0:T(8,128)S(1)} collective-permute-done((f32[16,1152]{1,0:T(8,128)S(1)}, f32[16,1152]{1,0:T(8,128)S(1)}, u32[]{:S(2)}, u32[]{:S(2)}) %collective-permute-start.21) | collective-permute-done | bytes 73760 | tf_op jit(solution)/shard_map/ppermute | solution.py:505
  197.0 3.0 %collective-permute-start.23 = (bf16[96,1024]{1,0:T(8,128)(2,1)S(1)}, bf16[96,1024]{1,0:T(8,128)(2,1)S(1)}, u32[]{:S(2)}, u32[]{:S(2)}) collective-permute-start(bf16[96,1024]{1,0:T(8,128)(2,1)S(1)} %get-tuple-element.144), channel_id=1, source_target_pairs={{0,8},{1,9},{2,10},{3,11},{4,12},{5,13},{6,14},{7,15},{8,0},{9,1},... | collective-permute-start | bytes 589832 | tf_op jit(solution)/shard_map/ppermute | solution.py:505
  201.3 7.0 %table.1 = (f32[320,256]{1,0:T(8,128)S(1)}, bf16[3,320,256]{2,1,0:T(8,128)(2,1)S(1)}) custom-call(s32[4]{0:T(128)S(1)} %copy-done.9, s32[32,512]{1,0:T(8,128)S(1)} %all_to_all.26.ids_ref, bf16[4608,128]{1,0:T(8,128)(2,1)S(1)} %bitcast.103), custom_call_target="tpu_custom_call" | custom-call | tf_op jit(solution)/shard_map/table/pallas_call | solution.py:724
  209.8 3.3 %collective-permute-done.23 = bf16[96,1024]{1,0:T(8,128)(2,1)S(1)} collective-permute-done((bf16[96,1024]{1,0:T(8,128)(2,1)S(1)}, bf16[96,1024]{1,0:T(8,128)(2,1)S(1)}, u32[]{:S(2)}, u32[]{:S(2)}) %collective-permute-start.23) | collective-permute-done | bytes 196640 | tf_op jit(solution)/shard_map/ppermute | solution.py:505
  214.1 2.8 %collective-permute-start.25 = (bf16[64,1024]{1,0:T(8,128)(2,1)S(1)}, bf16[64,1024]{1,0:T(8,128)(2,1)S(1)}, u32[]{:S(2)}, u32[]{:S(2)}) collective-permute-start(bf16[64,1024]{1,0:T(8,128)(2,1)S(1)} %slice.244), channel_id=1, source_target_pairs={{0,4},{1,5},{2,6},{3,7},{4,0},{5,1},{6,2},{7,3},{8,12},{9,13},{10,... | collective-permute-start | bytes 393224 | tf_op jit(solution)/shard_map/ppermute | solution.py:505
  220.7 7.2 %collective-permute-done.26 = bf16[64,1024]{1,0:T(8,128)(2,1)S(1)} collective-permute-done((bf16[64,1024]{1,0:T(8,128)(2,1)S(1)}, bf16[64,1024]{1,0:T(8,128)(2,1)S(1)}, u32[]{:S(2)}, u32[]{:S(2)}) %collective-permute-start.26) | collective-permute-done | bytes 131104 | tf_op jit(solution)/shard_map/ppermute | solution.py:505
  237.8 6.2 %collective-permute-done.30.refs_5_ = bf16[320,256]{1,0:T(8,128)(2,1)S(1)} collective-permute-done((bf16[320,256]{1,0:T(8,128)(2,1)S(1)}, bf16[320,256]{1,0:T(8,128)(2,1)S(1)}, u32[]{:S(2)}, u32[]{:S(2)}) %collective-permute-start.30) | collective-permute-done | bytes 163872 | tf_op jit(solution)/shard_map/ppermute | solution.py:505
  248.1 22.0 %cross.1 = (f32[1027,1,1027]{2,1,0:T(1,128)}, f32[1027,1,1027]{2,1,0:T(1,128)}, f32[1027,1,1027]{2,1,0:T(1,128)}, f32[1027,1,1027]{2,1,0:T(1,128)}, bf16[1027,1027]{1,0:T(8,128)(2,1)}) custom-call(s32[1]{0:T(128)} %bitcast.30.place_ref, bf16[2,4,64,1024]{3,2,1,0:T(8,128)(2,1)S(1)} %pad_maximum_fusion.near_ref, ...), custom_call_target="tpu_custom_call" | custom-call | tf_op jit(solution)/shard_map/cross/pallas_call | solution.py:779
  (171 shorter events, 68.8 us)
Async XLA Ops:
  9.8 17.8 %collective-permute-start.2 = (bf16[40,2048]{1,0:T(8,128)(2,1)S(1)}, bf16[40,2048]{1,0:T(8,128)(2,1)S(1)}, u32[]{:S(2)}, u32[]{:S(2)}) collective-permute-start(bf16[40,2048]{1,0:T(8,128)(2,1)S(1)} %get-tuple-element.101.refs_0_), channel_id=1, source_target_pairs={{0,12},{1,13},{2,14},{3,15},{4,8},{5,9},{6,10},{7,11},{8,4},{9,5},... | collective-permute-start | bytes 491528 | tf_op jit(solution)/shard_map/ppermute | solution.py:505
  14.9 13.9 %collective-permute-start.1 = (bf16[40,2048]{1,0:T(8,128)(2,1)S(1)}, bf16[40,2048]{1,0:T(8,128)(2,1)S(1)}, u32[]{:S(2)}, u32[]{:S(2)}) collective-permute-start(bf16[40,2048]{1,0:T(8,128)(2,1)S(1)} %get-tuple-element.101.refs_0_), channel_id=1, source_target_pairs={{0,8},{1,9},{2,10},{3,11},{4,12},{5,13},{6,14},{7,15},{8,0},{9,1},... | collective-permute-start | bytes 491528 | tf_op jit(solution)/shard_map/ppermute | solution.py:505
  14.9 13.9 %collective-permute-start = (bf16[40,2048]{1,0:T(8,128)(2,1)S(1)}, bf16[40,2048]{1,0:T(8,128)(2,1)S(1)}, u32[]{:S(2)}, u32[]{:S(2)}) collective-permute-start(bf16[40,2048]{1,0:T(8,128)(2,1)S(1)} %get-tuple-element.101.refs_0_), channel_id=1, source_target_pairs={{0,4},{1,5},{2,6},{3,7},{4,0},{5,1},{6,2},{7,3},{8,12},{9,13},{10,... | collective-permute-start | bytes 491528 | tf_op jit(solution)/shard_map/ppermute | solution.py:505
  21.0 24.9 %collective-permute-start.4 = (bf16[32,1152]{1,0:T(8,128)(2,1)S(1)}, bf16[32,1152]{1,0:T(8,128)(2,1)S(1)}, u32[]{:S(2)}, u32[]{:S(2)}) collective-permute-start(bf16[32,1152]{1,0:T(8,128)(2,1)S(1)} %pad.32), channel_id=1, source_target_pairs={{0,16},{16,0},{1,17},{17,1},{2,18},{18,2},{3,19},{19,3},{4,20},{20... | collective-permute-start | bytes 221192 | tf_op jit(solution)/shard_map/ppermute | solution.py:505
  29.9 40.8 %collective-permute-start.3 = (bf16[528,1152]{1,0:T(8,128)(2,1)}, bf16[528,1152]{1,0:T(8,128)(2,1)}, u32[]{:S(2)}, u32[]{:S(2)}) collective-permute-start(bf16[528,1152]{1,0:T(8,128)(2,1)} %constant_dynamic-slice_fusion.5), channel_id=1, source_target_pairs={{0,16},{16,0},{1,17},{17,1},{2,18},{18,2},{3,19},{19,3},{4,20},{20... | collective-permute-start | bytes 3649544 | tf_op jit(solution)/shard_map/ppermute | solution.py:505
  42.4 28.3 %all-to-all-start.1 = ((bf16[8,576,128]{2,1,0:T(8,128)(2,1)}), bf16[8,576,128]{2,1,0:T(8,128)(2,1)S(1)}, u32[]{:S(2)}, u32[]{:S(2)}) async-start(bf16[8,576,128]{2,1,0:T(8,128)(2,1)} %bitcast.9), calls=%async_computation.1 | async-start | bytes 2359296 | tf_op jit(solution)/shard_map/all_to_all | solution.py:589
  48.6 12.2 %collective-permute-start.6 = (bf16[2,32,1152]{2,1,0:T(8,128)(2,1)S(1)}, bf16[2,32,1152]{2,1,0:T(8,128)(2,1)S(1)}, u32[]{:S(2)}, u32[]{:S(2)}) collective-permute-start(bf16[2,32,1152]{2,1,0:T(8,128)(2,1)S(1)} %maximum_select_fusion.1), channel_id=1, source_target_pairs={{0,8},{1,9},{2,10},{3,11},{4,12},{5,13},{6,14},{7,15},{8,0},{9,1},... | collective-permute-start | bytes 442376 | tf_op jit(solution)/shard_map/ppermute | solution.py:505
  48.6 12.2 %collective-permute-start.5 = (bf16[2,32,1152]{2,1,0:T(8,128)(2,1)S(1)}, bf16[2,32,1152]{2,1,0:T(8,128)(2,1)S(1)}, u32[]{:S(2)}, u32[]{:S(2)}) collective-permute-start(bf16[2,32,1152]{2,1,0:T(8,128)(2,1)S(1)} %maximum_select_fusion.1), channel_id=1, source_target_pairs={{0,4},{1,5},{2,6},{3,7},{4,0},{5,1},{6,2},{7,3},{8,12},{9,13},{10,... | collective-permute-start | bytes 442376 | tf_op jit(solution)/shard_map/ppermute | solution.py:505
  70.7 22.6 %collective-permute-start.9 = (bf16[528,1152]{1,0:T(8,128)(2,1)}, bf16[528,1152]{1,0:T(8,128)(2,1)S(1)}, u32[]{:S(2)}, u32[]{:S(2)}) collective-permute-start(bf16[528,1152]{1,0:T(8,128)(2,1)} %collective-permute-done.3.half_ref), channel_id=1, source_target_pairs={{0,1},{1,0},{2,3},{3,2},{4,5},{5,4},{6,7},{7,6},{8,9},{9,8},{10,11... | collective-permute-start | bytes 3649544 | tf_op jit(solution)/shard_map/ppermute | solution.py:505
  70.7 20.4 %collective-permute-start.8 = (bf16[4,2,32,1152]{3,2,1,0:T(8,128)(2,1)S(1)}, bf16[4,2,32,1152]{3,2,1,0:T(8,128)(2,1)}, u32[]{:S(2)}, u32[]{:S(2)}) collective-permute-start(bf16[4,2,32,1152]{3,2,1,0:T(8,128)(2,1)S(1)} %pad_maximum_fusion.2.here_ref), channel_id=1, source_target_pairs={{0,2},{1,3},{2,0},{3,1},{4,6},{5,7},{6,4},{7,5},{8,10},{9,11},{10,... | collective-permute-start | bytes 1769480 | tf_op jit(solution)/shard_map/ppermute | solution.py:505
  72.4 20.3 %collective-permute-start.10 = (bf16[4,2,32,1152]{3,2,1,0:T(8,128)(2,1)S(1)}, bf16[4,2,32,1152]{3,2,1,0:T(8,128)(2,1)S(1)}, u32[]{:S(2)}, u32[]{:S(2)}) collective-permute-start(bf16[4,2,32,1152]{3,2,1,0:T(8,128)(2,1)S(1)} %pad_maximum_fusion.2.here_ref), channel_id=1, source_target_pairs={{0,1},{1,0},{2,3},{3,2},{4,5},{5,4},{6,7},{7,6},{8,9},{9,8},{10,11... | collective-permute-start | bytes 1769480 | tf_op jit(solution)/shard_map/ppermute | solution.py:505
  132.8 21.4 %collective-permute-start.14 = (bf16[2,2,96,1024]{3,2,1,0:T(8,128)(2,1)S(1)}, bf16[2,2,96,1024]{3,2,1,0:T(8,128)(2,1)S(1)}, u32[]{:S(2)}, u32[]{:S(2)}) collective-permute-start(bf16[2,2,96,1024]{3,2,1,0:T(8,128)(2,1)S(1)} %get-tuple-element.129), channel_id=1, source_target_pairs={{0,16},{16,0},{1,17},{17,1},{2,18},{18,2},{3,19},{19,3},{4,20},{20... | collective-permute-start | bytes 2359304 | tf_op jit(solution)/shard_map/ppermute | solution.py:505
  134.3 19.9 %collective-permute-start.15 = (bf16[2,2,96,1024]{3,2,1,0:T(8,128)(2,1)S(1)}, bf16[2,2,96,1024]{3,2,1,0:T(8,128)(2,1)S(1)}, u32[]{:S(2)}, u32[]{:S(2)}) collective-permute-start(bf16[2,2,96,1024]{3,2,1,0:T(8,128)(2,1)S(1)} %get-tuple-element.130), channel_id=1, source_target_pairs={{0,2},{1,3},{2,0},{3,1},{4,6},{5,7},{6,4},{7,5},{8,10},{9,11},{10,... | collective-permute-start | bytes 2359304 | tf_op jit(solution)/shard_map/ppermute | solution.py:505
  134.8 19.3 %collective-permute-start.16 = (f32[16,1152]{1,0:T(8,128)S(1)}, f32[16,1152]{1,0:T(8,128)S(1)}, u32[]{:S(2)}, u32[]{:S(2)}) collective-permute-start(f32[16,1152]{1,0:T(8,128)S(1)} %pad_maximum_fusion.5), channel_id=1, source_target_pairs={{0,16},{16,0},{1,17},{17,1},{2,18},{18,2},{3,19},{19,3},{4,20},{20... | collective-permute-start | bytes 221192 | tf_op jit(solution)/shard_map/ppermute | solution.py:505
  154.2 40.0 %all-to-all-start.2 = ((bf16[8,576,128]{2,1,0:T(8,128)(2,1)}), bf16[8,576,128]{2,1,0:T(8,128)(2,1)S(1)}, u32[]{:S(2)}, u32[]{:S(2)}) async-start(bf16[8,576,128]{2,1,0:T(8,128)(2,1)} %bitcast.26), calls=%async_computation.2 | async-start | bytes 2359296 | tf_op jit(solution)/shard_map/all_to_all | solution.py:589
  160.2 34.0 %collective-permute-start.17 = (bf16[2,96,1024]{2,1,0:T(8,128)(2,1)}, bf16[2,96,1024]{2,1,0:T(8,128)(2,1)}, u32[]{:S(2)}, u32[]{:S(2)}) collective-permute-start(bf16[2,96,1024]{2,1,0:T(8,128)(2,1)} %get-tuple-element.135), channel_id=1, source_target_pairs={{0,2},{1,3},{2,0},{3,1},{4,6},{5,7},{6,4},{7,5},{8,10},{9,11},{10,... | collective-permute-start | bytes 1179656 | tf_op jit(solution)/shard_map/ppermute | solution.py:505
  162.1 32.0 %collective-permute-start.18 = (bf16[2,96,1024]{2,1,0:T(8,128)(2,1)}, bf16[2,96,1024]{2,1,0:T(8,128)(2,1)}, u32[]{:S(2)}, u32[]{:S(2)}) collective-permute-start(bf16[2,96,1024]{2,1,0:T(8,128)(2,1)} %get-tuple-element.136), channel_id=1, source_target_pairs={{0,16},{16,0},{1,17},{17,1},{2,18},{18,2},{3,19},{19,3},{4,20},{20... | collective-permute-start | bytes 1179656 | tf_op jit(solution)/shard_map/ppermute | solution.py:505
  163.6 20.0 %collective-permute-start.19 = (f32[16,1152]{1,0:T(8,128)S(1)}, f32[16,1152]{1,0:T(8,128)S(1)}, u32[]{:S(2)}, u32[]{:S(2)}) collective-permute-start(f32[16,1152]{1,0:T(8,128)S(1)} %slice_add_fusion.6), channel_id=1, source_target_pairs={{0,2},{1,3},{2,0},{3,1},{4,6},{5,7},{6,4},{7,5},{8,10},{9,11},{10,... | collective-permute-start | bytes 221192 | tf_op jit(solution)/shard_map/ppermute | solution.py:505
  196.7 13.1 %collective-permute-start.22 = (bf16[96,1024]{1,0:T(8,128)(2,1)S(1)}, bf16[96,1024]{1,0:T(8,128)(2,1)S(1)}, u32[]{:S(2)}, u32[]{:S(2)}) collective-permute-start(bf16[96,1024]{1,0:T(8,128)(2,1)S(1)} %get-tuple-element.143), channel_id=1, source_target_pairs={{0,4},{1,5},{2,6},{3,7},{4,0},{5,1},{6,2},{7,3},{8,12},{9,13},{10,... | collective-permute-start | bytes 589832 | tf_op jit(solution)/shard_map/ppermute | solution.py:505
  197.0 16.0 %collective-permute-start.23 = (bf16[96,1024]{1,0:T(8,128)(2,1)S(1)}, bf16[96,1024]{1,0:T(8,128)(2,1)S(1)}, u32[]{:S(2)}, u32[]{:S(2)}) collective-permute-start(bf16[96,1024]{1,0:T(8,128)(2,1)S(1)} %get-tuple-element.144), channel_id=1, source_target_pairs={{0,8},{1,9},{2,10},{3,11},{4,12},{5,13},{6,14},{7,15},{8,0},{9,1},... | collective-permute-start | bytes 589832 | tf_op jit(solution)/shard_map/ppermute | solution.py:505
  200.1 13.0 %collective-permute-start.24 = (bf16[96,1024]{1,0:T(8,128)(2,1)S(1)}, bf16[96,1024]{1,0:T(8,128)(2,1)}, u32[]{:S(2)}, u32[]{:S(2)}) collective-permute-start(bf16[96,1024]{1,0:T(8,128)(2,1)S(1)} %get-tuple-element.145), channel_id=1, source_target_pairs={{0,12},{1,13},{2,14},{3,15},{4,8},{5,9},{6,10},{7,11},{8,4},{9,5},... | collective-permute-start | bytes 589832 | tf_op jit(solution)/shard_map/ppermute | solution.py:505
  228.0 17.2 %collective-permute-start.28 = (bf16[4,64,1024]{2,1,0:T(8,128)(2,1)S(1)}, bf16[4,64,1024]{2,1,0:T(8,128)(2,1)S(1)}, u32[]{:S(2)}, u32[]{:S(2)}) collective-permute-start(bf16[4,64,1024]{2,1,0:T(8,128)(2,1)S(1)} %get-tuple-element.201), channel_id=1, source_target_pairs={{0,2},{1,3},{2,0},{3,1},{4,6},{5,7},{6,4},{7,5},{8,10},{9,11},{10,... | collective-permute-start | bytes 1572872 | tf_op jit(solution)/shard_map/ppermute | solution.py:505
  230.9 13.1 %collective-permute-start.30 = (bf16[320,256]{1,0:T(8,128)(2,1)S(1)}, bf16[320,256]{1,0:T(8,128)(2,1)S(1)}, u32[]{:S(2)}, u32[]{:S(2)}) collective-permute-start(bf16[320,256]{1,0:T(8,128)(2,1)S(1)} %get-tuple-element.203), channel_id=1, source_target_pairs={{0,8},{1,9},{2,10},{3,11},{4,12},{5,13},{6,14},{7,15},{8,0},{9,1},... | collective-permute-start | bytes 491528 | tf_op jit(solution)/shard_map/ppermute | solution.py:505
  232.3 11.7 %collective-permute-start.29 = (bf16[320,256]{1,0:T(8,128)(2,1)S(1)}, bf16[320,256]{1,0:T(8,128)(2,1)S(1)}, u32[]{:S(2)}, u32[]{:S(2)}) collective-permute-start(bf16[320,256]{1,0:T(8,128)(2,1)S(1)} %get-tuple-element.204), channel_id=1, source_target_pairs={{0,4},{1,5},{2,6},{3,7},{4,0},{5,1},{6,2},{7,3},{8,12},{9,13},{10,... | collective-permute-start | bytes 491528 | tf_op jit(solution)/shard_map/ppermute | solution.py:505
  (35 other events, 417.5 us)

commit v4 on v3

--- a/solution.py
+++ b/solution.py
@@ -463,30 +463,54 @@
 
 
 def cross_kernel(
-    place_ref, near_ref, far_ref, rest_ref, weight_ref, first_ref, second_ref,
-    grad_ref, first_new_ref, second_new_ref, new_ref, copy_ref,
+    other, blocks, place_ref, near_ref, far_ref, rest_ref, weight_ref, first_ref, second_ref, *refs
 ):
-    block = pl.program_id(0)
+    held_ref, made_ref, arrival, departure = refs[-4:]
+    sources, targets, copy_ref = (weight_ref, first_ref, second_ref), refs[-9:-5], refs[-5]
+    step, full = pl.program_id(0), blocks // 2
     width = weight_ref.shape[2]
-    main = near_ref.shape[3]
-    half = near_ref.shape[2]
+    half, main = near_ref.shape[1:]
     rows = 2 * half
     even = (place_ref[0] & 1) == 0
 
+    def moves(at, size, inward):
+        start = pl.multiple_of(cross_block(other, blocks, at, place_ref) * rows, 8)
+        pairs = []
+        for k, ref in enumerate(sources if inward else targets):
+            outside = ref.at[pl.ds(start, size), 0, :]
+            inside = (held_ref if inward else made_ref).at[k, at, pl.ds(0, size), :]
+            if inward:
+                pairs.append(pltpu.make_async_copy(outside, inside, arrival.at[k, at]))
+            else:
+                pairs.append(pltpu.make_async_copy(inside, outside, departure.at[k, at]))
+        return pairs
+
+    spans = [(at, rows) for at in range(full)] + [(full, width - main)] * other
+
+    @pl.when(step == 0)
+    def _():
+        for at, size in spans:
+            for move in moves(at, size, True):
+                move.start()
+
     def update(at, columns, grad):
-        here = (slice(at, at + grad.shape[0]), 0, columns)
-        one, two, new = adamw(weight_ref[here], grad, first_ref[here], second_ref[here], 0.03)
-        grad_ref[here] = grad
-        first_new_ref[here] = one
-        second_new_ref[here] = two
-        new_ref[here] = new
-        copy_ref[slice(at, at + grad.shape[0]), columns] = new.astype(BF16)
-
-    @pl.when(block < pl.num_programs(0) - 1)
+        here = (slice(at, at + grad.shape[0]), columns)
+        weight, first, second = (held_ref[(k, step) + here] for k in range(3))
+        one, two, new = adamw(weight, grad, first, second, 0.03)
+        for k, value in enumerate((grad, one, two, new)):
+            made_ref[(k, step) + here] = value
+        copy_ref[here] = new.astype(BF16)
+
+    @pl.when(step < full)
     def _():
-        near, far = near_ref[0, 0].astype(F32), far_ref[0, 0].astype(F32)
-        update(0, slice(0, main), jnp.where(even, near, far))
-        update(half, slice(0, main), jnp.where(even, far, near))
+        for move in moves(step, rows, True):
+            move.wait()
+        for at in range(0, main, 256):
+            columns = slice(at, min(at + 256, main))
+            near, far = near_ref[0, :, columns].astype(F32), far_ref[0, :, columns].astype(F32)
+            update(0, columns, jnp.where(even, near, far))
+            update(half, columns, jnp.where(even, far, near))
+        block = cross_block(other, blocks, step, place_ref)
         lane = pl.multiple_of(block * rows // LANES * LANES, LANES)
         side = rest_ref[0, :, pl.ds(lane, LANES)]
         side = jnp.concatenate([side, jnp.zeros((LANES - 8, LANES), F32)], axis=0).T
@@ -495,10 +519,29 @@
         for k, part in enumerate(parts):
             side = jnp.where(block % len(parts) == k, part, side)
         update(0, slice(main, width), side[:, 3 : 3 + width - main])
-
-    @pl.when(block == pl.num_programs(0) - 1)
+        for move in moves(step, rows, False):
+            move.start()
+
+    if other:
+
+        @pl.when(step == full)
+        def _():
+            for move in moves(full, width - main, True):
+                move.wait()
+            update(0, slice(0, width), rest_ref[0, :, :width])
+            for move in moves(full, width - main, False):
+                move.start()
+
+    @pl.when(step == pl.num_programs(0) - 1)
     def _():
-        update(0, slice(0, width), rest_ref[0, :, :width])
+        for at, size in spans:
+            for move in moves(at, size, False):
+                move.wait()
+
+
+def cross_block(other, blocks, step, place_ref):
+    block = step * 2 + (((place_ref[0] >> 1) & 1) ^ other)
+    return jnp.where(step == blocks // 2, blocks, block)
 
 
 def flip(x, axis, bit, size):
@@ -694,7 +737,10 @@
 
     to_one, rest, d_inputs = lax.optimization_barrier(([keep[k, 1] + got[k, 1] for k in range(2)], rest, d_inputs))
     from_one = [by_tower(to_one[0]), by_near(to_one[1])]
-    rest = rest[:16] + by_tower(jnp.concatenate([rest[16:22], rest[6:16]]))
+    rest, cross_rest = rest[:16], jnp.concatenate([rest[16:22], rest[6:16]])
+    diagonal = [(i, i ^ batch ^ 2) for i in range(owners)]
+    diagonal = lax.ppermute(cross_rest, ("tower", "batch"), diagonal)
+    rest = (rest + by_tower(cross_rest)) + (by_near(rest) + diagonal)
     sent = pl.pallas_call(
         functools.partial(send_kernel, feats, slots, stride, embed, dense_width),
         out_shape=jax.ShapeDtypeStruct((owners * third, LANES), BF16),
@@ -712,8 +758,9 @@
     back = in_plane(sent)
     to_two = lax.optimization_barrier([keep[k, 0, 1] + got[k, 0, 1] + from_one[k][1] for k in range(2)])
     from_two = [by_near(to_two[0]), by_tower(to_two[1])]
-    rest = rest + by_near(rest)
-    for bit in [4 << k for k in range(groups.bit_length() - 1)]:
+    by_far = [flip(rest, "batch", k * 4, batch) for k in range(1, 4)]
+    rest = (rest + by_far[0]) + (by_far[1] + by_far[2])
+    for bit in [16 << k for k in range(groups.bit_length() - 3)]:
         rest = rest + flip(rest, "batch", bit, batch)
     from_two, rest, back = lax.optimization_barrier((from_two, rest, back))
     blocks_t = (rows_own // 256 * tall, 256)
@@ -730,22 +777,62 @@
         compiler_params=params(32),
         name="table",
     )(spot, arrived, back)
-    from_far, table_own, table_other = lax.optimization_barrier((from_far, table_own, table_other))
-    summed = both[0].astype(F32)
-    for part in from_far:
-        summed = summed + part.astype(F32)
-    chunk = flip_far(summed[:rows_c].astype(BF16), batch, groups)
-    table_got = [flip(table_other[k - 1], "batch", k * 4, batch) for k in range(1, groups)]
-    across = flip(chunk, "batch", 2, batch)
     vector_grad = jnp.concatenate(
         [rest[6, :width], rest[7, :width], rest[11, :hidden], rest[12, :width], rest[13, :hidden], rest[14, :1]]
     )
     vector_one, vector_two, vector_new = adamw(vectors, vector_grad, vector_first, vector_second, 0.03)
     tail = lax.dynamic_slice_in_dim(rest[8 : 8 + width - main], (tower * batch + place) * deep_rows, deep_rows, 1).T
+    from_far, table_own, table_other, tail, vector_grad, vector_one, vector_two, vector_new = lax.optimization_barrier(
+        (from_far, table_own, table_other, tail, vector_grad, vector_one, vector_two, vector_new)
+    )
+    summed = both[0].astype(F32)
+    for part in from_far:
+        summed = summed + part.astype(F32)
+    chunk = flip_far(summed[:rows_c].astype(BF16), batch, groups)
     deep_grad = jnp.concatenate([summed[rows_c:], tail], axis=1)
     deep_one, deep_two, deep_new = adamw(deep_weight, deep_grad, deep_first, deep_second, 0.03)
     deep_copy = deep_new.astype(BF16)
+    chunk, deep_grad, deep_one, deep_two, deep_new, deep_copy = lax.optimization_barrier(
+        (chunk, deep_grad, deep_one, deep_two, deep_new, deep_copy)
+    )
+    across = flip(chunk, "batch", 2, batch)
     side = rest[:8][None]
+    table_got = [flip(table_other[k - 1], "batch", k * 4, batch) for k in range(1, groups)]
+    cross_t = [x.transpose(1, 0, 2) for x in (cross_weight, cross_first, cross_second)]
+    blocks = batch // 2
+    rows = 2 * rows_c
+    shape_c = jax.ShapeDtypeStruct((width, 1, width), F32)
+
+    def update_cross(other, chunk, partner, done):
+        def from_far(step, at):
+            return (jnp.minimum(step, groups - 1) ^ (at[0] >> 2), 0, 0)
+
+        piece = pl.BlockSpec((1, rows_c, main), from_far)
+        low = pl.BlockSpec((rows, width), lambda step, at: (cross_block(other, blocks, step, at), 0))
+        return pl.pallas_call(
+            functools.partial(cross_kernel, other, blocks),
+            grid_spec=pltpu.PrefetchScalarGridSpec(
+                num_scalar_prefetch=1,
+                grid=(groups + other,),
+                in_specs=[piece, piece, pl.BlockSpec((1, 8, wide), lambda step, at: (0, 0, 0))]
+                + [pl.BlockSpec(memory_space=pl.ANY)] * (3 + len(done)),
+                out_specs=(pl.BlockSpec(memory_space=pl.ANY),) * 4 + (low,),
+                scratch_shapes=[
+                    pltpu.VMEM((3, groups + other, rows, width), F32),
+                    pltpu.VMEM((4, groups + other, rows, width), F32),
+                    pltpu.SemaphoreType.DMA((3, groups + other)),
+                    pltpu.SemaphoreType.DMA((4, groups + other)),
+                ],
+            ),
+            out_shape=(shape_c,) * 4 + (jax.ShapeDtypeStruct((width, width), BF16),),
+            input_output_aliases={7 + k: k for k in range(len(done))},
+            compiler_params=params(60),
+            name="cross_other" if other else "cross",
+        )(place.reshape(1), chunk, partner, side, *cross_t, *done)
+
+    cross_out = update_cross(0, chunk, flip(chunk, "batch", 1, batch), ())
+    cross_out, across, table_got = lax.optimization_barrier((cross_out, across, table_got))
+    across_core = flip(across, "batch", 1, batch)
     shape_t = jax.ShapeDtypeStruct((embed, rows_own), F32)
     table_grad, table_one, table_two, table_new = pl.pallas_call(
         update_kernel,
@@ -755,42 +842,10 @@
         compiler_params=params(32),
         name="update",
     )(table_own, table_t, table_first.T, table_second.T, *table_got)
-    (
-        across, side, vector_grad, vector_one, vector_two, vector_new,
-        deep_grad, deep_one, deep_two, deep_new, deep_copy, table_grad, table_one, table_two, table_new,
-    ) = lax.optimization_barrier(
-        (
-            across, side, vector_grad, vector_one, vector_two, vector_new,
-            deep_grad, deep_one, deep_two, deep_new, deep_copy, table_grad, table_one, table_two, table_new,
-        )
+    across_core, table_grad, table_one, table_two, table_new = lax.optimization_barrier(
+        (across_core, table_grad, table_one, table_two, table_new)
     )
-    chunk = jnp.stack([chunk, across])
-    partner = flip(chunk, "batch", 1, batch)
-    blocks = batch // 2
-    rows = 2 * rows_c
-
-    def relative(block, at):
-        other = jnp.minimum(block, blocks - 1) ^ (at[0] >> 1)
-        return (other & 1, other >> 1, 0, 0)
-
-    piece = pl.BlockSpec((1, 1, rows_c, main), relative)
-    slab = pl.BlockSpec((rows, 1, width), lambda block, at: (block, 0, 0))
-    shape_c = jax.ShapeDtypeStruct((width, 1, width), F32)
-    cross_out = pl.pallas_call(
-        cross_kernel,
-        grid_spec=pltpu.PrefetchScalarGridSpec(
-            num_scalar_prefetch=1,
-            grid=(blocks + 1,),
-            in_specs=[piece, piece, pl.BlockSpec((1, 8, wide), lambda block, at: (0, 0, 0)), slab, slab, slab],
-            out_specs=(slab, slab, slab, slab, pl.BlockSpec((rows, width), lambda block, at: (block, 0))),
-        ),
-        out_shape=(shape_c,) * 4 + (jax.ShapeDtypeStruct((width, width), BF16),),
-        compiler_params=params(48),
-        name="cross",
-    )(
-        place.reshape(1), chunk, partner, side,
-        cross_weight.transpose(1, 0, 2), cross_first.transpose(1, 0, 2), cross_second.transpose(1, 0, 2),
-    )
+    cross_out = update_cross(1, across, across_core, cross_out)
     cross_grad, cross_one, cross_two, cross_new = (x.transpose(1, 0, 2) for x in cross_out[:4])
     loss_sum = rest[14, 1]
     return (

time: 271 us -> 256 us (0.945)
  waiting for transfers between devices: 79.7 us -> 59.7 us
  starting transfers between devices: 51.9 us -> 57.4 us
  local copies, waits for them, and re-layouts: 12.4 us -> 17.6 us
  Pallas kernels: 110 us -> 106 us
    ppermute x33 -> x35, waiting for transfers between devices: 70 us -> 50.2 us  [flip(): return lax.ppermute(x, axis, [(i, i ^ bit) for i in range(size)])]
    ppermute x33 -> x35, starting transfers between devices: 40.9 us -> 45.5 us  [flip(): return lax.ppermute(x, axis, [(i, i ^ bit) for i in range(size)])]
    pallas_call x1 -> x2, Pallas kernels: 22 us -> 17.9 us  [update_cross(): pl.pallas_call(functools.partial(cross_kernel, other, blocks), grid_spec=...]
    unnamed x48 -> x56, local copies, waits for them, and re-layouts: 6.18 us -> 9.45 us
  transfers between devices with their start and end apart: 36 -> 39, of which waited for: 16 -> 14; matrix products, arithmetic and copies ran while one was open for 6% -> 7% of each run, Pallas kernels for 13% -> 18%
where the time goes in v4:
time: 256 us; the launch traced here: 255 us
  Pallas kernels  106 us (41%)
  waiting for transfers between devices  59.7 us (23%)
  starting transfers between devices  57.4 us (22%)
  local copies, waits for them, and re-layouts  17.6 us (7%)
  other arithmetic  13.3 us (5%)
    ppermute x35, waiting for transfers between devices, flip(): return lax.ppermute(x, axis, [(i, i ^ bit) for i in range(size)])  50.2 us
    ppermute x35, starting transfers between devices, flip(): return lax.ppermute(x, axis, [(i, i ^ bit) for i in range(size)])  45.5 us
    pallas_call x1, Pallas kernels, local(): pl.pallas_call(towers_kernel, out_shape=(low, low, low, low_deep, low, ja...  18.1 us
    pallas_call x2, Pallas kernels, update_cross(): pl.pallas_call(functools.partial(cross_kernel, other, blocks), grid_spec=...  17.9 us
    pallas_call x1, Pallas kernels, local(): pl.pallas_call(functools.partial(inputs_kernel, feats, stride, groups, em...  17.6 us
    pallas_call x1, Pallas kernels, local(): pl.pallas_call(functools.partial(send_kernel, feats, slots, stride, embed...  16.6 us
    all_to_all x3, starting transfers between devices, in_plane(): lax.all_to_all(x, ('tower', 'batch'), split_axis=0, concat_axis=0, axis_i...  11.1 us
    pallas_call x1, Pallas kernels, local(): pl.pallas_call(functools.partial(grads_kernel, deep_rows), out_shape=(par...  10.4 us
  transfers between devices with their start and end apart: 39, of which 14 were waited for; matrix products, arithmetic and copies ran while one was open for 7% of the time, Pallas kernels for 18%

profile of v4, /device:TPU:0, one launch (start us, length us, event | category | flops | bytes accessed | tf_op | source)
XLA Modules:
  0.0 255.4 jit_solution(4414790472221115082)
XLA Ops:
  2.6 7.2 %slots.1 = (s32[32,512]{1,0:T(8,128)S(1)}, s32[104,128]{1,0:T(8,128)S(1)}, bf16[40,2048]{1,0:T(8,128)(2,1)S(1)}) custom-call(s32[26,512]{1,0:T(8,128)S(1)} %dynamic-slice_bitcast_fusion.ids_ref, s32[1,512]{1,0:T(1,128)S(1)} %bitcast.108, f32[39,2048]{1,0:T(8,128)S(1)} %bitcast.102), custom_call_target="tpu_custom_call" | custom-call | tf_op jit(solution)/shard_map/slots/pallas_call | solution.py:616
  9.8 5.1 %collective-permute-start.2 = (bf16[40,2048]{1,0:T(8,128)(2,1)S(1)}, bf16[40,2048]{1,0:T(8,128)(2,1)S(1)}, u32[]{:S(2)}, u32[]{:S(2)}) collective-permute-start(bf16[40,2048]{1,0:T(8,128)(2,1)S(1)} %get-tuple-element.116.refs_0_), channel_id=1, source_target_pairs={{0,12},{1,13},{2,14},{3,15},{4,8},{5,9},{6,10},{7,11},{8,4},{9,5},... | collective-permute-start | bytes 491528 | tf_op jit(solution)/shard_map/ppermute | solution.py:548
  17.2 3.9 %all-to-all-start = ((s32[8,4,512]{2,1,0:T(4,128)}), s32[8,4,512]{2,1,0:T(4,128)S(1)}, u32[]{:S(2)}, u32[]{:S(2)}) async-start(s32[8,4,512]{2,1,0:T(4,128)} %all_to_all.24), calls=%async_computation | async-start | bytes 131072 | tf_op jit(solution)/shard_map/all_to_all | solution.py:632
  24.7 2.6 %copy.48 = bf16[1,1027,1027]{2,1,0:T(8,128)(2,1)S(1)} copy(f32[1,1027,1027]{2,0,1:T(1,128)} %param.23) | data formatting | bytes 6328374 | tf_op args[7]
  32.4 10.0 %lookup.1 = bf16[4608,128]{1,0:T(8,128)(2,1)} custom-call(s32[4]{0:T(128)S(1)} %pad_add_fusion.1.spot_ref, s32[32,512]{1,0:T(8,128)S(1)} %all_to_all.26.ids_ref, bf16[40,2048]{1,0:T(8,128)(2,1)S(1)} %get-tuple-element.116.refs_0_, bf16[40,2048]{1,0:T(8,128)(2,1)S(1)} %collective-permute-done.refs_1_, bf16[40,2048]{1,0:T(8,128)(2,1)S(1)} %collective-permute-done.1.refs_2_, ...), custom_call_target="tpu_custom_call" | custom-call | tf_op jit(solution)/shard_map/lookup/pallas_call | solution.py:649
  42.4 3.7 %all-to-all-start.1 = ((bf16[8,576,128]{2,1,0:T(8,128)(2,1)}), bf16[8,576,128]{2,1,0:T(8,128)(2,1)S(1)}, u32[]{:S(2)}, u32[]{:S(2)}) async-start(bf16[8,576,128]{2,1,0:T(8,128)(2,1)} %bitcast.9), calls=%async_computation.1 | async-start | bytes 2359296 | tf_op jit(solution)/shard_map/all_to_all | solution.py:632
  50.7 4.2 %collective-permute-done.7 = bf16[2,32,1152]{2,1,0:T(8,128)(2,1)S(1)} collective-permute-done((bf16[2,32,1152]{2,1,0:T(8,128)(2,1)S(1)}, bf16[2,32,1152]{2,1,0:T(8,128)(2,1)S(1)}, u32[]{:S(2)}, u32[]{:S(2)}) %collective-permute-start.7) | collective-permute-done | bytes 147488 | tf_op jit(solution)/shard_map/ppermute | solution.py:548
  54.9 6.1 %collective-permute-done.6 = bf16[2,32,1152]{2,1,0:T(8,128)(2,1)S(1)} collective-permute-done((bf16[2,32,1152]{2,1,0:T(8,128)(2,1)S(1)}, bf16[2,32,1152]{2,1,0:T(8,128)(2,1)S(1)}, u32[]{:S(2)}, u32[]{:S(2)}) %collective-permute-start.6) | collective-permute-done | bytes 147488 | tf_op jit(solution)/shard_map/ppermute | solution.py:548
  61.2 9.5 %all-to-all-done.1 = bf16[8,576,128]{2,1,0:T(8,128)(2,1)S(1)} async-done(((bf16[8,576,128]{2,1,0:T(8,128)(2,1)}), bf16[8,576,128]{2,1,0:T(8,128)(2,1)S(1)}, u32[]{:S(2)}, u32[]{:S(2)}) %all-to-all-start.1) | async-done | bytes 1179680 | tf_op jit(solution)/shard_map/all_to_all | solution.py:632
  72.7 17.6 %inputs.1 = (bf16[512,1152]{1,0:T(8,128)(2,1)S(1)}, f32[1,1]{1,0:T(1,128)}) custom-call(s32[13312]{0:T(1024)S(1)} %bitcast.106, bf16[4608,128]{1,0:T(8,128)(2,1)S(1)} %bitcast.101, bf16[512,128]{1,0:T(8,128)(2,1)S(1)} %pad.38.dense_ref), custom_call_target="tpu_custom_call" | custom-call | tf_op jit(solution)/shard_map/inputs/pallas_call | solution.py:678
  94.7 18.1 %towers.1 = (bf16[512,1152]{1,0:T(8,128)(2,1)}, bf16[512,1152]{1,0:T(8,128)(2,1)}, bf16[512,1152]{1,0:T(8,128)(2,1)}, bf16[512,1024]{1,0:T(8,128)(2,1)}, bf16[512,1152]{1,0:T(8,128)(2,1)}, /*index=5*/f32[8,1152]{1,0:T(8,128)}) custom-call(s32[4]{0:T(128)} %copy-done.8, f32[1,1]{1,0:T(1,128)} %get-tuple-element.130.count_ref, f32[1,1]{1,0:T(1,128)} %bitcast.18.bias_ref, ...), custom_call_target="tpu_custom_call" | custom-call | tf_op jit(solution)/shard_map/towers/pallas_call | solution.py:697
  112.8 10.4 %grads.1 = (bf16[2,2,2,2,96,1024]{5,4,3,2,1,0:T(8,128)(2,1)}, bf16[2,2,2,2,96,1024]{5,4,3,2,1,0:T(8,128)(2,1)}, f32[24,1152]{1,0:T(8,128)}) custom-call(s32[4]{0:T(128)} %copy-done.8, bf16[512,1152]{1,0:T(8,128)(2,1)} %copy-done.2, bf16[512,1152]{1,0:T(8,128)(2,1)} %get-tuple-element.135.one_ref, bf16[512,1152]{1,0:T(8,128)(2,1)} %get-tuple-element.136.d_second_ref, ...), custom_call_target="tpu_custom_call" | custom-call | tf_op jit(solution)/shard_map/grads/pallas_call | solution.py:720
  123.7 5.5 %collective-permute-done.13 = f32[24,1152]{1,0:T(8,128)S(1)} collective-permute-done((f32[24,1152]{1,0:T(8,128)}, f32[24,1152]{1,0:T(8,128)S(1)}, u32[]{:S(2)}, u32[]{:S(2)}) %collective-permute-start.13) | collective-permute-done | bytes 110624 | tf_op jit(solution)/shard_map/ppermute | solution.py:548
  139.1 16.6 %send.1 = bf16[4608,128]{1,0:T(8,128)(2,1)} custom-call(s32[13312]{0:T(1024)S(1)} %bitcast.107, bf16[512,1152]{1,0:T(8,128)(2,1)S(1)} %copy-done.5), custom_call_target="tpu_custom_call" | custom-call | tf_op jit(solution)/shard_map/send/pallas_call | solution.py:744
  157.6 3.6 %all-to-all-start.2 = ((bf16[8,576,128]{2,1,0:T(8,128)(2,1)}), bf16[8,576,128]{2,1,0:T(8,128)(2,1)S(1)}, u32[]{:S(2)}, u32[]{:S(2)}) async-start(bf16[8,576,128]{2,1,0:T(8,128)(2,1)} %bitcast.26), calls=%async_computation.2 | async-start | bytes 2359296 | tf_op jit(solution)/shard_map/all_to_all | solution.py:632
  170.7 14.6 %collective-permute-done.19 = bf16[2,96,1024]{2,1,0:T(8,128)(2,1)S(1)} collective-permute-done((bf16[2,96,1024]{2,1,0:T(8,128)(2,1)S(1)}, bf16[2,96,1024]{2,1,0:T(8,128)(2,1)S(1)}, u32[]{:S(2)}, u32[]{:S(2)}) %collective-permute-start.19) | collective-permute-done | bytes 393248 | tf_op jit(solution)/shard_map/ppermute | solution.py:548
  188.6 3.0 %collective-permute-start.25 = (bf16[96,1024]{1,0:T(8,128)(2,1)S(1)}, bf16[96,1024]{1,0:T(8,128)(2,1)S(1)}, u32[]{:S(2)}, u32[]{:S(2)}) collective-permute-start(bf16[96,1024]{1,0:T(8,128)(2,1)S(1)} %get-tuple-element.159), channel_id=1, source_target_pairs={{0,8},{1,9},{2,10},{3,11},{4,12},{5,13},{6,14},{7,15},{8,0},{9,1},... | collective-permute-start | bytes 589832 | tf_op jit(solution)/shard_map/ppermute | solution.py:548
  193.0 7.0 %table.1 = (f32[320,256]{1,0:T(8,128)S(1)}, bf16[3,320,256]{2,1,0:T(8,128)(2,1)S(1)}) custom-call(s32[4]{0:T(128)S(1)} %copy-done.9, s32[32,512]{1,0:T(8,128)S(1)} %all_to_all.26.ids_ref, bf16[4608,128]{1,0:T(8,128)(2,1)S(1)} %bitcast.100), custom_call_target="tpu_custom_call" | custom-call | tf_op jit(solution)/shard_map/table/pallas_call | solution.py:771
  202.2 3.6 %collective-permute-done.25 = bf16[96,1024]{1,0:T(8,128)(2,1)S(1)} collective-permute-done((bf16[96,1024]{1,0:T(8,128)(2,1)S(1)}, bf16[96,1024]{1,0:T(8,128)(2,1)S(1)}, u32[]{:S(2)}, u32[]{:S(2)}) %collective-permute-start.25) | collective-permute-done | bytes 196640 | tf_op jit(solution)/shard_map/ppermute | solution.py:548
  207.0 3.6 %collective-permute-start.27 = (bf16[64,1024]{1,0:T(8,128)(2,1)S(1)}, bf16[64,1024]{1,0:T(8,128)(2,1)S(1)}, u32[]{:S(2)}, u32[]{:S(2)}) collective-permute-start(bf16[64,1024]{1,0:T(8,128)(2,1)S(1)} %slice.244), channel_id=1, source_target_pairs={{0,4},{1,5},{2,6},{3,7},{4,0},{5,1},{6,2},{7,3},{8,12},{9,13},{10,... | collective-permute-start | bytes 393224 | tf_op jit(solution)/shard_map/ppermute | solution.py:548
  214.9 7.5 %collective-permute-done.28 = bf16[64,1024]{1,0:T(8,128)(2,1)S(1)} collective-permute-done((bf16[64,1024]{1,0:T(8,128)(2,1)S(1)}, bf16[64,1024]{1,0:T(8,128)(2,1)S(1)}, u32[]{:S(2)}, u32[]{:S(2)}) %collective-permute-start.28) | collective-permute-done | bytes 131104 | tf_op jit(solution)/shard_map/ppermute | solution.py:548
  230.6 9.0 %cross.1 = (f32[1027,1,1027]{2,1,0:T(1,128)}, f32[1027,1,1027]{2,1,0:T(1,128)}, f32[1027,1,1027]{2,1,0:T(1,128)}, f32[1027,1,1027]{2,1,0:T(1,128)}, bf16[1027,1027]{1,0:T(8,128)(2,1)}) custom-call(s32[1]{0:T(128)} %bitcast.30.place_ref, bf16[4,64,1024]{2,1,0:T(8,128)(2,1)} %copy-done.13, bf16[4,64,1024]{2,1,0:T(8,128)(2,1)} %copy-done.18, ...), custom_call_target="tpu_custom_call" | custom-call | tf_op jit(solution)/shard_map/cross/pallas_call | solution.py:812
  239.6 4.0 %collective-permute-done.33.refs_5_ = bf16[320,256]{1,0:T(8,128)(2,1)S(1)} collective-permute-done((bf16[320,256]{1,0:T(8,128)(2,1)S(1)}, bf16[320,256]{1,0:T(8,128)(2,1)S(1)}, u32[]{:S(2)}, u32[]{:S(2)}) %collective-permute-start.33) | collective-permute-done | bytes 163872 | tf_op jit(solution)/shard_map/ppermute | solution.py:548
  246.3 8.9 %cross_other.1 = (f32[1027,1,1027]{2,1,0:T(1,128)}, f32[1027,1,1027]{2,1,0:T(1,128)}, f32[1027,1,1027]{2,1,0:T(1,128)}, f32[1027,1,1027]{2,1,0:T(1,128)}, bf16[1027,1027]{1,0:T(8,128)(2,1)}) custom-call(s32[1]{0:T(128)} %bitcast.30.place_ref, ...), custom_call_target="tpu_custom_call", output_to_operand_aliasing={{0}: (7, {}), {1}: (8, {}), {2}: (9, {}), {3}: (10, {}), {4... | custom-call | tf_op jit(solution)/shard_map/cross_other/pallas_call | solution.py:812
  (184 shorter events, 68.6 us)
Async XLA Ops:
  9.8 17.8 %collective-permute-start.2 = (bf16[40,2048]{1,0:T(8,128)(2,1)S(1)}, bf16[40,2048]{1,0:T(8,128)(2,1)S(1)}, u32[]{:S(2)}, u32[]{:S(2)}) collective-permute-start(bf16[40,2048]{1,0:T(8,128)(2,1)S(1)} %get-tuple-element.116.refs_0_), channel_id=1, source_target_pairs={{0,12},{1,13},{2,14},{3,15},{4,8},{5,9},{6,10},{7,11},{8,4},{9,5},... | collective-permute-start | bytes 491528 | tf_op jit(solution)/shard_map/ppermute | solution.py:548
  14.9 13.9 %collective-permute-start.1 = (bf16[40,2048]{1,0:T(8,128)(2,1)S(1)}, bf16[40,2048]{1,0:T(8,128)(2,1)S(1)}, u32[]{:S(2)}, u32[]{:S(2)}) collective-permute-start(bf16[40,2048]{1,0:T(8,128)(2,1)S(1)} %get-tuple-element.116.refs_0_), channel_id=1, source_target_pairs={{0,8},{1,9},{2,10},{3,11},{4,12},{5,13},{6,14},{7,15},{8,0},{9,1},... | collective-permute-start | bytes 491528 | tf_op jit(solution)/shard_map/ppermute | solution.py:548
  14.9 13.9 %collective-permute-start = (bf16[40,2048]{1,0:T(8,128)(2,1)S(1)}, bf16[40,2048]{1,0:T(8,128)(2,1)S(1)}, u32[]{:S(2)}, u32[]{:S(2)}) collective-permute-start(bf16[40,2048]{1,0:T(8,128)(2,1)S(1)} %get-tuple-element.116.refs_0_), channel_id=1, source_target_pairs={{0,4},{1,5},{2,6},{3,7},{4,0},{5,1},{6,2},{7,3},{8,12},{9,13},{10,... | collective-permute-start | bytes 491528 | tf_op jit(solution)/shard_map/ppermute | solution.py:548
  21.0 25.1 %collective-permute-start.4 = (bf16[32,1152]{1,0:T(8,128)(2,1)S(1)}, bf16[32,1152]{1,0:T(8,128)(2,1)S(1)}, u32[]{:S(2)}, u32[]{:S(2)}) collective-permute-start(bf16[32,1152]{1,0:T(8,128)(2,1)S(1)} %pad.32), channel_id=1, source_target_pairs={{0,16},{16,0},{1,17},{17,1},{2,18},{18,2},{3,19},{19,3},{4,20},{20... | collective-permute-start | bytes 221192 | tf_op jit(solution)/shard_map/ppermute | solution.py:548
  29.9 40.8 %collective-permute-start.3 = (bf16[528,1152]{1,0:T(8,128)(2,1)}, bf16[528,1152]{1,0:T(8,128)(2,1)}, u32[]{:S(2)}, u32[]{:S(2)}) collective-permute-start(bf16[528,1152]{1,0:T(8,128)(2,1)} %constant_dynamic-slice_fusion.5), channel_id=1, source_target_pairs={{0,16},{16,0},{1,17},{17,1},{2,18},{18,2},{3,19},{19,3},{4,20},{20... | collective-permute-start | bytes 3649544 | tf_op jit(solution)/shard_map/ppermute | solution.py:548
  42.4 28.3 %all-to-all-start.1 = ((bf16[8,576,128]{2,1,0:T(8,128)(2,1)}), bf16[8,576,128]{2,1,0:T(8,128)(2,1)S(1)}, u32[]{:S(2)}, u32[]{:S(2)}) async-start(bf16[8,576,128]{2,1,0:T(8,128)(2,1)} %bitcast.9), calls=%async_computation.1 | async-start | bytes 2359296 | tf_op jit(solution)/shard_map/all_to_all | solution.py:632
  70.7 22.7 %collective-permute-start.9 = (bf16[528,1152]{1,0:T(8,128)(2,1)}, bf16[528,1152]{1,0:T(8,128)(2,1)S(1)}, u32[]{:S(2)}, u32[]{:S(2)}) collective-permute-start(bf16[528,1152]{1,0:T(8,128)(2,1)} %collective-permute-done.3.half_ref), channel_id=1, source_target_pairs={{0,1},{1,0},{2,3},{3,2},{4,5},{5,4},{6,7},{7,6},{8,9},{9,8},{10,11... | collective-permute-start | bytes 3649544 | tf_op jit(solution)/shard_map/ppermute | solution.py:548
  70.7 20.5 %collective-permute-start.8 = (bf16[4,2,32,1152]{3,2,1,0:T(8,128)(2,1)S(1)}, bf16[4,2,32,1152]{3,2,1,0:T(8,128)(2,1)}, u32[]{:S(2)}, u32[]{:S(2)}) collective-permute-start(bf16[4,2,32,1152]{3,2,1,0:T(8,128)(2,1)S(1)} %pad_maximum_fusion.1.here_ref), channel_id=1, source_target_pairs={{0,2},{1,3},{2,0},{3,1},{4,6},{5,7},{6,4},{7,5},{8,10},{9,11},{10,... | collective-permute-start | bytes 1769480 | tf_op jit(solution)/shard_map/ppermute | solution.py:548
  72.4 20.4 %collective-permute-start.10 = (bf16[4,2,32,1152]{3,2,1,0:T(8,128)(2,1)S(1)}, bf16[4,2,32,1152]{3,2,1,0:T(8,128)(2,1)S(1)}, u32[]{:S(2)}, u32[]{:S(2)}) collective-permute-start(bf16[4,2,32,1152]{3,2,1,0:T(8,128)(2,1)S(1)} %pad_maximum_fusion.1.here_ref), channel_id=1, source_target_pairs={{0,1},{1,0},{2,3},{3,2},{4,5},{5,4},{6,7},{7,6},{8,9},{9,8},{10,11... | collective-permute-start | bytes 1769480 | tf_op jit(solution)/shard_map/ppermute | solution.py:548
  133.4 24.1 %collective-permute-start.14 = (bf16[2,2,96,1024]{3,2,1,0:T(8,128)(2,1)S(1)}, bf16[2,2,96,1024]{3,2,1,0:T(8,128)(2,1)S(1)}, u32[]{:S(2)}, u32[]{:S(2)}) collective-permute-start(bf16[2,2,96,1024]{3,2,1,0:T(8,128)(2,1)S(1)} %get-tuple-element.144), channel_id=1, source_target_pairs={{0,16},{16,0},{1,17},{17,1},{2,18},{18,2},{3,19},{19,3},{4,20},{20... | collective-permute-start | bytes 2359304 | tf_op jit(solution)/shard_map/ppermute | solution.py:548
  134.9 22.7 %collective-permute-start.15 = (bf16[2,2,96,1024]{3,2,1,0:T(8,128)(2,1)S(1)}, bf16[2,2,96,1024]{3,2,1,0:T(8,128)(2,1)S(1)}, u32[]{:S(2)}, u32[]{:S(2)}) collective-permute-start(bf16[2,2,96,1024]{3,2,1,0:T(8,128)(2,1)S(1)} %get-tuple-element.145), channel_id=1, source_target_pairs={{0,2},{1,3},{2,0},{3,1},{4,6},{5,7},{6,4},{7,5},{8,10},{9,11},{10,... | collective-permute-start | bytes 2359304 | tf_op jit(solution)/shard_map/ppermute | solution.py:548
  135.5 22.1 %collective-permute-start.17 = (f32[16,1152]{1,0:T(8,128)S(1)}, f32[16,1152]{1,0:T(8,128)S(1)}, u32[]{:S(2)}, u32[]{:S(2)}) collective-permute-start(f32[16,1152]{1,0:T(8,128)S(1)} %slice.145), channel_id=1, source_target_pairs={{0,2},{1,3},{2,0},{3,1},{4,6},{5,7},{6,4},{7,5},{8,10},{9,11},{10,... | collective-permute-start | bytes 221192 | tf_op jit(solution)/shard_map/ppermute | solution.py:548
  137.1 20.5 %collective-permute-start.18 = (f32[16,1152]{1,0:T(8,128)S(1)}, f32[16,1152]{1,0:T(8,128)S(1)}, u32[]{:S(2)}, u32[]{:S(2)}) collective-permute-start(f32[16,1152]{1,0:T(8,128)S(1)} %pad_maximum_fusion.4), channel_id=1, source_target_pairs={{0,18},{1,19},{2,16},{3,17},{4,22},{5,23},{6,20},{7,21},{8,26},{9,... | collective-permute-start | bytes 221192 | tf_op jit(solution)/shard_map/ppermute | solution.py:742
  137.8 19.8 %collective-permute-start.16 = (f32[16,1152]{1,0:T(8,128)S(1)}, f32[16,1152]{1,0:T(8,128)S(1)}, u32[]{:S(2)}, u32[]{:S(2)}) collective-permute-start(f32[16,1152]{1,0:T(8,128)S(1)} %pad_maximum_fusion.4), channel_id=1, source_target_pairs={{0,16},{16,0},{1,17},{17,1},{2,18},{18,2},{3,19},{19,3},{4,20},{20... | collective-permute-start | bytes 221192 | tf_op jit(solution)/shard_map/ppermute | solution.py:548
  157.6 27.9 %all-to-all-start.2 = ((bf16[8,576,128]{2,1,0:T(8,128)(2,1)}), bf16[8,576,128]{2,1,0:T(8,128)(2,1)S(1)}, u32[]{:S(2)}, u32[]{:S(2)}) async-start(bf16[8,576,128]{2,1,0:T(8,128)(2,1)} %bitcast.26), calls=%async_computation.2 | async-start | bytes 2359296 | tf_op jit(solution)/shard_map/all_to_all | solution.py:632
  167.1 18.3 %collective-permute-start.19 = (bf16[2,96,1024]{2,1,0:T(8,128)(2,1)S(1)}, bf16[2,96,1024]{2,1,0:T(8,128)(2,1)S(1)}, u32[]{:S(2)}, u32[]{:S(2)}) collective-permute-start(bf16[2,96,1024]{2,1,0:T(8,128)(2,1)S(1)} %get-tuple-element.150), channel_id=1, source_target_pairs={{0,2},{1,3},{2,0},{3,1},{4,6},{5,7},{6,4},{7,5},{8,10},{9,11},{10,... | collective-permute-start | bytes 1179656 | tf_op jit(solution)/shard_map/ppermute | solution.py:548
  169.0 16.5 %collective-permute-start.20 = (bf16[2,96,1024]{2,1,0:T(8,128)(2,1)S(1)}, bf16[2,96,1024]{2,1,0:T(8,128)(2,1)}, u32[]{:S(2)}, u32[]{:S(2)}) collective-permute-start(bf16[2,96,1024]{2,1,0:T(8,128)(2,1)S(1)} %get-tuple-element.151), channel_id=1, source_target_pairs={{0,16},{16,0},{1,17},{17,1},{2,18},{18,2},{3,19},{19,3},{4,20},{20... | collective-permute-start | bytes 1179656 | tf_op jit(solution)/shard_map/ppermute | solution.py:548
  188.6 13.6 %collective-permute-start.24 = (bf16[96,1024]{1,0:T(8,128)(2,1)}, bf16[96,1024]{1,0:T(8,128)(2,1)S(1)}, u32[]{:S(2)}, u32[]{:S(2)}) collective-permute-start(bf16[96,1024]{1,0:T(8,128)(2,1)} %get-tuple-element.158), channel_id=1, source_target_pairs={{0,4},{1,5},{2,6},{3,7},{4,0},{5,1},{6,2},{7,3},{8,12},{9,13},{10,... | collective-permute-start | bytes 589832 | tf_op jit(solution)/shard_map/ppermute | solution.py:548
  188.6 17.3 %collective-permute-start.25 = (bf16[96,1024]{1,0:T(8,128)(2,1)S(1)}, bf16[96,1024]{1,0:T(8,128)(2,1)S(1)}, u32[]{:S(2)}, u32[]{:S(2)}) collective-permute-start(bf16[96,1024]{1,0:T(8,128)(2,1)S(1)} %get-tuple-element.159), channel_id=1, source_target_pairs={{0,8},{1,9},{2,10},{3,11},{4,12},{5,13},{6,14},{7,15},{8,0},{9,1},... | collective-permute-start | bytes 589832 | tf_op jit(solution)/shard_map/ppermute | solution.py:548
  191.7 14.2 %collective-permute-start.26 = (bf16[96,1024]{1,0:T(8,128)(2,1)S(1)}, bf16[96,1024]{1,0:T(8,128)(2,1)}, u32[]{:S(2)}, u32[]{:S(2)}) collective-permute-start(bf16[96,1024]{1,0:T(8,128)(2,1)S(1)} %get-tuple-element.160), channel_id=1, source_target_pairs={{0,12},{1,13},{2,14},{3,15},{4,8},{5,9},{6,10},{7,11},{8,4},{9,5},... | collective-permute-start | bytes 589832 | tf_op jit(solution)/shard_map/ppermute | solution.py:548
  222.5 21.0 %collective-permute-start.31 = (bf16[4,64,1024]{2,1,0:T(8,128)(2,1)S(1)}, bf16[4,64,1024]{2,1,0:T(8,128)(2,1)S(1)}, u32[]{:S(2)}, u32[]{:S(2)}) collective-permute-start(bf16[4,64,1024]{2,1,0:T(8,128)(2,1)S(1)} %pad_maximum_fusion.2.near_ref), channel_id=1, source_target_pairs={{0,2},{1,3},{2,0},{3,1},{4,6},{5,7},{6,4},{7,5},{8,10},{9,11},{10,... | collective-permute-start | bytes 1572872 | tf_op jit(solution)/shard_map/ppermute | solution.py:548
  224.8 14.8 %collective-permute-start.34 = (bf16[320,256]{1,0:T(8,128)(2,1)}, bf16[320,256]{1,0:T(8,128)(2,1)S(1)}, u32[]{:S(2)}, u32[]{:S(2)}) collective-permute-start(bf16[320,256]{1,0:T(8,128)(2,1)} %get-tuple-element.230), channel_id=1, source_target_pairs={{0,12},{1,13},{2,14},{3,15},{4,8},{5,9},{6,10},{7,11},{8,4},{9,5},... | collective-permute-start | bytes 491528 | tf_op jit(solution)/shard_map/ppermute | solution.py:548
  226.7 16.9 %collective-permute-start.33 = (bf16[320,256]{1,0:T(8,128)(2,1)S(1)}, bf16[320,256]{1,0:T(8,128)(2,1)S(1)}, u32[]{:S(2)}, u32[]{:S(2)}) collective-permute-start(bf16[320,256]{1,0:T(8,128)(2,1)S(1)} %get-tuple-element.231), channel_id=1, source_target_pairs={{0,8},{1,9},{2,10},{3,11},{4,12},{5,13},{6,14},{7,15},{8,0},{9,1},... | collective-permute-start | bytes 491528 | tf_op jit(solution)/shard_map/ppermute | solution.py:548
  228.2 15.3 %collective-permute-start.32 = (bf16[320,256]{1,0:T(8,128)(2,1)S(1)}, bf16[320,256]{1,0:T(8,128)(2,1)S(1)}, u32[]{:S(2)}, u32[]{:S(2)}) collective-permute-start(bf16[320,256]{1,0:T(8,128)(2,1)S(1)} %get-tuple-element.232), channel_id=1, source_target_pairs={{0,4},{1,5},{2,6},{3,7},{4,0},{5,1},{6,2},{7,3},{8,12},{9,13},{10,... | collective-permute-start | bytes 491528 | tf_op jit(solution)/shard_map/ppermute | solution.py:548
  (42 other events, 474.2 us)

commit v5 on v4

--- a/solution.py
+++ b/solution.py
@@ -755,19 +755,18 @@
         name="send",
     )(slot, d_inputs)
     from_one, rest, sent = lax.optimization_barrier((from_one, rest, sent))
-    back = in_plane(sent)
     to_two = lax.optimization_barrier([keep[k, 0, 1] + got[k, 0, 1] + from_one[k][1] for k in range(2)])
     from_two = [by_near(to_two[0]), by_tower(to_two[1])]
     by_far = [flip(rest, "batch", k * 4, batch) for k in range(1, 4)]
     rest = (rest + by_far[0]) + (by_far[1] + by_far[2])
     for bit in [16 << k for k in range(groups.bit_length() - 3)]:
         rest = rest + flip(rest, "batch", bit, batch)
-    from_two, rest, back = lax.optimization_barrier((from_two, rest, back))
+    from_two, rest, sent = lax.optimization_barrier((from_two, rest, sent))
+    back = in_plane(sent)
     blocks_t = (rows_own // 256 * tall, 256)
     both = [keep[k, 0, 0] + got[k, 0, 0] + from_one[k][0] + from_two[k] for k in range(2)]
     both = lax.optimization_barrier([part[k] for part in both for k in range(groups // 2)])
     from_far = [flip(both[k], "batch", k * 4, batch) for k in range(1, groups)]
-    both, back = lax.optimization_barrier((both, back))
     table_own, table_other = pl.pallas_call(
         functools.partial(table_kernel, embed, slots, stride),
         out_shape=(jax.ShapeDtypeStruct(blocks_t, F32), jax.ShapeDtypeStruct((groups - 1,) + blocks_t, BF16)),
@@ -782,8 +781,8 @@
     )
     vector_one, vector_two, vector_new = adamw(vectors, vector_grad, vector_first, vector_second, 0.03)
     tail = lax.dynamic_slice_in_dim(rest[8 : 8 + width - main], (tower * batch + place) * deep_rows, deep_rows, 1).T
-    from_far, table_own, table_other, tail, vector_grad, vector_one, vector_two, vector_new = lax.optimization_barrier(
-        (from_far, table_own, table_other, tail, vector_grad, vector_one, vector_two, vector_new)
+    from_far, tail, vector_grad, vector_one, vector_two, vector_new = lax.optimization_barrier(
+        (from_far, tail, vector_grad, vector_one, vector_two, vector_new)
     )
     summed = both[0].astype(F32)
     for part in from_far:
@@ -792,8 +791,8 @@
     deep_grad = jnp.concatenate([summed[rows_c:], tail], axis=1)
     deep_one, deep_two, deep_new = adamw(deep_weight, deep_grad, deep_first, deep_second, 0.03)
     deep_copy = deep_new.astype(BF16)
-    chunk, deep_grad, deep_one, deep_two, deep_new, deep_copy = lax.optimization_barrier(
-        (chunk, deep_grad, deep_one, deep_two, deep_new, deep_copy)
+    chunk, table_own, table_other, deep_grad, deep_one, deep_two, deep_new, deep_copy = lax.optimization_barrier(
+        (chunk, table_own, table_other, deep_grad, deep_one, deep_two, deep_new, deep_copy)
     )
     across = flip(chunk, "batch", 2, batch)
     side = rest[:8][None]

time: 256 us -> 254 us (level)
  waiting for transfers between devices: 59.7 us -> 62.6 us
    ppermute x35, waiting for transfers between devices: 50.2 us -> 53.1 us  [flip(): return lax.ppermute(x, axis, [(i, i ^ bit) for i in range(size)])]
    unnamed x56 -> x60, local copies, waits for them, and re-layouts: 9.45 us -> 9.48 us
  transfers between devices with their start and end apart: 39 -> 39, of which waited for: 14 -> 16; matrix products, arithmetic and copies ran while one was open for 7% -> 6% of each run, Pallas kernels for 18% -> 15%
where the time goes in v5:
time: 254 us; the launch traced here: 253 us
  Pallas kernels  106 us (42%)
  waiting for transfers between devices  62.6 us (25%)
  starting transfers between devices  55.8 us (22%)
  local copies, waits for them, and re-layouts  16.3 us (6%)
  other arithmetic  11 us (4%)
    ppermute x35, waiting for transfers between devices, flip(): return lax.ppermute(x, axis, [(i, i ^ bit) for i in range(size)])  53.1 us
    ppermute x35, starting transfers between devices, flip(): return lax.ppermute(x, axis, [(i, i ^ bit) for i in range(size)])  43.8 us
    pallas_call x1, Pallas kernels, local(): pl.pallas_call(towers_kernel, out_shape=(low, low, low, low_deep, low, ja...  18 us
    pallas_call x2, Pallas kernels, update_cross(): pl.pallas_call(functools.partial(cross_kernel, other, blocks), grid_spec=...  17.9 us
    pallas_call x1, Pallas kernels, local(): pl.pallas_call(functools.partial(inputs_kernel, feats, stride, groups, em...  17.4 us
    pallas_call x1, Pallas kernels, local(): pl.pallas_call(functools.partial(send_kernel, feats, slots, stride, embed...  16.6 us
    all_to_all x3, starting transfers between devices, in_plane(): lax.all_to_all(x, ('tower', 'batch'), split_axis=0, concat_axis=0, axis_i...  11.3 us
    pallas_call x1, Pallas kernels, local(): pl.pallas_call(functools.partial(grads_kernel, deep_rows), out_shape=(par...  10.4 us
  transfers between devices with their start and end apart: 39, of which 16 were waited for; matrix products, arithmetic and copies ran while one was open for 6% of the time, Pallas kernels for 15%

profile of v5, /device:TPU:0, one launch (start us, length us, event | category | flops | bytes accessed | tf_op | source)
XLA Modules:
  0.0 252.9 jit_solution(12543418337739556676)
XLA Ops:
  2.6 7.2 %slots.1 = (s32[32,512]{1,0:T(8,128)S(1)}, s32[104,128]{1,0:T(8,128)S(1)}, bf16[40,2048]{1,0:T(8,128)(2,1)S(1)}) custom-call(s32[26,512]{1,0:T(8,128)S(1)} %dynamic-slice_bitcast_fusion.ids_ref, s32[1,512]{1,0:T(1,128)S(1)} %bitcast.108, f32[39,2048]{1,0:T(8,128)S(1)} %bitcast.102), custom_call_target="tpu_custom_call" | custom-call | tf_op jit(solution)/shard_map/slots/pallas_call | solution.py:616
  9.8 5.1 %collective-permute-start.2 = (bf16[40,2048]{1,0:T(8,128)(2,1)S(1)}, bf16[40,2048]{1,0:T(8,128)(2,1)S(1)}, u32[]{:S(2)}, u32[]{:S(2)}) collective-permute-start(bf16[40,2048]{1,0:T(8,128)(2,1)S(1)} %get-tuple-element.114.refs_0_), channel_id=1, source_target_pairs={{0,12},{1,13},{2,14},{3,15},{4,8},{5,9},{6,10},{7,11},{8,4},{9,5},... | collective-permute-start | bytes 491528 | tf_op jit(solution)/shard_map/ppermute | solution.py:548
  17.2 3.9 %all-to-all-start = ((s32[8,4,512]{2,1,0:T(4,128)}), s32[8,4,512]{2,1,0:T(4,128)S(1)}, u32[]{:S(2)}, u32[]{:S(2)}) async-start(s32[8,4,512]{2,1,0:T(4,128)} %all_to_all.23), calls=%async_computation | async-start | bytes 131072 | tf_op jit(solution)/shard_map/all_to_all | solution.py:632
  32.4 10.0 %lookup.1 = bf16[4608,128]{1,0:T(8,128)(2,1)} custom-call(s32[4]{0:T(128)S(1)} %pad_add_fusion.1.spot_ref, s32[32,512]{1,0:T(8,128)S(1)} %all_to_all.25.ids_ref, bf16[40,2048]{1,0:T(8,128)(2,1)S(1)} %get-tuple-element.114.refs_0_, bf16[40,2048]{1,0:T(8,128)(2,1)S(1)} %collective-permute-done.refs_1_, bf16[40,2048]{1,0:T(8,128)(2,1)S(1)} %collective-permute-done.1.refs_2_, ...), custom_call_target="tpu_custom_call" | custom-call | tf_op jit(solution)/shard_map/lookup/pallas_call | solution.py:649
  42.4 3.7 %all-to-all-start.1 = ((bf16[8,576,128]{2,1,0:T(8,128)(2,1)}), bf16[8,576,128]{2,1,0:T(8,128)(2,1)S(1)}, u32[]{:S(2)}, u32[]{:S(2)}) async-start(bf16[8,576,128]{2,1,0:T(8,128)(2,1)} %bitcast.9), calls=%async_computation.1 | async-start | bytes 2359296 | tf_op jit(solution)/shard_map/all_to_all | solution.py:632
  50.7 4.2 %collective-permute-done.7 = bf16[2,32,1152]{2,1,0:T(8,128)(2,1)S(1)} collective-permute-done((bf16[2,32,1152]{2,1,0:T(8,128)(2,1)S(1)}, bf16[2,32,1152]{2,1,0:T(8,128)(2,1)S(1)}, u32[]{:S(2)}, u32[]{:S(2)}) %collective-permute-start.7) | collective-permute-done | bytes 147488 | tf_op jit(solution)/shard_map/ppermute | solution.py:548
  54.9 6.1 %collective-permute-done.6 = bf16[2,32,1152]{2,1,0:T(8,128)(2,1)S(1)} collective-permute-done((bf16[2,32,1152]{2,1,0:T(8,128)(2,1)S(1)}, bf16[2,32,1152]{2,1,0:T(8,128)(2,1)S(1)}, u32[]{:S(2)}, u32[]{:S(2)}) %collective-permute-start.6) | collective-permute-done | bytes 147488 | tf_op jit(solution)/shard_map/ppermute | solution.py:548
  61.2 9.5 %all-to-all-done.1 = bf16[8,576,128]{2,1,0:T(8,128)(2,1)S(1)} async-done(((bf16[8,576,128]{2,1,0:T(8,128)(2,1)}), bf16[8,576,128]{2,1,0:T(8,128)(2,1)S(1)}, u32[]{:S(2)}, u32[]{:S(2)}) %all-to-all-start.1) | async-done | bytes 1179680 | tf_op jit(solution)/shard_map/all_to_all | solution.py:632
  72.7 17.4 %inputs.1 = (bf16[512,1152]{1,0:T(8,128)(2,1)S(1)}, f32[1,1]{1,0:T(1,128)}) custom-call(s32[13312]{0:T(1024)S(1)} %bitcast.106, bf16[4608,128]{1,0:T(8,128)(2,1)S(1)} %bitcast.101, bf16[512,128]{1,0:T(8,128)(2,1)S(1)} %pad.38.dense_ref), custom_call_target="tpu_custom_call" | custom-call | tf_op jit(solution)/shard_map/inputs/pallas_call | solution.py:678
  94.6 18.0 %towers.1 = (bf16[512,1152]{1,0:T(8,128)(2,1)}, bf16[512,1152]{1,0:T(8,128)(2,1)}, bf16[512,1152]{1,0:T(8,128)(2,1)}, bf16[512,1024]{1,0:T(8,128)(2,1)}, bf16[512,1152]{1,0:T(8,128)(2,1)}, /*index=5*/f32[8,1152]{1,0:T(8,128)}) custom-call(s32[4]{0:T(128)} %copy-done.8, f32[1,1]{1,0:T(1,128)} %get-tuple-element.128.count_ref, f32[1,1]{1,0:T(1,128)} %bitcast.18.bias_ref, ...), custom_call_target="tpu_custom_call" | custom-call | tf_op jit(solution)/shard_map/towers/pallas_call | solution.py:697
  112.6 10.4 %grads.1 = (bf16[2,2,2,2,96,1024]{5,4,3,2,1,0:T(8,128)(2,1)}, bf16[2,2,2,2,96,1024]{5,4,3,2,1,0:T(8,128)(2,1)}, f32[24,1152]{1,0:T(8,128)}) custom-call(s32[4]{0:T(128)} %copy-done.8, bf16[512,1152]{1,0:T(8,128)(2,1)} %copy-done.2, bf16[512,1152]{1,0:T(8,128)(2,1)} %get-tuple-element.133.one_ref, bf16[512,1152]{1,0:T(8,128)(2,1)} %get-tuple-element.134.d_second_ref, ...), custom_call_target="tpu_custom_call" | custom-call | tf_op jit(solution)/shard_map/grads/pallas_call | solution.py:720
  123.6 5.5 %collective-permute-done.13 = f32[24,1152]{1,0:T(8,128)S(1)} collective-permute-done((f32[24,1152]{1,0:T(8,128)}, f32[24,1152]{1,0:T(8,128)S(1)}, u32[]{:S(2)}, u32[]{:S(2)}) %collective-permute-start.13) | collective-permute-done | bytes 110624 | tf_op jit(solution)/shard_map/ppermute | solution.py:548
  138.9 16.6 %send.1 = bf16[4608,128]{1,0:T(8,128)(2,1)} custom-call(s32[13312]{0:T(1024)S(1)} %bitcast.107, bf16[512,1152]{1,0:T(8,128)(2,1)S(1)} %copy-done.5), custom_call_target="tpu_custom_call" | custom-call | tf_op jit(solution)/shard_map/send/pallas_call | solution.py:744
  166.0 7.0 %collective-permute-done.19 = bf16[2,96,1024]{2,1,0:T(8,128)(2,1)S(1)} collective-permute-done((bf16[2,96,1024]{2,1,0:T(8,128)(2,1)S(1)}, bf16[2,96,1024]{2,1,0:T(8,128)(2,1)S(1)}, u32[]{:S(2)}, u32[]{:S(2)}) %collective-permute-start.19) | collective-permute-done | bytes 393248 | tf_op jit(solution)/shard_map/ppermute | solution.py:548
  175.8 3.7 %all-to-all-start.2 = ((bf16[8,576,128]{2,1,0:T(8,128)(2,1)}), bf16[8,576,128]{2,1,0:T(8,128)(2,1)S(1)}, u32[]{:S(2)}, u32[]{:S(2)}) async-start(bf16[8,576,128]{2,1,0:T(8,128)(2,1)} %bitcast.45), calls=%async_computation.2 | async-start | bytes 2359296 | tf_op jit(solution)/shard_map/all_to_all | solution.py:632
  180.0 2.6 %collective-permute-start.25 = (bf16[96,1024]{1,0:T(8,128)(2,1)S(1)}, bf16[96,1024]{1,0:T(8,128)(2,1)S(1)}, u32[]{:S(2)}, u32[]{:S(2)}) collective-permute-start(bf16[96,1024]{1,0:T(8,128)(2,1)S(1)} %get-tuple-element.157), channel_id=1, source_target_pairs={{0,8},{1,9},{2,10},{3,11},{4,12},{5,13},{6,14},{7,15},{8,0},{9,1},... | collective-permute-start | bytes 589832 | tf_op jit(solution)/shard_map/ppermute | solution.py:548
  185.5 5.0 %collective-permute-done.24 = bf16[96,1024]{1,0:T(8,128)(2,1)S(1)} collective-permute-done((bf16[96,1024]{1,0:T(8,128)(2,1)S(1)}, bf16[96,1024]{1,0:T(8,128)(2,1)S(1)}, u32[]{:S(2)}, u32[]{:S(2)}) %collective-permute-start.24) | collective-permute-done | bytes 196640 | tf_op jit(solution)/shard_map/ppermute | solution.py:548
  190.5 6.6 %collective-permute-done.25 = bf16[96,1024]{1,0:T(8,128)(2,1)S(1)} collective-permute-done((bf16[96,1024]{1,0:T(8,128)(2,1)S(1)}, bf16[96,1024]{1,0:T(8,128)(2,1)S(1)}, u32[]{:S(2)}, u32[]{:S(2)}) %collective-permute-start.25) | collective-permute-done | bytes 196640 | tf_op jit(solution)/shard_map/ppermute | solution.py:548
  197.3 4.1 %collective-permute-start.27 = (bf16[64,1024]{1,0:T(8,128)(2,1)S(1)}, bf16[64,1024]{1,0:T(8,128)(2,1)S(1)}, u32[]{:S(2)}, u32[]{:S(2)}) collective-permute-start(bf16[64,1024]{1,0:T(8,128)(2,1)S(1)} %slice.244), channel_id=1, source_target_pairs={{0,4},{1,5},{2,6},{3,7},{4,0},{5,1},{6,2},{7,3},{8,12},{9,13},{10,... | collective-permute-start | bytes 393224 | tf_op jit(solution)/shard_map/ppermute | solution.py:548
  205.5 8.2 %collective-permute-done.28 = bf16[64,1024]{1,0:T(8,128)(2,1)S(1)} collective-permute-done((bf16[64,1024]{1,0:T(8,128)(2,1)S(1)}, bf16[64,1024]{1,0:T(8,128)(2,1)S(1)}, u32[]{:S(2)}, u32[]{:S(2)}) %collective-permute-start.28) | collective-permute-done | bytes 131104 | tf_op jit(solution)/shard_map/ppermute | solution.py:548
  213.9 7.0 %table.1 = (f32[320,256]{1,0:T(8,128)S(1)}, bf16[3,320,256]{2,1,0:T(8,128)(2,1)S(1)}) custom-call(s32[4]{0:T(128)S(1)} %copy-done.9, s32[32,512]{1,0:T(8,128)S(1)} %all_to_all.25.ids_ref, bf16[4608,128]{1,0:T(8,128)(2,1)S(1)} %bitcast.100), custom_call_target="tpu_custom_call" | custom-call | tf_op jit(solution)/shard_map/table/pallas_call | solution.py:770
  228.2 9.0 %cross.1 = (f32[1027,1,1027]{2,1,0:T(1,128)}, f32[1027,1,1027]{2,1,0:T(1,128)}, f32[1027,1,1027]{2,1,0:T(1,128)}, f32[1027,1,1027]{2,1,0:T(1,128)}, bf16[1027,1027]{1,0:T(8,128)(2,1)}) custom-call(s32[1]{0:T(128)} %bitcast.28.place_ref, bf16[4,64,1024]{2,1,0:T(8,128)(2,1)} %copy-done.13, bf16[4,64,1024]{2,1,0:T(8,128)(2,1)} %copy-done.18, ...), custom_call_target="tpu_custom_call" | custom-call | tf_op jit(solution)/shard_map/cross/pallas_call | solution.py:811
  237.2 3.8 %collective-permute-done.33.refs_5_ = bf16[320,256]{1,0:T(8,128)(2,1)S(1)} collective-permute-done((bf16[320,256]{1,0:T(8,128)(2,1)S(1)}, bf16[320,256]{1,0:T(8,128)(2,1)S(1)}, u32[]{:S(2)}, u32[]{:S(2)}) %collective-permute-start.33) | collective-permute-done | bytes 163872 | tf_op jit(solution)/shard_map/ppermute | solution.py:548
  243.8 8.9 %cross_other.1 = (f32[1027,1,1027]{2,1,0:T(1,128)}, f32[1027,1,1027]{2,1,0:T(1,128)}, f32[1027,1,1027]{2,1,0:T(1,128)}, f32[1027,1,1027]{2,1,0:T(1,128)}, bf16[1027,1027]{1,0:T(8,128)(2,1)}) custom-call(s32[1]{0:T(128)} %bitcast.28.place_ref, ...), custom_call_target="tpu_custom_call", output_to_operand_aliasing={{0}: (7, {}), {1}: (8, {}), {2}: (9, {}), {3}: (10, {}), {4... | custom-call | tf_op jit(solution)/shard_map/cross_other/pallas_call | solution.py:811
  (188 shorter events, 67.8 us)
Async XLA Ops:
  9.8 17.8 %collective-permute-start.2 = (bf16[40,2048]{1,0:T(8,128)(2,1)S(1)}, bf16[40,2048]{1,0:T(8,128)(2,1)S(1)}, u32[]{:S(2)}, u32[]{:S(2)}) collective-permute-start(bf16[40,2048]{1,0:T(8,128)(2,1)S(1)} %get-tuple-element.114.refs_0_), channel_id=1, source_target_pairs={{0,12},{1,13},{2,14},{3,15},{4,8},{5,9},{6,10},{7,11},{8,4},{9,5},... | collective-permute-start | bytes 491528 | tf_op jit(solution)/shard_map/ppermute | solution.py:548
  14.9 13.9 %collective-permute-start.1 = (bf16[40,2048]{1,0:T(8,128)(2,1)S(1)}, bf16[40,2048]{1,0:T(8,128)(2,1)S(1)}, u32[]{:S(2)}, u32[]{:S(2)}) collective-permute-start(bf16[40,2048]{1,0:T(8,128)(2,1)S(1)} %get-tuple-element.114.refs_0_), channel_id=1, source_target_pairs={{0,8},{1,9},{2,10},{3,11},{4,12},{5,13},{6,14},{7,15},{8,0},{9,1},... | collective-permute-start | bytes 491528 | tf_op jit(solution)/shard_map/ppermute | solution.py:548
  14.9 13.9 %collective-permute-start = (bf16[40,2048]{1,0:T(8,128)(2,1)S(1)}, bf16[40,2048]{1,0:T(8,128)(2,1)S(1)}, u32[]{:S(2)}, u32[]{:S(2)}) collective-permute-start(bf16[40,2048]{1,0:T(8,128)(2,1)S(1)} %get-tuple-element.114.refs_0_), channel_id=1, source_target_pairs={{0,4},{1,5},{2,6},{3,7},{4,0},{5,1},{6,2},{7,3},{8,12},{9,13},{10,... | collective-permute-start | bytes 491528 | tf_op jit(solution)/shard_map/ppermute | solution.py:548
  21.0 25.1 %collective-permute-start.4 = (bf16[32,1152]{1,0:T(8,128)(2,1)S(1)}, bf16[32,1152]{1,0:T(8,128)(2,1)S(1)}, u32[]{:S(2)}, u32[]{:S(2)}) collective-permute-start(bf16[32,1152]{1,0:T(8,128)(2,1)S(1)} %pad.32), channel_id=1, source_target_pairs={{0,16},{16,0},{1,17},{17,1},{2,18},{18,2},{3,19},{19,3},{4,20},{20... | collective-permute-start | bytes 221192 | tf_op jit(solution)/shard_map/ppermute | solution.py:548
  29.9 40.8 %collective-permute-start.3 = (bf16[528,1152]{1,0:T(8,128)(2,1)}, bf16[528,1152]{1,0:T(8,128)(2,1)}, u32[]{:S(2)}, u32[]{:S(2)}) collective-permute-start(bf16[528,1152]{1,0:T(8,128)(2,1)} %constant_dynamic-slice_fusion.5), channel_id=1, source_target_pairs={{0,16},{16,0},{1,17},{17,1},{2,18},{18,2},{3,19},{19,3},{4,20},{20... | collective-permute-start | bytes 3649544 | tf_op jit(solution)/shard_map/ppermute | solution.py:548
  42.4 28.3 %all-to-all-start.1 = ((bf16[8,576,128]{2,1,0:T(8,128)(2,1)}), bf16[8,576,128]{2,1,0:T(8,128)(2,1)S(1)}, u32[]{:S(2)}, u32[]{:S(2)}) async-start(bf16[8,576,128]{2,1,0:T(8,128)(2,1)} %bitcast.9), calls=%async_computation.1 | async-start | bytes 2359296 | tf_op jit(solution)/shard_map/all_to_all | solution.py:632
  48.7 12.2 %collective-permute-start.6 = (bf16[2,32,1152]{2,1,0:T(8,128)(2,1)S(1)}, bf16[2,32,1152]{2,1,0:T(8,128)(2,1)S(1)}, u32[]{:S(2)}, u32[]{:S(2)}) collective-permute-start(bf16[2,32,1152]{2,1,0:T(8,128)(2,1)S(1)} %maximum_select_fusion.1), channel_id=1, source_target_pairs={{0,8},{1,9},{2,10},{3,11},{4,12},{5,13},{6,14},{7,15},{8,0},{9,1},... | collective-permute-start | bytes 442376 | tf_op jit(solution)/shard_map/ppermute | solution.py:548
  48.7 12.2 %collective-permute-start.5 = (bf16[2,32,1152]{2,1,0:T(8,128)(2,1)S(1)}, bf16[2,32,1152]{2,1,0:T(8,128)(2,1)S(1)}, u32[]{:S(2)}, u32[]{:S(2)}) collective-permute-start(bf16[2,32,1152]{2,1,0:T(8,128)(2,1)S(1)} %maximum_select_fusion.1), channel_id=1, source_target_pairs={{0,4},{1,5},{2,6},{3,7},{4,0},{5,1},{6,2},{7,3},{8,12},{9,13},{10,... | collective-permute-start | bytes 442376 | tf_op jit(solution)/shard_map/ppermute | solution.py:548
  70.7 22.6 %collective-permute-start.9 = (bf16[528,1152]{1,0:T(8,128)(2,1)}, bf16[528,1152]{1,0:T(8,128)(2,1)S(1)}, u32[]{:S(2)}, u32[]{:S(2)}) collective-permute-start(bf16[528,1152]{1,0:T(8,128)(2,1)} %collective-permute-done.3.half_ref), channel_id=1, source_target_pairs={{0,1},{1,0},{2,3},{3,2},{4,5},{5,4},{6,7},{7,6},{8,9},{9,8},{10,11... | collective-permute-start | bytes 3649544 | tf_op jit(solution)/shard_map/ppermute | solution.py:548
  70.7 20.4 %collective-permute-start.8 = (bf16[4,2,32,1152]{3,2,1,0:T(8,128)(2,1)S(1)}, bf16[4,2,32,1152]{3,2,1,0:T(8,128)(2,1)}, u32[]{:S(2)}, u32[]{:S(2)}) collective-permute-start(bf16[4,2,32,1152]{3,2,1,0:T(8,128)(2,1)S(1)} %pad_maximum_fusion.1.here_ref), channel_id=1, source_target_pairs={{0,2},{1,3},{2,0},{3,1},{4,6},{5,7},{6,4},{7,5},{8,10},{9,11},{10,... | collective-permute-start | bytes 1769480 | tf_op jit(solution)/shard_map/ppermute | solution.py:548
  72.4 20.3 %collective-permute-start.10 = (bf16[4,2,32,1152]{3,2,1,0:T(8,128)(2,1)S(1)}, bf16[4,2,32,1152]{3,2,1,0:T(8,128)(2,1)S(1)}, u32[]{:S(2)}, u32[]{:S(2)}) collective-permute-start(bf16[4,2,32,1152]{3,2,1,0:T(8,128)(2,1)S(1)} %pad_maximum_fusion.1.here_ref), channel_id=1, source_target_pairs={{0,1},{1,0},{2,3},{3,2},{4,5},{5,4},{6,7},{7,6},{8,9},{9,8},{10,11... | collective-permute-start | bytes 1769480 | tf_op jit(solution)/shard_map/ppermute | solution.py:548
  133.2 24.1 %collective-permute-start.14 = (bf16[2,2,96,1024]{3,2,1,0:T(8,128)(2,1)S(1)}, bf16[2,2,96,1024]{3,2,1,0:T(8,128)(2,1)}, u32[]{:S(2)}, u32[]{:S(2)}) collective-permute-start(bf16[2,2,96,1024]{3,2,1,0:T(8,128)(2,1)S(1)} %get-tuple-element.142), channel_id=1, source_target_pairs={{0,16},{16,0},{1,17},{17,1},{2,18},{18,2},{3,19},{19,3},{4,20},{20... | collective-permute-start | bytes 2359304 | tf_op jit(solution)/shard_map/ppermute | solution.py:548
  134.7 22.7 %collective-permute-start.15 = (bf16[2,2,96,1024]{3,2,1,0:T(8,128)(2,1)S(1)}, bf16[2,2,96,1024]{3,2,1,0:T(8,128)(2,1)}, u32[]{:S(2)}, u32[]{:S(2)}) collective-permute-start(bf16[2,2,96,1024]{3,2,1,0:T(8,128)(2,1)S(1)} %get-tuple-element.143), channel_id=1, source_target_pairs={{0,2},{1,3},{2,0},{3,1},{4,6},{5,7},{6,4},{7,5},{8,10},{9,11},{10,... | collective-permute-start | bytes 2359304 | tf_op jit(solution)/shard_map/ppermute | solution.py:548
  135.2 22.1 %collective-permute-start.17 = (f32[16,1152]{1,0:T(8,128)S(1)}, f32[16,1152]{1,0:T(8,128)S(1)}, u32[]{:S(2)}, u32[]{:S(2)}) collective-permute-start(f32[16,1152]{1,0:T(8,128)S(1)} %slice.145), channel_id=1, source_target_pairs={{0,2},{1,3},{2,0},{3,1},{4,6},{5,7},{6,4},{7,5},{8,10},{9,11},{10,... | collective-permute-start | bytes 221192 | tf_op jit(solution)/shard_map/ppermute | solution.py:548
  136.8 20.5 %collective-permute-start.18 = (f32[16,1152]{1,0:T(8,128)S(1)}, f32[16,1152]{1,0:T(8,128)S(1)}, u32[]{:S(2)}, u32[]{:S(2)}) collective-permute-start(f32[16,1152]{1,0:T(8,128)S(1)} %pad_maximum_fusion.4), channel_id=1, source_target_pairs={{0,18},{1,19},{2,16},{3,17},{4,22},{5,23},{6,20},{7,21},{8,26},{9,... | collective-permute-start | bytes 221192 | tf_op jit(solution)/shard_map/ppermute | solution.py:742
  137.5 19.8 %collective-permute-start.16 = (f32[16,1152]{1,0:T(8,128)S(1)}, f32[16,1152]{1,0:T(8,128)S(1)}, u32[]{:S(2)}, u32[]{:S(2)}) collective-permute-start(f32[16,1152]{1,0:T(8,128)S(1)} %pad_maximum_fusion.4), channel_id=1, source_target_pairs={{0,16},{16,0},{1,17},{17,1},{2,18},{18,2},{3,19},{19,3},{4,20},{20... | collective-permute-start | bytes 221192 | tf_op jit(solution)/shard_map/ppermute | solution.py:548
  175.8 38.0 %all-to-all-start.2 = ((bf16[8,576,128]{2,1,0:T(8,128)(2,1)}), bf16[8,576,128]{2,1,0:T(8,128)(2,1)S(1)}, u32[]{:S(2)}, u32[]{:S(2)}) async-start(bf16[8,576,128]{2,1,0:T(8,128)(2,1)} %bitcast.45), calls=%async_computation.2 | async-start | bytes 2359296 | tf_op jit(solution)/shard_map/all_to_all | solution.py:632
  180.0 17.1 %collective-permute-start.25 = (bf16[96,1024]{1,0:T(8,128)(2,1)S(1)}, bf16[96,1024]{1,0:T(8,128)(2,1)S(1)}, u32[]{:S(2)}, u32[]{:S(2)}) collective-permute-start(bf16[96,1024]{1,0:T(8,128)(2,1)S(1)} %get-tuple-element.157), channel_id=1, source_target_pairs={{0,8},{1,9},{2,10},{3,11},{4,12},{5,13},{6,14},{7,15},{8,0},{9,1},... | collective-permute-start | bytes 589832 | tf_op jit(solution)/shard_map/ppermute | solution.py:548
  182.6 14.5 %collective-permute-start.26 = (bf16[96,1024]{1,0:T(8,128)(2,1)S(1)}, bf16[96,1024]{1,0:T(8,128)(2,1)S(1)}, u32[]{:S(2)}, u32[]{:S(2)}) collective-permute-start(bf16[96,1024]{1,0:T(8,128)(2,1)S(1)} %get-tuple-element.158), channel_id=1, source_target_pairs={{0,12},{1,13},{2,14},{3,15},{4,8},{5,9},{6,10},{7,11},{8,4},{9,5},... | collective-permute-start | bytes 589832 | tf_op jit(solution)/shard_map/ppermute | solution.py:548
  201.3 12.4 %collective-permute-start.28 = (bf16[64,1024]{1,0:T(8,128)(2,1)S(1)}, bf16[64,1024]{1,0:T(8,128)(2,1)S(1)}, u32[]{:S(2)}, u32[]{:S(2)}) collective-permute-start(bf16[64,1024]{1,0:T(8,128)(2,1)S(1)} %slice.244), channel_id=1, source_target_pairs={{0,8},{1,9},{2,10},{3,11},{4,12},{5,13},{6,14},{7,15},{8,0},{9,1},... | collective-permute-start | bytes 393224 | tf_op jit(solution)/shard_map/ppermute | solution.py:548
  220.8 20.2 %collective-permute-start.31 = (bf16[4,64,1024]{2,1,0:T(8,128)(2,1)S(1)}, bf16[4,64,1024]{2,1,0:T(8,128)(2,1)S(1)}, u32[]{:S(2)}, u32[]{:S(2)}) collective-permute-start(bf16[4,64,1024]{2,1,0:T(8,128)(2,1)S(1)} %pad_maximum_fusion.2.near_ref), channel_id=1, source_target_pairs={{0,2},{1,3},{2,0},{3,1},{4,6},{5,7},{6,4},{7,5},{8,10},{9,11},{10,... | collective-permute-start | bytes 1572872 | tf_op jit(solution)/shard_map/ppermute | solution.py:548
  222.3 14.9 %collective-permute-start.34 = (bf16[320,256]{1,0:T(8,128)(2,1)S(1)}, bf16[320,256]{1,0:T(8,128)(2,1)S(1)}, u32[]{:S(2)}, u32[]{:S(2)}) collective-permute-start(bf16[320,256]{1,0:T(8,128)(2,1)S(1)} %get-tuple-element.226), channel_id=1, source_target_pairs={{0,12},{1,13},{2,14},{3,15},{4,8},{5,9},{6,10},{7,11},{8,4},{9,5},... | collective-permute-start | bytes 491528 | tf_op jit(solution)/shard_map/ppermute | solution.py:548
  224.3 16.7 %collective-permute-start.33 = (bf16[320,256]{1,0:T(8,128)(2,1)S(1)}, bf16[320,256]{1,0:T(8,128)(2,1)S(1)}, u32[]{:S(2)}, u32[]{:S(2)}) collective-permute-start(bf16[320,256]{1,0:T(8,128)(2,1)S(1)} %get-tuple-element.227), channel_id=1, source_target_pairs={{0,8},{1,9},{2,10},{3,11},{4,12},{5,13},{6,14},{7,15},{8,0},{9,1},... | collective-permute-start | bytes 491528 | tf_op jit(solution)/shard_map/ppermute | solution.py:548
  225.9 15.1 %collective-permute-start.32 = (bf16[320,256]{1,0:T(8,128)(2,1)S(1)}, bf16[320,256]{1,0:T(8,128)(2,1)S(1)}, u32[]{:S(2)}, u32[]{:S(2)}) collective-permute-start(bf16[320,256]{1,0:T(8,128)(2,1)S(1)} %get-tuple-element.228), channel_id=1, source_target_pairs={{0,4},{1,5},{2,6},{3,7},{4,0},{5,1},{6,2},{7,3},{8,12},{9,13},{10,... | collective-permute-start | bytes 491528 | tf_op jit(solution)/shard_map/ppermute | solution.py:548
  (44 other events, 521.4 us)

commit v6 on v5

--- a/solution.py
+++ b/solution.py
@@ -137,7 +137,7 @@
             rows_ref[pl.ds(pl.multiple_of(block * third, 16), third), :] = packed.astype(BF16)
         return carry
 
-    lax.fori_loop(0, ids_ref.shape[0] // groups, step, 0)
+    lax.fori_loop(0, ids_ref.shape[0] // groups, step, 0, unroll=2)
 
 
 def column_map(feat, dense_width, embed, turned):
@@ -219,25 +219,25 @@
 
     def cut(ref, at, spread):
         start, spread = spread
-        here = slice(at, at + CHUNK)
+        here = slice(at, at + half)
         ref[here, :] = contract(dx_ref[here, pl.ds(start, 2 * LANES)], spread, 1, 0)
 
     def put(feat, ref, at):
-        rows = [ref[at + k : at + k + 1, :] for k in range(CHUNK)]
-        for k in range(CHUNK):
+        rows = [ref[at + k : at + k + 1, :] for k in range(half)]
+        for k in range(half):
             far_ref[pl.ds(place_ref[feat * half + at + k], 1), :] = rows[k]
 
     spread = column_map(0, dense_width, embed, 1)
-    for at in range(0, half, CHUNK):
+    for at in range(0, half, half):
         cut(even_ref, at, spread)
 
     def step(pair, carry):
         spread = column_map(2 * pair + 1, dense_width, embed, 1)
-        for at in range(0, half, CHUNK):
+        for at in range(0, half, half):
             cut(odd_ref, at, spread)
             put(2 * pair, even_ref, at)
         spread = column_map(jnp.minimum(2 * pair + 2, feats - 1), dense_width, embed, 1)
-        for at in range(0, half, CHUNK):
+        for at in range(0, half, half):
             cut(even_ref, at, spread)
             put(2 * pair + 1, odd_ref, at)
         return carry
@@ -281,7 +281,7 @@
             total_ref[group] += contract(jnp.concatenate(spread, axis=0).astype(BF16), pick, 1, 1)
         return carry
 
-    lax.fori_loop(0, ids_ref.shape[0] // groups, step, 0)
+    lax.fori_loop(0, ids_ref.shape[0] // groups, step, 0, unroll=2)
     own_ref[...] = total_ref[spot_ref[1]]
     for k in range(1, groups):
         other_ref[k - 1] = total_ref[spot_ref[1] ^ k].astype(BF16)

time: 254 us -> 253 us (level)
  Pallas kernels: 106 us -> 102 us
  waiting for transfers between devices: 62.6 us -> 65.6 us
  transfers between devices with their start and end apart: 39 -> 39, of which waited for: 16 -> 16; matrix products, arithmetic and copies ran while one was open for 6% -> 6% of each run, Pallas kernels for 15% -> 14%
where the time goes in v6:
time: 253 us; the launch traced here: 252 us
  Pallas kernels  102 us (40%)
  waiting for transfers between devices  65.6 us (26%)
  starting transfers between devices  55.8 us (22%)
  local copies, waits for them, and re-layouts  16.3 us (6%)
  other arithmetic  11 us (4%)
    ppermute x35, waiting for transfers between devices, flip(): return lax.ppermute(x, axis, [(i, i ^ bit) for i in range(size)])  54.1 us
    ppermute x35, starting transfers between devices, flip(): return lax.ppermute(x, axis, [(i, i ^ bit) for i in range(size)])  43.8 us
    pallas_call x1, Pallas kernels, local(): pl.pallas_call(towers_kernel, out_shape=(low, low, low, low_deep, low, ja...  18 us
    pallas_call x2, Pallas kernels, update_cross(): pl.pallas_call(functools.partial(cross_kernel, other, blocks), grid_spec=...  17.9 us
    pallas_call x1, Pallas kernels, local(): pl.pallas_call(functools.partial(inputs_kernel, feats, stride, groups, em...  17.4 us
    pallas_call x1, Pallas kernels, local(): pl.pallas_call(functools.partial(send_kernel, feats, slots, stride, embed...  15.5 us
    all_to_all x3, waiting for transfers between devices, in_plane(): lax.all_to_all(x, ('tower', 'batch'), split_axis=0, concat_axis=0, axis_i...  11.5 us
    all_to_all x3, starting transfers between devices, in_plane(): lax.all_to_all(x, ('tower', 'batch'), split_axis=0, concat_axis=0, axis_i...  11.3 us
  transfers between devices with their start and end apart: 39, of which 16 were waited for; matrix products, arithmetic and copies ran while one was open for 6% of the time, Pallas kernels for 14%

profile of v6, /device:TPU:0, one launch (start us, length us, event | category | flops | bytes accessed | tf_op | source)
XLA Modules:
  0.0 252.1 jit_solution(7359466880269805316)
XLA Ops:
  2.6 7.2 %slots.1 = (s32[32,512]{1,0:T(8,128)S(1)}, s32[104,128]{1,0:T(8,128)S(1)}, bf16[40,2048]{1,0:T(8,128)(2,1)S(1)}) custom-call(s32[26,512]{1,0:T(8,128)S(1)} %dynamic-slice_bitcast_fusion.ids_ref, s32[1,512]{1,0:T(1,128)S(1)} %bitcast.108, f32[39,2048]{1,0:T(8,128)S(1)} %bitcast.102), custom_call_target="tpu_custom_call" | custom-call | tf_op jit(solution)/shard_map/slots/pallas_call | solution.py:616
  9.8 5.1 %collective-permute-start.2 = (bf16[40,2048]{1,0:T(8,128)(2,1)S(1)}, bf16[40,2048]{1,0:T(8,128)(2,1)S(1)}, u32[]{:S(2)}, u32[]{:S(2)}) collective-permute-start(bf16[40,2048]{1,0:T(8,128)(2,1)S(1)} %get-tuple-element.114.refs_0_), channel_id=1, source_target_pairs={{0,12},{1,13},{2,14},{3,15},{4,8},{5,9},{6,10},{7,11},{8,4},{9,5},... | collective-permute-start | bytes 491528 | tf_op jit(solution)/shard_map/ppermute | solution.py:548
  17.2 3.9 %all-to-all-start = ((s32[8,4,512]{2,1,0:T(4,128)}), s32[8,4,512]{2,1,0:T(4,128)S(1)}, u32[]{:S(2)}, u32[]{:S(2)}) async-start(s32[8,4,512]{2,1,0:T(4,128)} %all_to_all.23), calls=%async_computation | async-start | bytes 131072 | tf_op jit(solution)/shard_map/all_to_all | solution.py:632
  32.4 8.0 %lookup.1 = bf16[4608,128]{1,0:T(8,128)(2,1)} custom-call(s32[4]{0:T(128)S(1)} %pad_add_fusion.1.spot_ref, s32[32,512]{1,0:T(8,128)S(1)} %all_to_all.25.ids_ref, bf16[40,2048]{1,0:T(8,128)(2,1)S(1)} %get-tuple-element.114.refs_0_, bf16[40,2048]{1,0:T(8,128)(2,1)S(1)} %collective-permute-done.refs_1_, bf16[40,2048]{1,0:T(8,128)(2,1)S(1)} %collective-permute-done.1.refs_2_, ...), custom_call_target="tpu_custom_call" | custom-call | tf_op jit(solution)/shard_map/lookup/pallas_call | solution.py:649
  40.4 3.7 %all-to-all-start.1 = ((bf16[8,576,128]{2,1,0:T(8,128)(2,1)}), bf16[8,576,128]{2,1,0:T(8,128)(2,1)S(1)}, u32[]{:S(2)}, u32[]{:S(2)}) async-start(bf16[8,576,128]{2,1,0:T(8,128)(2,1)} %bitcast.9), calls=%async_computation.1 | async-start | bytes 2359296 | tf_op jit(solution)/shard_map/all_to_all | solution.py:632
  48.7 4.2 %collective-permute-done.7 = bf16[2,32,1152]{2,1,0:T(8,128)(2,1)S(1)} collective-permute-done((bf16[2,32,1152]{2,1,0:T(8,128)(2,1)S(1)}, bf16[2,32,1152]{2,1,0:T(8,128)(2,1)S(1)}, u32[]{:S(2)}, u32[]{:S(2)}) %collective-permute-start.7) | collective-permute-done | bytes 147488 | tf_op jit(solution)/shard_map/ppermute | solution.py:548
  52.9 6.1 %collective-permute-done.6 = bf16[2,32,1152]{2,1,0:T(8,128)(2,1)S(1)} collective-permute-done((bf16[2,32,1152]{2,1,0:T(8,128)(2,1)S(1)}, bf16[2,32,1152]{2,1,0:T(8,128)(2,1)S(1)}, u32[]{:S(2)}, u32[]{:S(2)}) %collective-permute-start.6) | collective-permute-done | bytes 147488 | tf_op jit(solution)/shard_map/ppermute | solution.py:548
  59.2 11.5 %all-to-all-done.1 = bf16[8,576,128]{2,1,0:T(8,128)(2,1)S(1)} async-done(((bf16[8,576,128]{2,1,0:T(8,128)(2,1)}), bf16[8,576,128]{2,1,0:T(8,128)(2,1)S(1)}, u32[]{:S(2)}, u32[]{:S(2)}) %all-to-all-start.1) | async-done | bytes 1179680 | tf_op jit(solution)/shard_map/all_to_all | solution.py:632
  72.7 17.4 %inputs.1 = (bf16[512,1152]{1,0:T(8,128)(2,1)S(1)}, f32[1,1]{1,0:T(1,128)}) custom-call(s32[13312]{0:T(1024)S(1)} %bitcast.106, bf16[4608,128]{1,0:T(8,128)(2,1)S(1)} %bitcast.101, bf16[512,128]{1,0:T(8,128)(2,1)S(1)} %pad.38.dense_ref), custom_call_target="tpu_custom_call" | custom-call | tf_op jit(solution)/shard_map/inputs/pallas_call | solution.py:678
  94.6 18.0 %towers.1 = (bf16[512,1152]{1,0:T(8,128)(2,1)}, bf16[512,1152]{1,0:T(8,128)(2,1)}, bf16[512,1152]{1,0:T(8,128)(2,1)}, bf16[512,1024]{1,0:T(8,128)(2,1)}, bf16[512,1152]{1,0:T(8,128)(2,1)}, /*index=5*/f32[8,1152]{1,0:T(8,128)}) custom-call(s32[4]{0:T(128)} %copy-done.8, f32[1,1]{1,0:T(1,128)} %get-tuple-element.128.count_ref, f32[1,1]{1,0:T(1,128)} %bitcast.18.bias_ref, ...), custom_call_target="tpu_custom_call" | custom-call | tf_op jit(solution)/shard_map/towers/pallas_call | solution.py:697
  112.6 10.5 %grads.1 = (bf16[2,2,2,2,96,1024]{5,4,3,2,1,0:T(8,128)(2,1)}, bf16[2,2,2,2,96,1024]{5,4,3,2,1,0:T(8,128)(2,1)}, f32[24,1152]{1,0:T(8,128)}) custom-call(s32[4]{0:T(128)} %copy-done.8, bf16[512,1152]{1,0:T(8,128)(2,1)} %copy-done.2, bf16[512,1152]{1,0:T(8,128)(2,1)} %get-tuple-element.133.one_ref, bf16[512,1152]{1,0:T(8,128)(2,1)} %get-tuple-element.134.d_second_ref, ...), custom_call_target="tpu_custom_call" | custom-call | tf_op jit(solution)/shard_map/grads/pallas_call | solution.py:720
  123.6 5.5 %collective-permute-done.13 = f32[24,1152]{1,0:T(8,128)S(1)} collective-permute-done((f32[24,1152]{1,0:T(8,128)}, f32[24,1152]{1,0:T(8,128)S(1)}, u32[]{:S(2)}, u32[]{:S(2)}) %collective-permute-start.13) | collective-permute-done | bytes 110624 | tf_op jit(solution)/shard_map/ppermute | solution.py:548
  138.9 15.5 %send.1 = bf16[4608,128]{1,0:T(8,128)(2,1)} custom-call(s32[13312]{0:T(1024)S(1)} %bitcast.107, bf16[512,1152]{1,0:T(8,128)(2,1)S(1)} %copy-done.5), custom_call_target="tpu_custom_call" | custom-call | tf_op jit(solution)/shard_map/send/pallas_call | solution.py:744
  154.4 2.9 %collective-permute-done.17 = f32[16,1152]{1,0:T(8,128)S(1)} collective-permute-done((f32[16,1152]{1,0:T(8,128)S(1)}, f32[16,1152]{1,0:T(8,128)S(1)}, u32[]{:S(2)}, u32[]{:S(2)}) %collective-permute-start.17) | collective-permute-done | bytes 73760 | tf_op jit(solution)/shard_map/ppermute | solution.py:548
  166.0 7.1 %collective-permute-done.19 = bf16[2,96,1024]{2,1,0:T(8,128)(2,1)S(1)} collective-permute-done((bf16[2,96,1024]{2,1,0:T(8,128)(2,1)S(1)}, bf16[2,96,1024]{2,1,0:T(8,128)(2,1)S(1)}, u32[]{:S(2)}, u32[]{:S(2)}) %collective-permute-start.19) | collective-permute-done | bytes 393248 | tf_op jit(solution)/shard_map/ppermute | solution.py:548
  175.8 3.7 %all-to-all-start.2 = ((bf16[8,576,128]{2,1,0:T(8,128)(2,1)}), bf16[8,576,128]{2,1,0:T(8,128)(2,1)S(1)}, u32[]{:S(2)}, u32[]{:S(2)}) async-start(bf16[8,576,128]{2,1,0:T(8,128)(2,1)} %bitcast.45), calls=%async_computation.2 | async-start | bytes 2359296 | tf_op jit(solution)/shard_map/all_to_all | solution.py:632
  185.5 5.0 %collective-permute-done.24 = bf16[96,1024]{1,0:T(8,128)(2,1)S(1)} collective-permute-done((bf16[96,1024]{1,0:T(8,128)(2,1)S(1)}, bf16[96,1024]{1,0:T(8,128)(2,1)S(1)}, u32[]{:S(2)}, u32[]{:S(2)}) %collective-permute-start.24) | collective-permute-done | bytes 196640 | tf_op jit(solution)/shard_map/ppermute | solution.py:548
  190.5 6.7 %collective-permute-done.25 = bf16[96,1024]{1,0:T(8,128)(2,1)S(1)} collective-permute-done((bf16[96,1024]{1,0:T(8,128)(2,1)S(1)}, bf16[96,1024]{1,0:T(8,128)(2,1)S(1)}, u32[]{:S(2)}, u32[]{:S(2)}) %collective-permute-start.25) | collective-permute-done | bytes 196640 | tf_op jit(solution)/shard_map/ppermute | solution.py:548
  197.3 4.1 %collective-permute-start.27 = (bf16[64,1024]{1,0:T(8,128)(2,1)S(1)}, bf16[64,1024]{1,0:T(8,128)(2,1)S(1)}, u32[]{:S(2)}, u32[]{:S(2)}) collective-permute-start(bf16[64,1024]{1,0:T(8,128)(2,1)S(1)} %slice.244), channel_id=1, source_target_pairs={{0,4},{1,5},{2,6},{3,7},{4,0},{5,1},{6,2},{7,3},{8,12},{9,13},{10,... | collective-permute-start | bytes 393224 | tf_op jit(solution)/shard_map/ppermute | solution.py:548
  205.6 8.2 %collective-permute-done.28 = bf16[64,1024]{1,0:T(8,128)(2,1)S(1)} collective-permute-done((bf16[64,1024]{1,0:T(8,128)(2,1)S(1)}, bf16[64,1024]{1,0:T(8,128)(2,1)S(1)}, u32[]{:S(2)}, u32[]{:S(2)}) %collective-permute-start.28) | collective-permute-done | bytes 131104 | tf_op jit(solution)/shard_map/ppermute | solution.py:548
  213.9 6.2 %table.1 = (f32[320,256]{1,0:T(8,128)S(1)}, bf16[3,320,256]{2,1,0:T(8,128)(2,1)S(1)}) custom-call(s32[4]{0:T(128)S(1)} %copy-done.9, s32[32,512]{1,0:T(8,128)S(1)} %all_to_all.25.ids_ref, bf16[4608,128]{1,0:T(8,128)(2,1)S(1)} %bitcast.100), custom_call_target="tpu_custom_call" | custom-call | tf_op jit(solution)/shard_map/table/pallas_call | solution.py:770
  227.5 9.0 %cross.1 = (f32[1027,1,1027]{2,1,0:T(1,128)}, f32[1027,1,1027]{2,1,0:T(1,128)}, f32[1027,1,1027]{2,1,0:T(1,128)}, f32[1027,1,1027]{2,1,0:T(1,128)}, bf16[1027,1027]{1,0:T(8,128)(2,1)}) custom-call(s32[1]{0:T(128)} %bitcast.28.place_ref, bf16[4,64,1024]{2,1,0:T(8,128)(2,1)} %copy-done.13, bf16[4,64,1024]{2,1,0:T(8,128)(2,1)} %copy-done.18, ...), custom_call_target="tpu_custom_call" | custom-call | tf_op jit(solution)/shard_map/cross/pallas_call | solution.py:811
  236.4 3.8 %collective-permute-done.33.refs_5_ = bf16[320,256]{1,0:T(8,128)(2,1)S(1)} collective-permute-done((bf16[320,256]{1,0:T(8,128)(2,1)S(1)}, bf16[320,256]{1,0:T(8,128)(2,1)S(1)}, u32[]{:S(2)}, u32[]{:S(2)}) %collective-permute-start.33) | collective-permute-done | bytes 163872 | tf_op jit(solution)/shard_map/ppermute | solution.py:548
  243.0 8.9 %cross_other.1 = (f32[1027,1,1027]{2,1,0:T(1,128)}, f32[1027,1,1027]{2,1,0:T(1,128)}, f32[1027,1,1027]{2,1,0:T(1,128)}, f32[1027,1,1027]{2,1,0:T(1,128)}, bf16[1027,1027]{1,0:T(8,128)(2,1)}) custom-call(s32[1]{0:T(128)} %bitcast.28.place_ref, ...), custom_call_target="tpu_custom_call", output_to_operand_aliasing={{0}: (7, {}), {1}: (8, {}), {2}: (9, {}), {3}: (10, {}), {4... | custom-call | tf_op jit(solution)/shard_map/cross_other/pallas_call | solution.py:811
  (188 shorter events, 68.5 us)
Async XLA Ops:
  9.8 17.8 %collective-permute-start.2 = (bf16[40,2048]{1,0:T(8,128)(2,1)S(1)}, bf16[40,2048]{1,0:T(8,128)(2,1)S(1)}, u32[]{:S(2)}, u32[]{:S(2)}) collective-permute-start(bf16[40,2048]{1,0:T(8,128)(2,1)S(1)} %get-tuple-element.114.refs_0_), channel_id=1, source_target_pairs={{0,12},{1,13},{2,14},{3,15},{4,8},{5,9},{6,10},{7,11},{8,4},{9,5},... | collective-permute-start | bytes 491528 | tf_op jit(solution)/shard_map/ppermute | solution.py:548
  14.9 13.9 %collective-permute-start.1 = (bf16[40,2048]{1,0:T(8,128)(2,1)S(1)}, bf16[40,2048]{1,0:T(8,128)(2,1)S(1)}, u32[]{:S(2)}, u32[]{:S(2)}) collective-permute-start(bf16[40,2048]{1,0:T(8,128)(2,1)S(1)} %get-tuple-element.114.refs_0_), channel_id=1, source_target_pairs={{0,8},{1,9},{2,10},{3,11},{4,12},{5,13},{6,14},{7,15},{8,0},{9,1},... | collective-permute-start | bytes 491528 | tf_op jit(solution)/shard_map/ppermute | solution.py:548
  14.9 13.9 %collective-permute-start = (bf16[40,2048]{1,0:T(8,128)(2,1)S(1)}, bf16[40,2048]{1,0:T(8,128)(2,1)S(1)}, u32[]{:S(2)}, u32[]{:S(2)}) collective-permute-start(bf16[40,2048]{1,0:T(8,128)(2,1)S(1)} %get-tuple-element.114.refs_0_), channel_id=1, source_target_pairs={{0,4},{1,5},{2,6},{3,7},{4,0},{5,1},{6,2},{7,3},{8,12},{9,13},{10,... | collective-permute-start | bytes 491528 | tf_op jit(solution)/shard_map/ppermute | solution.py:548
  21.0 23.1 %collective-permute-start.4 = (bf16[32,1152]{1,0:T(8,128)(2,1)S(1)}, bf16[32,1152]{1,0:T(8,128)(2,1)S(1)}, u32[]{:S(2)}, u32[]{:S(2)}) collective-permute-start(bf16[32,1152]{1,0:T(8,128)(2,1)S(1)} %pad.32), channel_id=1, source_target_pairs={{0,16},{16,0},{1,17},{17,1},{2,18},{18,2},{3,19},{19,3},{4,20},{20... | collective-permute-start | bytes 221192 | tf_op jit(solution)/shard_map/ppermute | solution.py:548
  29.9 40.8 %collective-permute-start.3 = (bf16[528,1152]{1,0:T(8,128)(2,1)}, bf16[528,1152]{1,0:T(8,128)(2,1)}, u32[]{:S(2)}, u32[]{:S(2)}) collective-permute-start(bf16[528,1152]{1,0:T(8,128)(2,1)} %constant_dynamic-slice_fusion.5), channel_id=1, source_target_pairs={{0,16},{16,0},{1,17},{17,1},{2,18},{18,2},{3,19},{19,3},{4,20},{20... | collective-permute-start | bytes 3649544 | tf_op jit(solution)/shard_map/ppermute | solution.py:548
  40.4 30.3 %all-to-all-start.1 = ((bf16[8,576,128]{2,1,0:T(8,128)(2,1)}), bf16[8,576,128]{2,1,0:T(8,128)(2,1)S(1)}, u32[]{:S(2)}, u32[]{:S(2)}) async-start(bf16[8,576,128]{2,1,0:T(8,128)(2,1)} %bitcast.9), calls=%async_computation.1 | async-start | bytes 2359296 | tf_op jit(solution)/shard_map/all_to_all | solution.py:632
  46.7 12.2 %collective-permute-start.6 = (bf16[2,32,1152]{2,1,0:T(8,128)(2,1)S(1)}, bf16[2,32,1152]{2,1,0:T(8,128)(2,1)S(1)}, u32[]{:S(2)}, u32[]{:S(2)}) collective-permute-start(bf16[2,32,1152]{2,1,0:T(8,128)(2,1)S(1)} %maximum_select_fusion.1), channel_id=1, source_target_pairs={{0,8},{1,9},{2,10},{3,11},{4,12},{5,13},{6,14},{7,15},{8,0},{9,1},... | collective-permute-start | bytes 442376 | tf_op jit(solution)/shard_map/ppermute | solution.py:548
  46.7 12.2 %collective-permute-start.5 = (bf16[2,32,1152]{2,1,0:T(8,128)(2,1)S(1)}, bf16[2,32,1152]{2,1,0:T(8,128)(2,1)S(1)}, u32[]{:S(2)}, u32[]{:S(2)}) collective-permute-start(bf16[2,32,1152]{2,1,0:T(8,128)(2,1)S(1)} %maximum_select_fusion.1), channel_id=1, source_target_pairs={{0,4},{1,5},{2,6},{3,7},{4,0},{5,1},{6,2},{7,3},{8,12},{9,13},{10,... | collective-permute-start | bytes 442376 | tf_op jit(solution)/shard_map/ppermute | solution.py:548
  70.7 22.6 %collective-permute-start.9 = (bf16[528,1152]{1,0:T(8,128)(2,1)}, bf16[528,1152]{1,0:T(8,128)(2,1)S(1)}, u32[]{:S(2)}, u32[]{:S(2)}) collective-permute-start(bf16[528,1152]{1,0:T(8,128)(2,1)} %collective-permute-done.3.half_ref), channel_id=1, source_target_pairs={{0,1},{1,0},{2,3},{3,2},{4,5},{5,4},{6,7},{7,6},{8,9},{9,8},{10,11... | collective-permute-start | bytes 3649544 | tf_op jit(solution)/shard_map/ppermute | solution.py:548
  70.7 20.4 %collective-permute-start.8 = (bf16[4,2,32,1152]{3,2,1,0:T(8,128)(2,1)S(1)}, bf16[4,2,32,1152]{3,2,1,0:T(8,128)(2,1)}, u32[]{:S(2)}, u32[]{:S(2)}) collective-permute-start(bf16[4,2,32,1152]{3,2,1,0:T(8,128)(2,1)S(1)} %pad_maximum_fusion.1.here_ref), channel_id=1, source_target_pairs={{0,2},{1,3},{2,0},{3,1},{4,6},{5,7},{6,4},{7,5},{8,10},{9,11},{10,... | collective-permute-start | bytes 1769480 | tf_op jit(solution)/shard_map/ppermute | solution.py:548
  72.4 20.3 %collective-permute-start.10 = (bf16[4,2,32,1152]{3,2,1,0:T(8,128)(2,1)S(1)}, bf16[4,2,32,1152]{3,2,1,0:T(8,128)(2,1)S(1)}, u32[]{:S(2)}, u32[]{:S(2)}) collective-permute-start(bf16[4,2,32,1152]{3,2,1,0:T(8,128)(2,1)S(1)} %pad_maximum_fusion.1.here_ref), channel_id=1, source_target_pairs={{0,1},{1,0},{2,3},{3,2},{4,5},{5,4},{6,7},{7,6},{8,9},{9,8},{10,11... | collective-permute-start | bytes 1769480 | tf_op jit(solution)/shard_map/ppermute | solution.py:548
  133.2 24.1 %collective-permute-start.14 = (bf16[2,2,96,1024]{3,2,1,0:T(8,128)(2,1)S(1)}, bf16[2,2,96,1024]{3,2,1,0:T(8,128)(2,1)}, u32[]{:S(2)}, u32[]{:S(2)}) collective-permute-start(bf16[2,2,96,1024]{3,2,1,0:T(8,128)(2,1)S(1)} %get-tuple-element.142), channel_id=1, source_target_pairs={{0,16},{16,0},{1,17},{17,1},{2,18},{18,2},{3,19},{19,3},{4,20},{20... | collective-permute-start | bytes 2359304 | tf_op jit(solution)/shard_map/ppermute | solution.py:548
  134.7 22.7 %collective-permute-start.15 = (bf16[2,2,96,1024]{3,2,1,0:T(8,128)(2,1)S(1)}, bf16[2,2,96,1024]{3,2,1,0:T(8,128)(2,1)}, u32[]{:S(2)}, u32[]{:S(2)}) collective-permute-start(bf16[2,2,96,1024]{3,2,1,0:T(8,128)(2,1)S(1)} %get-tuple-element.143), channel_id=1, source_target_pairs={{0,2},{1,3},{2,0},{3,1},{4,6},{5,7},{6,4},{7,5},{8,10},{9,11},{10,... | collective-permute-start | bytes 2359304 | tf_op jit(solution)/shard_map/ppermute | solution.py:548
  135.2 22.1 %collective-permute-start.17 = (f32[16,1152]{1,0:T(8,128)S(1)}, f32[16,1152]{1,0:T(8,128)S(1)}, u32[]{:S(2)}, u32[]{:S(2)}) collective-permute-start(f32[16,1152]{1,0:T(8,128)S(1)} %slice.145), channel_id=1, source_target_pairs={{0,2},{1,3},{2,0},{3,1},{4,6},{5,7},{6,4},{7,5},{8,10},{9,11},{10,... | collective-permute-start | bytes 221192 | tf_op jit(solution)/shard_map/ppermute | solution.py:548
  136.8 20.5 %collective-permute-start.18 = (f32[16,1152]{1,0:T(8,128)S(1)}, f32[16,1152]{1,0:T(8,128)S(1)}, u32[]{:S(2)}, u32[]{:S(2)}) collective-permute-start(f32[16,1152]{1,0:T(8,128)S(1)} %pad_maximum_fusion.4), channel_id=1, source_target_pairs={{0,18},{1,19},{2,16},{3,17},{4,22},{5,23},{6,20},{7,21},{8,26},{9,... | collective-permute-start | bytes 221192 | tf_op jit(solution)/shard_map/ppermute | solution.py:742
  137.5 19.8 %collective-permute-start.16 = (f32[16,1152]{1,0:T(8,128)S(1)}, f32[16,1152]{1,0:T(8,128)S(1)}, u32[]{:S(2)}, u32[]{:S(2)}) collective-permute-start(f32[16,1152]{1,0:T(8,128)S(1)} %pad_maximum_fusion.4), channel_id=1, source_target_pairs={{0,16},{16,0},{1,17},{17,1},{2,18},{18,2},{3,19},{19,3},{4,20},{20... | collective-permute-start | bytes 221192 | tf_op jit(solution)/shard_map/ppermute | solution.py:548
  175.8 38.1 %all-to-all-start.2 = ((bf16[8,576,128]{2,1,0:T(8,128)(2,1)}), bf16[8,576,128]{2,1,0:T(8,128)(2,1)S(1)}, u32[]{:S(2)}, u32[]{:S(2)}) async-start(bf16[8,576,128]{2,1,0:T(8,128)(2,1)} %bitcast.45), calls=%async_computation.2 | async-start | bytes 2359296 | tf_op jit(solution)/shard_map/all_to_all | solution.py:632
  180.0 17.1 %collective-permute-start.25 = (bf16[96,1024]{1,0:T(8,128)(2,1)S(1)}, bf16[96,1024]{1,0:T(8,128)(2,1)S(1)}, u32[]{:S(2)}, u32[]{:S(2)}) collective-permute-start(bf16[96,1024]{1,0:T(8,128)(2,1)S(1)} %get-tuple-element.157), channel_id=1, source_target_pairs={{0,8},{1,9},{2,10},{3,11},{4,12},{5,13},{6,14},{7,15},{8,0},{9,1},... | collective-permute-start | bytes 589832 | tf_op jit(solution)/shard_map/ppermute | solution.py:548
  182.6 14.5 %collective-permute-start.26 = (bf16[96,1024]{1,0:T(8,128)(2,1)S(1)}, bf16[96,1024]{1,0:T(8,128)(2,1)S(1)}, u32[]{:S(2)}, u32[]{:S(2)}) collective-permute-start(bf16[96,1024]{1,0:T(8,128)(2,1)S(1)} %get-tuple-element.158), channel_id=1, source_target_pairs={{0,12},{1,13},{2,14},{3,15},{4,8},{5,9},{6,10},{7,11},{8,4},{9,5},... | collective-permute-start | bytes 589832 | tf_op jit(solution)/shard_map/ppermute | solution.py:548
  201.4 12.4 %collective-permute-start.28 = (bf16[64,1024]{1,0:T(8,128)(2,1)S(1)}, bf16[64,1024]{1,0:T(8,128)(2,1)S(1)}, u32[]{:S(2)}, u32[]{:S(2)}) collective-permute-start(bf16[64,1024]{1,0:T(8,128)(2,1)S(1)} %slice.244), channel_id=1, source_target_pairs={{0,8},{1,9},{2,10},{3,11},{4,12},{5,13},{6,14},{7,15},{8,0},{9,1},... | collective-permute-start | bytes 393224 | tf_op jit(solution)/shard_map/ppermute | solution.py:548
  220.1 20.1 %collective-permute-start.31 = (bf16[4,64,1024]{2,1,0:T(8,128)(2,1)S(1)}, bf16[4,64,1024]{2,1,0:T(8,128)(2,1)S(1)}, u32[]{:S(2)}, u32[]{:S(2)}) collective-permute-start(bf16[4,64,1024]{2,1,0:T(8,128)(2,1)S(1)} %pad_maximum_fusion.2.near_ref), channel_id=1, source_target_pairs={{0,2},{1,3},{2,0},{3,1},{4,6},{5,7},{6,4},{7,5},{8,10},{9,11},{10,... | collective-permute-start | bytes 1572872 | tf_op jit(solution)/shard_map/ppermute | solution.py:548
  221.6 14.9 %collective-permute-start.34 = (bf16[320,256]{1,0:T(8,128)(2,1)S(1)}, bf16[320,256]{1,0:T(8,128)(2,1)S(1)}, u32[]{:S(2)}, u32[]{:S(2)}) collective-permute-start(bf16[320,256]{1,0:T(8,128)(2,1)S(1)} %get-tuple-element.226), channel_id=1, source_target_pairs={{0,12},{1,13},{2,14},{3,15},{4,8},{5,9},{6,10},{7,11},{8,4},{9,5},... | collective-permute-start | bytes 491528 | tf_op jit(solution)/shard_map/ppermute | solution.py:548
  223.5 16.7 %collective-permute-start.33 = (bf16[320,256]{1,0:T(8,128)(2,1)S(1)}, bf16[320,256]{1,0:T(8,128)(2,1)S(1)}, u32[]{:S(2)}, u32[]{:S(2)}) collective-permute-start(bf16[320,256]{1,0:T(8,128)(2,1)S(1)} %get-tuple-element.227), channel_id=1, source_target_pairs={{0,8},{1,9},{2,10},{3,11},{4,12},{5,13},{6,14},{7,15},{8,0},{9,1},... | collective-permute-start | bytes 491528 | tf_op jit(solution)/shard_map/ppermute | solution.py:548
  225.1 15.1 %collective-permute-start.32 = (bf16[320,256]{1,0:T(8,128)(2,1)S(1)}, bf16[320,256]{1,0:T(8,128)(2,1)S(1)}, u32[]{:S(2)}, u32[]{:S(2)}) collective-permute-start(bf16[320,256]{1,0:T(8,128)(2,1)S(1)} %get-tuple-element.228), channel_id=1, source_target_pairs={{0,4},{1,5},{2,6},{3,7},{4,0},{5,1},{6,2},{7,3},{8,12},{9,13},{10,... | collective-permute-start | bytes 491528 | tf_op jit(solution)/shard_map/ppermute | solution.py:548
  (44 other events, 522.1 us)
